TPU v7x, 128 devices: a whole 4x4x4 slice. The times are simulated.
128 devices in a mesh: dp: 4 (over x_hi, core), ep: 32 (over x_lo, y, z).
Axes of the slice: x: 4 (x_hi: 2, x_lo: 2; x = x_hi * 2 + x_lo), y: 4, z: 4, core: 2. Of those that a mesh axis runs over, the one named last changes fastest.
Arguments:
- queries: bfloat16 [2048, 8192], P(('dp', 'ep')), may hold values from -40 to 40
- kv_cache: bfloat16 [2048, 2, 128, 512], P(('dp', 'ep')), may hold values from -40 to 40
- kv_new: bfloat16 [2048, 2, 512], P(('dp', 'ep')), may hold values from -40 to 40
- lengths: int32 [2048], P(('dp', 'ep')), may hold values from 1 to 128, as said below
- residual: bfloat16 [2048, 4096], P(('dp', 'ep')), may hold values from -64 to 64
- norm_gain: float32 [4096], replicated, may hold values from 0.1 to 1.9
- expert_ids: int32 [2048, 8], P(('dp', 'ep')), may hold values from 0 to 63, all different within a row; in each aligned block of 16 rows (0 to 15, 16 to 31, ...) at most 4 rows name the same one
- route_probs: float32 [2048, 8], P(('dp', 'ep')), may hold values from 0.05 to 1
- w_out: bfloat16 [8192, 4096], P(None, 'ep'), may hold values from -0.0625 to 0.0625
- w_gate: bfloat16 [64, 4096, 1536], P('ep', None, 'dp'), may hold values from -0.09375 to 0.09375
- w_up: bfloat16 [64, 4096, 1536], P('ep', None, 'dp'), may hold values from -0.09375 to 0.09375
- w_down: bfloat16 [64, 1536, 4096], P('ep', 'dp'), may hold values from -0.15625 to 0.15625
Outputs:
- attn_out: bfloat16 [2048, 4096], P(('dp', 'ep'))
- moe_out: bfloat16 [2048, 4096], P(('dp', 'ep'))
Inputs may be any that keep to these rules, and one draw needn't show every extreme that they name: `lengths`: some row of the first device has all 128 positions valid. `expert_ids`: each row names 8 different experts; within the rows of one device no expert is named more than 4 times, a bound that some block reaches.
All inputs are finite; a program needn't handle non-finite values.
Results may differ from a plain program's by a relative error of at most 0.018.
Values may be sent and summed in bfloat16 or wider, within the bound.
No kernel may reach another device: no remote copies, remote signals or barrier semaphores. Data moves between devices by JAX's collectives and lax.ppermute only.
A program may use at most 128 MiB of HBM per device.

v0:
```python
import math

import jax
import jax.numpy as jnp
from jax import lax
from jax.sharding import PartitionSpec as P

HEADS = 64
KVH = 4
HD = 128
TOP = 8
SLOTS = 4


def attend(queries, kv_cache, kv_new, lengths):
    row_count = queries.shape[0]
    groups = HEADS // KVH
    span_len = kv_cache.shape[2]
    query_heads = queries.reshape(row_count, KVH, groups, HD)
    cache_keys = kv_cache[:, 0].reshape(row_count, span_len, KVH, HD)
    cache_values = kv_cache[:, 1].reshape(row_count, span_len, KVH, HD)
    fresh_keys = kv_new[:, 0].reshape(row_count, KVH, HD)
    fresh_values = kv_new[:, 1].reshape(row_count, KVH, HD)
    scaling = 1.0 / math.sqrt(HD)
    cache_scores = (
        jnp.einsum("rkgd,rpkd->rkgp", query_heads, cache_keys, preferred_element_type=jnp.float32)
        * scaling
    )
    live = jnp.arange(span_len, dtype=jnp.int32)[None, :] < lengths[:, None]
    cache_scores = jnp.where(live[:, None, None, :], cache_scores, -1e30)
    fresh_scores = (
        jnp.einsum("rkgd,rkd->rkg", query_heads, fresh_keys, preferred_element_type=jnp.float32)
        * scaling
    )
    highest = jnp.maximum(jnp.max(cache_scores, -1), fresh_scores)
    cache_exp = jnp.exp(cache_scores - highest[..., None])
    fresh_exp = jnp.exp(fresh_scores - highest)
    denominator = jnp.sum(cache_exp, -1) + fresh_exp
    cache_weights = (cache_exp / denominator[..., None]).astype(jnp.bfloat16)
    fresh_weights = (fresh_exp / denominator).astype(jnp.bfloat16)
    mixed = jnp.einsum(
        "rkgp,rpkd->rkgd", cache_weights, cache_values, preferred_element_type=jnp.float32
    )
    mixed = mixed + jnp.einsum(
        "rkg,rkd->rkgd", fresh_weights, fresh_values, preferred_element_type=jnp.float32
    )
    return mixed.reshape(row_count, HEADS * HD).astype(jnp.bfloat16)


def on_device(
    queries,
    kv_cache,
    kv_new,
    lengths,
    residual,
    norm_gain,
    expert_ids,
    route_probs,
    w_out,
    w_gate,
    w_up,
    w_down,
):
    row_count = queries.shape[0]
    attention = attend(queries, kv_cache, kv_new, lengths)
    columns = jnp.dot(
        lax.all_gather(attention, "ep", axis=0, tiled=True),
        w_out,
        preferred_element_type=jnp.float32,
    )
    attn_out = lax.all_to_all(
        columns.astype(jnp.bfloat16), "ep", split_axis=0, concat_axis=1, tiled=True
    )
    stream = residual.astype(jnp.float32) + attn_out.astype(jnp.float32)
    normed = (
        stream * lax.rsqrt(jnp.mean(stream * stream, -1, keepdims=True) + 1e-06) * norm_gain
    ).astype(jnp.bfloat16)
    gates = route_probs / jnp.sum(route_probs, -1, keepdims=True)
    local_experts = w_gate.shape[0]
    expert_total = local_experts * lax.axis_size("ep")
    slot_total = expert_total * SLOTS
    pair_ids = expert_ids.reshape(-1)
    member = (pair_ids[:, None] == jnp.arange(expert_total, dtype=jnp.int32)[None, :]).astype(
        jnp.int32
    )
    ranking = jnp.sum((jnp.cumsum(member, 0) - 1) * member, 1)
    slot_of_pair = pair_ids * SLOTS + ranking
    chosen = slot_of_pair[:, None] == jnp.arange(slot_total, dtype=jnp.int32)[None, :]
    chosen = chosen.reshape(row_count, TOP, slot_total).astype(jnp.float32)
    placing = jnp.sum(chosen, 1).astype(jnp.bfloat16)
    outgoing = jnp.einsum("rs,rd->sd", placing, normed, preferred_element_type=jnp.float32)
    outgoing = outgoing.astype(jnp.bfloat16).reshape(expert_total, SLOTS, -1)
    arrived = lax.all_to_all(outgoing, "ep", split_axis=0, concat_axis=1, tiled=True)
    block_rows = lax.all_gather(arrived, "dp", axis=1, tiled=True)
    gate_act = jnp.einsum("end,edf->enf", block_rows, w_gate, preferred_element_type=jnp.float32)
    up_act = jnp.einsum("end,edf->enf", block_rows, w_up, preferred_element_type=jnp.float32)
    hidden = (jax.nn.silu(gate_act) * up_act).astype(jnp.bfloat16)
    partial_value = jnp.einsum("enf,efd->end", hidden, w_down, preferred_element_type=jnp.float32)
    partial_value = partial_value.reshape(
        local_experts, lax.axis_size("dp"), lax.axis_size("ep"), SLOTS, -1
    )
    returned = lax.all_to_all(
        lax.all_to_all(
            partial_value.astype(jnp.bfloat16), "dp", split_axis=1, concat_axis=1, tiled=True
        ),
        "ep",
        split_axis=2,
        concat_axis=2,
        tiled=True,
    )
    summed = jnp.sum(returned.astype(jnp.float32), 1).astype(jnp.bfloat16)
    expert_out = jnp.transpose(summed, (1, 0, 2, 3)).reshape(slot_total, -1).astype(jnp.float32)
    mixing = jnp.sum(chosen * gates[:, :, None], 1)
    moe_out = jnp.dot(
        mixing, expert_out, precision=lax.Precision.HIGHEST, preferred_element_type=jnp.float32
    )
    return (attn_out, moe_out.astype(jnp.bfloat16))


def solution(mesh):
    return jax.shard_map(
        on_device,
        mesh=mesh,
        in_specs=(
            P(("dp", "ep"), None),
            P(("dp", "ep"), None, None, None),
            P(("dp", "ep"), None, None),
            P(("dp", "ep")),
            P(("dp", "ep"), None),
            P(),
            P(("dp", "ep"), None),
            P(("dp", "ep"), None),
            P(None, "ep"),
            P("ep", None, "dp"),
            P("ep", None, "dp"),
            P("ep", "dp", None),
        ),
        out_specs=(P(("dp", "ep"), None), P(("dp", "ep"), None)),
        check_vma=False,
    )
```

profile of v0, /device:TPU:1, one launch (start us, length us, event | category | flops | bytes accessed | tf_op | source)
XLA Modules:
  0.0 591.0 jit_solution(8304645529868136838)
XLA Ops:
  7.2 0.0 copy-start
  7.2 0.0 all-gather.3.cloned.1.call-start
  7.2 0.9 iota_compare_fusion.2
  8.1 0.8 slice_convert_fusion
  8.9 1.0 copy.63
  9.9 1.0 fusion.9
  10.9 4.7 fusion.16
  15.5 3.9 copy.59
  19.5 2.3 fusion.17
  21.8 0.4 fusion.3
  22.3 3.9 copy.60
  26.2 2.9 fusion.1
  29.1 0.9 copy.70
  30.0 0.0 all-gather.3.cloned.1.call-update
  30.0 0.1 copy.46
  30.1 0.1 eq.29
  30.2 0.1 fusion.8
  30.3 0.2 reduce_window_sum.11
  30.5 0.2 select_reduce_fusion.1
  30.6 0.1 reduce_sum.70
  30.7 0.0 copy-done.5
  30.8 0.0 copy-start.2
  30.8 0.0 copy-start.4
  30.8 151.5 %all-gather.3.cloned.1.call-done = bf16[512,8192]{1,0:T(8,128)(2,1)} async-done(((bf16[16,8192]{1,0:T(8,128)(2,1)}), bf16[512,8192]{1,0:T(8,128)(2,1)}) %all-gather.3.cloned.1.call-update) | async-done | bytes 8388624 | tf_op jit(solution)/shard_map/all_gather | solution.py:67
  182.3 6.4 %convolution_convert_fusion.3 = bf16[512,128]{1,0:T(8,128)(2,1)} fusion(bf16[512,8192]{1,0:T(8,128)(2,1)} %all-gather.3.cloned.1.call-done, bf16[8192,128]{1,0:T(8,128)(2,1)S(1)} %copy-done), kind=kOutput, calls=%fused_computation.9 | convolution fusion | flops 1073807360 | bytes 10616832 | tf_op jit(solution)/shard_map/dot_general | solution.py:66
  188.7 5.6 all-to-all-start
  194.3 0.0 all-gather.5.cloned.1.call-start
  194.4 0.1 copy.48
  194.5 0.1 convert_reduce_fusion
  194.6 7.1 %all-to-all-done = bf16[32,16,128]{2,1,0:T(8,128)(2,1)S(1)} async-done(((bf16[32,16,128]{2,1,0:T(8,128)(2,1)}), bf16[32,16,128]{2,1,0:T(8,128)(2,1)S(1)}, u32[]{:S(2)}, u32[]{:S(2)}) %all-to-all-start) | async-done | bytes 131104 | tf_op jit(solution)/shard_map/all_to_all | solution.py:71
  201.7 0.2 multiply_reduce_fusion
  201.9 0.8 convolution_convert_fusion.1
  202.7 2.2 reshape.75
  204.9 21.4 %all_to_all.47 = bf16[64,4,4096]{2,1,0:T(4,128)(2,1)S(1)} all-to-all(bf16[64,4,4096]{2,1,0:T(4,128)(2,1)} %reshape.75), channel_id=1, replica_groups=mesh['dp'=4,'ep'=32] {'ep'}, dimensions={0} | all-to-all | bytes 4194304 | tf_op jit(solution)/shard_map/all_to_all | solution.py:93
  226.3 2.9 copy.69
  229.2 4.0 all_to_all.40
  233.2 0.0 all-gather.5.cloned.1.call-update
  233.2 86.1 %all-gather.5.cloned.1.call-done = bf16[2,512,4096]{2,1,0:T(8,128)(2,1)} async-done(((bf16[2,128,4096]{2,1,0:T(8,128)(2,1)}), bf16[2,512,4096]{2,1,0:T(8,128)(2,1)}) %all-gather.5.cloned.1.call-update) | async-done | bytes 8388624 | tf_op jit(solution)/shard_map/all_gather | solution.py:94
  319.4 8.8 %fusion.18 = f32[2,512,384]{2,1,0:T(8,128)S(1)} fusion(bf16[2,512,4096]{2,1,0:T(8,128)(2,1)} %all-gather.5.cloned.1.call-done, bf16[2,4096,384]{2,1,0:T(8,128)(2,1)} %param.21), kind=kOutput, calls=%fused_computation.46 | convolution fusion | flops 3221225472 | bytes 16252928 | tf_op jit(solution)/shard_map/end,edf->enf/dot_general | solution.py:95
  328.2 15.1 %convolution_convert_fusion = bf16[2,512,4096]{2,1,0:T(8,128)(2,1)} fusion(bf16[2,384,4096]{2,1,0:T(8,128)(2,1)} %param.23, f32[2,512,384]{2,1,0:T(8,128)S(1)} %fusion.18, bf16[2,512,4096]{2,1,0:T(8,128)(2,1)} %all-gather.5.cloned.1.call-done, bf16[2,4096,384]{2,1,0:T(8,128)(2,1)} %param.22), kind=kOutput, calls=%fused_computation | convolution fusion | flops 6449004544 | bytes 30932992 | tf_op jit(solution)/shard_map/enf,efd->end/dot_general | solution.py:98
  343.3 13.1 %convert_element_type.65 = bf16[2,4,32,4,4096]{4,3,2,1,0:T(4,128)(2,1)} reshape(bf16[2,512,4096]{2,1,0:T(8,128)(2,1)} %convolution_convert_fusion) | data formatting | bytes 16777216 | tf_op jit(solution)/shard_map/convert_element_type | solution.py:104
  356.3 5.7 copy.50
  362.0 96.6 %all_to_all.48 = bf16[2,4,32,4,4096]{4,3,2,0,1:T(4,128)(2,1)S(1)} all-to-all(bf16[2,4,32,4,4096]{4,3,2,0,1:T(4,128)(2,1)S(1)} %copy.50), channel_id=1, replica_groups=mesh['dp'=4,'ep'=32] {'dp'}, dimensions={1} | all-to-all | bytes 16777216 | tf_op jit(solution)/shard_map/all_to_all | solution.py:103
  458.6 4.0 copy.51
  462.6 103.4 %all_to_all.49 = bf16[2,4,32,4,4096]{4,3,1,0,2:T(4,128)(2,1)} all-to-all(bf16[2,4,32,4,4096]{4,3,1,0,2:T(4,128)(2,1)S(1)} %copy.51), channel_id=1, replica_groups=mesh['dp'=4,'ep'=32] {'ep'}, dimensions={2} | all-to-all | bytes 16777216 | tf_op jit(solution)/shard_map/all_to_all | solution.py:102
  566.0 10.8 %reduce_sum.75 = bf16[2,32,4,4096]{3,2,0,1:T(4,128)(2,1)} reduce(bf16[2,4,32,4,4096]{4,3,1,0,2:T(4,128)(2,1)} %all_to_all.49, bf16[]{:T(256)} %constant.30.clone.1), dimensions={1}, to_apply=%region_8.9 | reduce | flops 3145728 | bytes 10485762 | tf_op jit(solution)/shard_map/reduce_sum | solution.py:111
  576.8 4.1 reshape.76
  581.0 3.2 convolution_convert_fusion.2
  (16 shorter events, 0.1 us)
Async XLA Ops:
  7.2 175.2 %copy-start = (bf16[8192,128]{1,0:T(8,128)(2,1)S(1)}, bf16[8192,128]{1,0:T(8,128)(2,1)}, u32[]{:S(2)}) copy-start(bf16[8192,128]{1,0:T(8,128)(2,1)} %param.20) | copy-start | bytes 6291460
  7.2 175.2 %all-gather.3.cloned.1.call-start = ((), (), s32[]{:S(2)}) async-start(), calls=%async_computation.4 | async-start | bytes 8650752 | tf_op jit(solution)/shard_map/all_gather | solution.py:67
  26.2 3.8 copy-start.6
  26.2 4.5 copy-start.5
  30.8 170.9 %copy-start.2 = (bf16[16,4096]{1,0:T(8,128)(2,1)S(1)}, bf16[16,4096]{1,0:T(8,128)(2,1)}, u32[]{:S(2)}) copy-start(bf16[16,4096]{1,0:T(8,128)(2,1)} %param.16) | copy-start | bytes 393220
  30.8 171.1 %copy-start.4 = (f32[4096]{0:T(1024)S(1)}, f32[4096]{0:T(1024)}, u32[]{:S(2)}) copy-start(f32[4096]{0:T(1024)} %param.17) | copy-start | bytes 49156
  188.7 13.0 %all-to-all-start = ((bf16[32,16,128]{2,1,0:T(8,128)(2,1)}), bf16[32,16,128]{2,1,0:T(8,128)(2,1)S(1)}, u32[]{:S(2)}, u32[]{:S(2)}) async-start(bf16[32,16,128]{2,1,0:T(8,128)(2,1)} %bitcast.6), calls=%async_computation | async-start | bytes 262144 | tf_op jit(solution)/shard_map/all_to_all | solution.py:71
  194.3 125.0 %all-gather.5.cloned.1.call-start = ((), (), s32[]{:S(2)}) async-start(), calls=%async_computation.5 | async-start | bytes 10485760 | tf_op jit(solution)/shard_map/all_gather | solution.py:94
  201.9 3.0 copy-start.3
  576.8 7.3 %copy-start.1 = (bf16[8192,128]{1,0:T(8,128)(2,1)S(1)}, bf16[8192,128]{1,0:T(8,128)(2,1)}, u32[]{:S(2)}) copy-start(bf16[8192,128]{1,0:T(8,128)(2,1)} %param.20) | copy-start | bytes 6291460
Sparse Core Ops, SparseCore 0:
  30.1 152.1 all-gather.2
  233.4 85.9 all-gather.4
where the time goes:
time: 593 us; the launch traced here: 591 us
  waiting for transfers between devices  245 us (41%)
  blocking collectives  221 us (37%)
  local copies, waits for them, and re-layouts  50.8 us (9%)
  matrix products  40.4 us (7%)
  between operations  14.2 us (2%)
  other arithmetic  13.7 us (2%)
    all_gather x1, waiting for transfers between devices, on_device(): lax.all_gather(attention, 'ep', axis=0, tiled=True)  152 us
    all_to_all x1, blocking collectives, on_device(): lax.all_to_all(lax.all_to_all(partial_value.astype(jnp.bfloat16), 'dp', s...  103 us
    all_to_all x1, blocking collectives, on_device(): lax.all_to_all(partial_value.astype(jnp.bfloat16), 'dp', split_axis=1, co...  96.6 us
    all_gather x1, waiting for transfers between devices, on_device(): block_rows = lax.all_gather(arrived, 'dp', axis=1, tiled=True)  86.1 us
    all_to_all x1, blocking collectives, on_device(): lax.all_to_all(outgoing, 'ep', split_axis=0, concat_axis=1, tiled=True)  21.4 us
    convert_element_type x2, local copies, waits for them, and re-layouts, on_device(): partial_value.astype(jnp.bfloat16)  18.7 us
    dot_general x1, matrix products, on_device(): jnp.einsum('enf,efd->end', hidden, w_down, preferred_element_type=jnp.flo...  15.1 us
  transfers between devices with their start and end apart: 3, of which 3 were waited for; matrix products, arithmetic and copies ran while one was open for 0% of the time, Pallas kernels for 0%

commit v1 on v0

v1 whole, which is shorter than its diff:
```python
import math

import jax
import jax.numpy as jnp
from jax import lax
from jax.experimental import pallas as pl
from jax.experimental.pallas import tpu as pltpu
from jax.sharding import Mesh, PartitionSpec as P

HEADS = 64
KVH = 4
HD = 128
TOP = 8
SLOTS = 4

DP = ("xh", "core")
EP = ("xl", "yh", "yl", "z")
SPLIT = ("yl", "z")
CHIPS = ("xh",) + EP
ALL = DP + EP
SWAP = ((0, 1), (1, 0))
MIB = 1 << 20


def attend(queries, kv_cache, kv_new, lengths):
    row_count = queries.shape[0]
    groups = HEADS // KVH
    span_len = kv_cache.shape[2]
    query_heads = queries.reshape(row_count, KVH, groups, HD)
    cache_keys = kv_cache[:, 0].reshape(row_count, span_len, KVH, HD)
    cache_values = kv_cache[:, 1].reshape(row_count, span_len, KVH, HD)
    fresh_keys = kv_new[:, 0].reshape(row_count, KVH, HD)
    fresh_values = kv_new[:, 1].reshape(row_count, KVH, HD)
    scaling = 1.0 / math.sqrt(HD)
    cache_scores = (
        jnp.einsum("rkgd,rpkd->rkgp", query_heads, cache_keys, preferred_element_type=jnp.float32)
        * scaling
    )
    live = jnp.arange(span_len, dtype=jnp.int32)[None, :] < lengths[:, None]
    cache_scores = jnp.where(live[:, None, None, :], cache_scores, -1e30)
    fresh_scores = (
        jnp.einsum("rkgd,rkd->rkg", query_heads, fresh_keys, preferred_element_type=jnp.float32)
        * scaling
    )
    highest = jnp.maximum(jnp.max(cache_scores, -1), fresh_scores)
    cache_exp = jnp.exp(cache_scores - highest[..., None])
    fresh_exp = jnp.exp(fresh_scores - highest)
    denominator = jnp.sum(cache_exp, -1) + fresh_exp
    cache_weights = (cache_exp / denominator[..., None]).astype(jnp.bfloat16)
    fresh_weights = (fresh_exp / denominator).astype(jnp.bfloat16)
    mixed = jnp.einsum(
        "rkgp,rpkd->rkgd", cache_weights, cache_values, preferred_element_type=jnp.float32
    )
    mixed = mixed + jnp.einsum(
        "rkg,rkd->rkgd", fresh_weights, fresh_values, preferred_element_type=jnp.float32
    )
    return mixed.reshape(row_count, HEADS * HD).astype(jnp.bfloat16)


def expert_kernel(
    core_ref,
    rows_hbm,
    gate_a,
    up_a,
    down_a,
    gate_b,
    up_b,
    down_b,
    out_ref,
    rows,
    gate,
    up,
    down,
    hidden,
    sems,
):
    mine = core_ref[0]
    copies = [pltpu.make_async_copy(rows_hbm, rows, sems.at[0])]
    sources = ((gate_a, gate, 0), (up_a, up, 0), (gate_b, gate, 1), (up_b, up, 1), (down_a, down, 0), (down_b, down, 1))
    for number, (source, target, place) in enumerate(sources):
        copies.append(pltpu.make_async_copy(source.at[mine], target.at[place], sems.at[number + 1]))
    for copy in copies:
        copy.start()
    copies[0].wait()
    share = gate.shape[2]
    step = 128
    for place in range(2):
        copies[1 + 2 * place].wait()
        copies[2 + 2 * place].wait()

        @pl.loop(0, share // step)
        def _(block, place=place):
            columns = pl.ds(pl.multiple_of(block * step, step), step)
            both = jnp.concatenate([gate[place, :, columns], up[place, :, columns]], axis=1)
            acts = jnp.dot(rows[...], both, preferred_element_type=jnp.float32)
            gate_act = acts[:, :step]
            value = gate_act / (1.0 + jnp.exp(-gate_act)) * acts[:, step:]
            at = pl.ds(pl.multiple_of(place * share + block * step, step), step)
            hidden[:, at] = value.astype(jnp.bfloat16)

    copies[5].wait()
    copies[6].wait()
    width = 512

    @pl.loop(0, out_ref.shape[1] // width)
    def _(block):
        columns = pl.ds(pl.multiple_of(block * width, width), width)
        both = jnp.concatenate([down[0, :, columns], down[1, :, columns]], axis=0)
        out_ref[:, columns] = jnp.dot(
            hidden[...], both, preferred_element_type=jnp.float32
        ).astype(out_ref.dtype)


def run_expert(core, rows, gate_a, up_a, down_a, gate_b, up_b, down_b):
    count, depth = rows.shape
    share = gate_a.shape[2]
    hbm = pl.BlockSpec(memory_space=pl.ANY)
    return pl.pallas_call(
        expert_kernel,
        out_shape=jax.ShapeDtypeStruct((count, depth), jnp.bfloat16),
        in_specs=[pl.BlockSpec(memory_space=pltpu.SMEM)] + [hbm] * 7,
        out_specs=pl.BlockSpec(memory_space=pltpu.VMEM),
        scratch_shapes=[
            pltpu.VMEM((count, depth), jnp.bfloat16),
            pltpu.VMEM((2, depth, share), jnp.bfloat16),
            pltpu.VMEM((2, depth, share), jnp.bfloat16),
            pltpu.VMEM((2, share, depth), jnp.bfloat16),
            pltpu.VMEM((count, 2 * share), jnp.bfloat16),
            pltpu.SemaphoreType.DMA((7,)),
        ],
        compiler_params=pltpu.CompilerParams(vmem_limit_bytes=56 * MIB),
        cost_estimate=pl.CostEstimate(
            flops=2 * count * depth * share * 6,
            bytes_accessed=2 * (2 * count * depth + 6 * depth * share),
            transcendentals=count * share * 2,
        ),
    )(core, rows, gate_a, up_a, down_a, gate_b, up_b, down_b)


def swap(value):
    return lax.ppermute(value, "core", SWAP)


def places(expert_ids, core, expert_total):
    row_count = expert_ids.shape[0]
    pair_ids = expert_ids.reshape(-1)
    member = (pair_ids[:, None] == jnp.arange(expert_total, dtype=jnp.int32)[None, :]).astype(
        jnp.int32
    )
    ranking = jnp.sum((jnp.cumsum(member, 0) - 1) * member, 1)
    here = (pair_ids % 2) == core
    slot = (pair_ids // 2) * (2 * SLOTS) + ranking
    slot = jnp.where(here, slot, -1)
    return slot.reshape(row_count, TOP)


def on_device(
    queries,
    kv_cache,
    kv_new,
    lengths,
    residual,
    norm_gain,
    expert_ids,
    route_probs,
    w_out,
    w_gate,
    w_up,
    w_down,
):
    row_count = queries.shape[0]
    core = lax.axis_index("core")
    ep_size = lax.axis_size(EP)
    parts = lax.axis_size(SPLIT)
    groups = ep_size // parts
    chips = lax.axis_size(CHIPS)
    depth = w_out.shape[0] // parts
    half = depth // 2
    width = w_out.shape[1]

    mine = lax.dynamic_index_in_dim(
        w_out.reshape(parts, 2, half, width), core, axis=1, keepdims=False
    )
    mine = lax.all_to_all(mine, SPLIT, split_axis=0, concat_axis=0, tiled=True)
    other = swap(mine)
    low = jnp.where(core == 0, mine, other)
    high = jnp.where(core == 0, other, mine)
    weights = jnp.stack([low, high], 1).reshape(parts, depth, width)
    weights = weights.transpose(1, 0, 2).reshape(depth, parts * width)

    gate_b, up_b, down_b = swap(w_gate), swap(w_up), swap(w_down)

    expert_total = w_gate.shape[0] * ep_size
    slot_total = 2 * SLOTS * ep_size
    gates = route_probs / jnp.sum(route_probs, -1, keepdims=True)
    own_slots = places(expert_ids, core, expert_total)
    other_slots = places(swap(expert_ids), core, expert_total)
    other_slots = jnp.where(other_slots >= 0, other_slots + SLOTS, -1)
    slots = jnp.concatenate([own_slots, other_slots], 0)
    both_gates = jnp.concatenate([gates, swap(gates)], 0)
    chosen = slots[:, :, None] == jnp.arange(slot_total, dtype=jnp.int32)[None, None, :]
    placing = jnp.any(chosen, 1)
    mixing = jnp.sum(jnp.where(chosen, both_gates[:, :, None], 0.0), 1)
    placing = jnp.concatenate([placing, placing], 1).astype(jnp.bfloat16)
    mixing = jnp.concatenate([mixing, mixing], 1)
    mixing_high = mixing.astype(jnp.bfloat16)
    mixing_low = (mixing - mixing_high.astype(jnp.float32)).astype(jnp.bfloat16)
    mixing = jnp.concatenate([mixing_high, mixing_low], 0)

    attention = attend(queries, kv_cache, kv_new, lengths)
    sent = attention.reshape(row_count, parts, depth).transpose(1, 0, 2)
    sent = jnp.broadcast_to(sent[None], (groups, parts, row_count, depth))
    sent = sent.reshape(ep_size, row_count, depth)
    gathered = lax.all_to_all(sent, EP, split_axis=0, concat_axis=0, tiled=True)
    columns = jnp.dot(
        gathered.reshape(ep_size * row_count, depth), weights, preferred_element_type=jnp.float32
    ).astype(jnp.bfloat16)
    terms = lax.all_to_all(
        columns.reshape(ep_size, row_count, parts * width), EP, split_axis=0, concat_axis=0, tiled=True
    )
    terms = terms.reshape(groups, parts, row_count, parts * width)
    summed = jnp.sum(terms.astype(jnp.float32), 1).astype(jnp.bfloat16)
    attn_out = summed.transpose(1, 0, 2).reshape(row_count, ep_size * width)
    stream = residual.astype(jnp.float32) + attn_out.astype(jnp.float32)
    normed = (
        stream * lax.rsqrt(jnp.mean(stream * stream, -1, keepdims=True) + 1e-06) * norm_gain
    ).astype(jnp.bfloat16)

    rows = jnp.concatenate([normed, swap(normed)], 0)
    outgoing = lax.dot_general(
        placing, rows, (((0,), (0,)), ((), ())), preferred_element_type=jnp.float32
    ).astype(jnp.bfloat16)
    arrived = lax.all_to_all(
        outgoing.reshape(chips, 2 * SLOTS, -1), CHIPS, split_axis=0, concat_axis=0, tiled=True
    )
    partial_value = run_expert(
        core.astype(jnp.int32).reshape(1),
        arrived.reshape(chips * 2 * SLOTS, -1),
        w_gate,
        w_up,
        w_down,
        gate_b,
        up_b,
        down_b,
    )
    returned = lax.all_to_all(
        partial_value.reshape(chips, 2 * SLOTS, -1), CHIPS, split_axis=0, concat_axis=0, tiled=True
    )
    mixed = jnp.dot(
        mixing, returned.reshape(chips * 2 * SLOTS, -1), preferred_element_type=jnp.float32
    )
    mixed = mixed[: 2 * row_count] + mixed[2 * row_count :]
    moe_out = mixed[:row_count] + swap(mixed[row_count:])
    return (attn_out, moe_out.astype(jnp.bfloat16))


def solution(mesh):
    fine = Mesh(mesh.devices.reshape(2, 2, 2, 2, 2, 4), ALL)
    return jax.shard_map(
        on_device,
        mesh=fine,
        in_specs=(
            P(ALL, None),
            P(ALL, None, None, None),
            P(ALL, None, None),
            P(ALL),
            P(ALL, None),
            P(),
            P(ALL, None),
            P(ALL, None),
            P(None, EP),
            P(EP, None, DP),
            P(EP, None, DP),
            P(EP, DP, None),
        ),
        out_specs=(P(ALL, None), P(ALL, None)),
        check_vma=False,
    )
```

time: 593 us -> 237 us (0.40)
  blocking collectives: 221 us -> 0 us
  waiting for transfers between devices: 245 us -> 127 us
  starting transfers between devices: 5.7 us -> 50.3 us
  local copies, waits for them, and re-layouts: 50.8 us -> 19.3 us
  matrix products: 40.4 us -> 14.7 us
  Pallas kernels: 0 us -> 18.5 us
  between operations: 14.2 us -> 1 us
  other arithmetic: 13.7 us -> 3.47 us
    all_gather x2 -> x0, waiting for transfers between devices: 238 us -> none  [the longest x1 152 us: on_device(): lax.all_gather(attention, 'ep', axis=0, tiled=True)]
    all_to_all x3 -> x0, blocking collectives: 221 us -> none  [the longest x1 103 us: on_device(): lax.all_to_all(lax.all_to_all(partial_value.astype(jnp.bfloat16), 'dp', s...]
    all_to_all x1 -> x5, waiting for transfers between devices: 7.09 us -> 124 us  [the longest x1 53.2 us: on_device(): lax.all_to_all(outgoing.reshape(chips, 2 * SLOTS, -1), CHIPS, split_axis=...]
    all_to_all x1 -> x5, starting transfers between devices: 5.62 us -> 39.1 us  [the longest x1 12 us: on_device(): lax.all_to_all(partial_value.reshape(chips, 2 * SLOTS, -1), CHIPS, split_...]
    dot_general x5 -> x3, matrix products: 34.2 us -> 10.7 us  [the longest x1 4.22 us: on_device(): jnp.dot(gathered.reshape(ep_size * row_count, depth), weights, preferred_...]
    convert_element_type x2 -> x1, local copies, waits for them, and re-layouts: 18.7 us -> 0.12 us  [attend(): return mixed.reshape(row_count, HEADS * HD).astype(jnp.bfloat16)]
    pallas_call x0 -> x1, Pallas kernels: none -> 18.5 us  [run_expert(): pl.pallas_call(expert_kernel, out_shape=jax.ShapeDtypeStruct((count, dept...]
    ppermute x0 -> x8, starting transfers between devices: none -> 11.1 us  [swap(): return lax.ppermute(value, 'core', SWAP)]
  transfers between devices with their start and end apart: 3 -> 13, of which waited for: 3 -> 8; matrix products, arithmetic and copies ran while one was open for 0% -> 13% of each run, Pallas kernels for 0% -> 0%
where the time goes in v1:
time: 237 us; the launch traced here: 234 us
  waiting for transfers between devices  127 us (54%)
  starting transfers between devices  50.3 us (21%)
  local copies, waits for them, and re-layouts  19.3 us (8%)
  Pallas kernels  18.5 us (8%)
  matrix products  14.7 us (6%)
  other arithmetic  3.47 us (1%)
    all_to_all x1, waiting for transfers between devices, on_device(): lax.all_to_all(outgoing.reshape(chips, 2 * SLOTS, -1), CHIPS, split_axis=...  53.2 us
    all_to_all x1, waiting for transfers between devices, on_device(): lax.all_to_all(partial_value.reshape(chips, 2 * SLOTS, -1), CHIPS, split_...  45 us
    pallas_call x1, Pallas kernels, run_expert(): pl.pallas_call(expert_kernel, out_shape=jax.ShapeDtypeStruct((count, dept...  18.5 us
    all_to_all x1, waiting for transfers between devices, on_device(): lax.all_to_all(columns.reshape(ep_size, row_count, parts * width), EP, sp...  13.7 us
    all_to_all x1, starting transfers between devices, on_device(): lax.all_to_all(partial_value.reshape(chips, 2 * SLOTS, -1), CHIPS, split_...  12 us
    all_to_all x1, waiting for transfers between devices, on_device(): gathered = lax.all_to_all(sent, EP, split_axis=0, concat_axis=0, tiled=True)  11.2 us
    ppermute x8, starting transfers between devices, swap(): return lax.ppermute(value, 'core', SWAP)  11.1 us
    unnamed x26, local copies, waits for them, and re-layouts  9.06 us
  transfers between devices with their start and end apart: 13, of which 8 were waited for; matrix products, arithmetic and copies ran while one was open for 13% of the time, Pallas kernels for 0%

profile of v1, /device:TPU:1, one launch (start us, length us, event | category | flops | bytes accessed | tf_op | source)
XLA Modules:
  0.0 234.5 jit_solution(3927377297715840740)
XLA Ops:
  0.7 1.6 copy-done
  2.2 1.0 dynamic-slice_bitcast_fusion
  3.3 6.9 %all-to-all-start.1 = ((bf16[8,512,128]{2,1,0:T(8,128)(2,1)}), bf16[8,512,128]{2,1,0:T(8,128)(2,1)S(1)}, u32[]{:S(2)}, u32[]{:S(2)}) async-start(bf16[8,512,128]{2,1,0:T(8,128)(2,1)} %dynamic-slice_bitcast_fusion), calls=%async_computation.1 | async-start | bytes 2097152 | tf_op jit(solution)/shard_map/all_to_all | solution.py:184
  10.2 4.6 %fusion.44 = (bf16[16,1,128,512]{3,2,1,0:T(8,128)(2,1)}, bf16[16,1,128,512]{3,2,1,0:T(8,128)(2,1)}) fusion(bf16[16,2,128,512]{3,2,1,0:T(8,128)(2,1)} %param.13), kind=kLoop, calls=%fused_computation.89 | loop fusion | bytes 8388608 | tf_op jit(solution)/shard_map/slice | solution.py:30
  14.9 0.2 fusion.24
  15.2 3.0 %copy.94 = bf16[16,1,128,512]{2,3,0,1:T(8,128)(2,1)S(1)} copy(bf16[16,1,128,512]{3,2,1,0:T(8,128)(2,1)} %get-tuple-element.2) | data formatting | bytes 4194304
  18.2 3.9 %copy.95 = bf16[16,1,128,512]{2,3,0,1:T(8,128)(2,1)} copy(bf16[16,1,128,512]{3,2,1,0:T(8,128)(2,1)} %get-tuple-element.3) | data formatting | bytes 4194304
  22.2 0.7 fusion.45
  23.0 0.4 fusion.5
  23.4 0.3 copy-done.2
  23.8 1.3 all-to-all-done.1
  25.1 0.8 collective-permute-start
  25.9 3.0 %fusion.4 = bf16[16,4,16,128]{3,2,1,0:T(8,128)(2,1)S(1)} fusion(bf16[16,128,4,128]{1,3,2,0:T(8,128)(2,1)} %bitcast.55, f32[16,4,16,128]{3,2,1,0:T(8,128)} %copy-done.2, f32[16,4,128]{2,1,0:T(4,128)S(1)} %bitcast.67, f32[16,4,16]{2,1,0:T(4,128)S(1)} %get-tuple-element.7, f32[16,4,16]{2,1,0:T(4,128)S(1)} %get-tuple-element.6, ...), kind=kOutput, calls=%fused_computation.9 | convolution fusion | flops 34340864 | bytes 2928640 | tf_op jit(solution)/shard_map/rkgp,rpkd->rkgd/dot_general | solution.py:51
  29.1 0.2 copy.78
  29.2 1.1 broadcast_in_dim.33
  30.4 7.2 %all-to-all-start = ((bf16[32,16,1024]{2,1,0:T(8,128)(2,1)}), bf16[32,16,1024]{2,1,0:T(8,128)(2,1)}, u32[]{:S(2)}, u32[]{:S(2)}) async-start(bf16[32,16,1024]{2,1,0:T(8,128)(2,1)} %bitcast.7), calls=%async_computation | async-start | bytes 2097152 | tf_op jit(solution)/shard_map/all_to_all | solution.py:214
  37.7 0.3 collective-permute-start.1
  38.0 0.2 collective-permute-start.4
  38.2 0.3 collective-permute-start.5
  38.5 0.2 collective-permute-start.6
  39.0 0.2 pad_maximum_fusion
  39.2 2.7 %copy.81 = bf16[1024,8,128]{0,2,1:T(8,128)(2,1)} copy(bf16[1024,8,128]{2,0,1:T(8,128)(2,1)S(1)} %bitcast.54) | data formatting | bytes 4194304 | tf_op jit(solution)/shard_map/transpose | solution.py:189
  41.8 11.2 %all-to-all-done = bf16[32,16,1024]{2,1,0:T(8,128)(2,1)} async-done(((bf16[32,16,1024]{2,1,0:T(8,128)(2,1)}), bf16[32,16,1024]{2,1,0:T(8,128)(2,1)}, u32[]{:S(2)}, u32[]{:S(2)}) %all-to-all-start) | async-done | bytes 1048608 | tf_op jit(solution)/shard_map/all_to_all | solution.py:214
  53.0 4.2 %convolution_convert_fusion.1 = bf16[512,1024]{1,0:T(8,128)(2,1)} fusion(bf16[512,1024]{1,0:T(8,128)(2,1)} %bitcast.8, bf16[1024,1024]{0,1:T(8,128)(2,1)} %bitcast.56), kind=kOutput, calls=%fused_computation.5 | convolution fusion | flops 1074266112 | bytes 4194304 | tf_op jit(solution)/shard_map/dot_general | solution.py:215
  57.3 5.8 %all-to-all-start.2 = ((bf16[32,16,1024]{2,1,0:T(8,128)(2,1)}), bf16[32,16,1024]{2,1,0:T(8,128)(2,1)S(1)}, u32[]{:S(2)}, u32[]{:S(2)}) async-start(bf16[32,16,1024]{2,1,0:T(8,128)(2,1)} %bitcast.17), calls=%async_computation.2 | async-start | bytes 2097152 | tf_op jit(solution)/shard_map/all_to_all | solution.py:218
  63.1 0.2 reduce_window_sum.17
  63.3 0.2 select_reduce_fusion.2
  63.8 0.2 reduce_window_sum.18
  64.0 0.2 select_reduce_fusion.1
  64.3 13.7 %all-to-all-done.2 = bf16[32,16,1024]{2,1,0:T(8,128)(2,1)S(1)} async-done(((bf16[32,16,1024]{2,1,0:T(8,128)(2,1)}), bf16[32,16,1024]{2,1,0:T(8,128)(2,1)S(1)}, u32[]{:S(2)}, u32[]{:S(2)}) %all-to-all-start.2) | async-done | bytes 1048608 | tf_op jit(solution)/shard_map/all_to_all | solution.py:218
  78.0 0.2 bitcast_reduce_fusion
  78.2 0.2 multiply_reduce_fusion
  78.4 2.6 %collective-permute-start.3 = (bf16[16,4096]{1,0:T(8,128)(2,1)S(1)}, bf16[16,4096]{1,0:T(8,128)(2,1)S(1)}, u32[]{:S(2)}, u32[]{:S(2)}) collective-permute-start(bf16[16,4096]{1,0:T(8,128)(2,1)S(1)} %multiply_convert_fusion), channel_id=1, source_target_pairs={{0,32},{32,0},{1,33},{33,1},{2,34},{34,2},{3,35},{35,3},{4,36},{36... | collective-permute-start | bytes 393224 | tf_op jit(solution)/shard_map/ppermute | solution.py:141
  81.0 0.2 fusion.10
  81.2 0.8 collective-permute-done.3
  82.0 3.3 %fusion = bf16[64,8,4096]{2,1,0:T(8,128)(2,1)} fusion(bf16[16,4096]{1,0:T(8,128)(2,1)S(1)} %collective-permute-done.3, bf16[16,4096]{1,0:T(8,128)(2,1)S(1)} %multiply_convert_fusion, pred[32,256]{1,0:T(8,128)(4,1)S(1)} %fusion.10), kind=kOutput, calls=%fused_computation.1 | convolution fusion | flops 136855552 | bytes 4464640 | tf_op jit(solution)/shard_map/dot_general | solution.py:230
  85.3 7.3 %all-to-all-start.3 = ((bf16[64,8,4096]{2,1,0:T(8,128)(2,1)}), bf16[64,8,4096]{2,1,0:T(8,128)(2,1)}, u32[]{:S(2)}, u32[]{:S(2)}) async-start(bf16[64,8,4096]{2,1,0:T(8,128)(2,1)} %fusion), calls=%async_computation.3 | async-start | bytes 8388608 | tf_op jit(solution)/shard_map/all_to_all | solution.py:233
  92.7 53.2 %all-to-all-done.3 = bf16[64,8,4096]{2,1,0:T(8,128)(2,1)} async-done(((bf16[64,8,4096]{2,1,0:T(8,128)(2,1)}), bf16[64,8,4096]{2,1,0:T(8,128)(2,1)}, u32[]{:S(2)}, u32[]{:S(2)}) %all-to-all-start.3) | async-done | bytes 4194336 | tf_op jit(solution)/shard_map/all_to_all | solution.py:233
  145.9 18.5 %shard_map.131 = bf16[512,4096]{1,0:T(8,128)(2,1)} custom-call(s32[1]{0:T(128)} %bitcast.20.core_ref, bf16[512,4096]{1,0:T(8,128)(2,1)} %bitcast.22.rows_hbm, bf16[2,4096,384]{2,1,0:T(8,128)(2,1)} %gate_a.1, bf16[2,4096,384]{2,1,0:T(8,128)(2,1)} %up_a.1, bf16[2,384,4096]{2,1,0:T(8,128)(2,1)} %down_a.1, bf16[2,4096,384]{2,1,0:T(8,128)(2,1)} %collective-permute-done.4.gate_b, ...), custom_call_target="tpu_custom_call" | custom-call | flops 9663676416 | bytes 27262976 | tf_op jit(solution)/shard_map/pallas_call | solution.py:118
  164.5 12.0 %all-to-all-start.4 = ((bf16[64,8,4096]{2,1,0:T(8,128)(2,1)}), bf16[64,8,4096]{2,1,0:T(8,128)(2,1)}, u32[]{:S(2)}, u32[]{:S(2)}) async-start(bf16[64,8,4096]{2,1,0:T(8,128)(2,1)} %bitcast.52), calls=%async_computation.4 | async-start | bytes 8388608 | tf_op jit(solution)/shard_map/all_to_all | solution.py:246
  176.5 2.2 collective-permute-start.2
  178.7 0.8 collective-permute-done.2
  179.7 0.2 select_reduce_fusion
  179.8 45.0 %all-to-all-done.4 = bf16[64,8,4096]{2,1,0:T(8,128)(2,1)} async-done(((bf16[64,8,4096]{2,1,0:T(8,128)(2,1)}), bf16[64,8,4096]{2,1,0:T(8,128)(2,1)}, u32[]{:S(2)}, u32[]{:S(2)}) %all-to-all-start.4) | async-done | bytes 4194336 | tf_op jit(solution)/shard_map/all_to_all | solution.py:246
  224.9 3.2 %fusion.1 = f32[64,4096]{1,0:T(8,128)S(1)} fusion(bf16[64,8,4096]{2,1,0:T(8,128)(2,1)} %all-to-all-done.4, bf16[32,512]{1,0:T(8,128)(2,1)S(1)} %fusion.15, bf16[32,512]{1,0:T(8,128)(2,1)S(1)} %fusion.14), kind=kOutput, calls=%fused_computation.2 | convolution fusion | flops 268566528 | bytes 5308416 | tf_op jit(solution)/shard_map/dot_general | solution.py:249
  228.1 4.5 %collective-permute-start.7 = (f32[16,4096]{1,0:T(8,128)S(1)}, f32[16,4096]{1,0:T(8,128)S(1)}, u32[]{:S(2)}, u32[]{:S(2)}) collective-permute-start(f32[16,4096]{1,0:T(8,128)S(1)} %slice.35), channel_id=1, source_target_pairs={{0,32},{32,0},{1,33},{33,1},{2,34},{34,2},{3,35},{35,3},{4,36},{36... | collective-permute-start | bytes 786440 | tf_op jit(solution)/shard_map/ppermute | solution.py:141
  232.6 1.2 collective-permute-done.7
  233.8 0.7 fusion.6
  (53 shorter events, 1.6 us)
Async XLA Ops:
  0.6 1.6 copy-start
  3.3 21.8 %all-to-all-start.1 = ((bf16[8,512,128]{2,1,0:T(8,128)(2,1)}), bf16[8,512,128]{2,1,0:T(8,128)(2,1)S(1)}, u32[]{:S(2)}, u32[]{:S(2)}) async-start(bf16[8,512,128]{2,1,0:T(8,128)(2,1)} %dynamic-slice_bitcast_fusion), calls=%async_computation.1 | async-start | bytes 2097152 | tf_op jit(solution)/shard_map/all_to_all | solution.py:184
  10.1 4.7 %copy-start.5 = (bf16[16,8192]{1,0:T(8,128)(2,1)S(1)}, bf16[16,8192]{1,0:T(8,128)(2,1)}, u32[]{:S(2)}) copy-start(bf16[16,8192]{1,0:T(8,128)(2,1)} %param.12) | copy-start | bytes 786436
  10.1 4.7 %copy-start.6 = (bf16[16,2,512]{2,1,0:T(2,128)(2,1)S(1)}, bf16[16,2,512]{2,1,0:T(2,128)(2,1)}, u32[]{:S(2)}) copy-start(bf16[16,2,512]{2,1,0:T(2,128)(2,1)} %param.14) | copy-start | bytes 98308
  10.2 5.0 %copy-start.10 = (s32[16]{0:T(128)S(1)}, s32[16]{0:T(128)}, u32[]{:S(2)}) copy-start(s32[16]{0:T(128)} %param.15) | copy-start | bytes 196
  22.9 0.8 copy-start.2
  25.1 13.8 %collective-permute-start = (bf16[8,512,128]{2,1,0:T(8,128)(2,1)S(1)}, bf16[8,512,128]{2,1,0:T(8,128)(2,1)S(1)}, u32[]{:S(2)}, u32[]{:S(2)}) collective-permute-start(bf16[8,512,128]{2,1,0:T(8,128)(2,1)S(1)} %all-to-all-done.1), channel_id=1, source_target_pairs={{0,32},{32,0},{1,33},{33,1},{2,34},{34,2},{3,35},{35,3},{4,36},{36... | collective-permute-start | bytes 3145736 | tf_op jit(solution)/shard_map/ppermute | solution.py:141
  29.1 8.5 %copy-start.9 = (s32[16,8]{0,1:T(8,128)S(1)}, s32[16,8]{0,1:T(8,128)}, u32[]{:S(2)}) copy-start(s32[16,8]{0,1:T(8,128)} %param.18) | copy-start | bytes 1540
  30.4 22.7 %all-to-all-start = ((bf16[32,16,1024]{2,1,0:T(8,128)(2,1)}), bf16[32,16,1024]{2,1,0:T(8,128)(2,1)}, u32[]{:S(2)}, u32[]{:S(2)}) async-start(bf16[32,16,1024]{2,1,0:T(8,128)(2,1)} %bitcast.7), calls=%async_computation | async-start | bytes 2097152 | tf_op jit(solution)/shard_map/all_to_all | solution.py:214
  37.7 25.9 %collective-permute-start.1 = (s32[16,8]{1,0:T(8,128)S(1)}, s32[16,8]{1,0:T(8,128)S(1)}, u32[]{:S(2)}, u32[]{:S(2)}) collective-permute-start(s32[16,8]{1,0:T(8,128)S(1)} %copy.83), channel_id=1, source_target_pairs={{0,32},{32,0},{1,33},{33,1},{2,34},{34,2},{3,35},{35,3},{4,36},{36... | collective-permute-start | bytes 1544 | tf_op jit(solution)/shard_map/ppermute | solution.py:141
  38.0 54.7 %collective-permute-start.4 = (bf16[2,4096,384]{2,1,0:T(8,128)(2,1)}, bf16[2,4096,384]{2,1,0:T(8,128)(2,1)}, u32[]{:S(2)}, u32[]{:S(2)}) collective-permute-start(bf16[2,4096,384]{2,1,0:T(8,128)(2,1)} %gate_a.1), channel_id=1, source_target_pairs={{0,32},{32,0},{1,33},{33,1},{2,34},{34,2},{3,35},{35,3},{4,36},{36... | collective-permute-start | bytes 18874376 | tf_op jit(solution)/shard_map/ppermute | solution.py:141
  38.2 54.5 %collective-permute-start.5 = (bf16[2,4096,384]{2,1,0:T(8,128)(2,1)}, bf16[2,4096,384]{2,1,0:T(8,128)(2,1)}, u32[]{:S(2)}, u32[]{:S(2)}) collective-permute-start(bf16[2,4096,384]{2,1,0:T(8,128)(2,1)} %up_a.1), channel_id=1, source_target_pairs={{0,32},{32,0},{1,33},{33,1},{2,34},{34,2},{3,35},{35,3},{4,36},{36... | collective-permute-start | bytes 18874376 | tf_op jit(solution)/shard_map/ppermute | solution.py:141
  38.5 54.2 %collective-permute-start.6 = (bf16[2,384,4096]{2,1,0:T(8,128)(2,1)}, bf16[2,384,4096]{2,1,0:T(8,128)(2,1)}, u32[]{:S(2)}, u32[]{:S(2)}) collective-permute-start(bf16[2,384,4096]{2,1,0:T(8,128)(2,1)} %down_a.1), channel_id=1, source_target_pairs={{0,32},{32,0},{1,33},{33,1},{2,34},{34,2},{3,35},{35,3},{4,36},{36... | collective-permute-start | bytes 18874376 | tf_op jit(solution)/shard_map/ppermute | solution.py:141
  57.3 20.9 %copy-start.4 = (bf16[16,4096]{1,0:T(8,128)(2,1)S(1)}, bf16[16,4096]{1,0:T(8,128)(2,1)}, u32[]{:S(2)}) copy-start(bf16[16,4096]{1,0:T(8,128)(2,1)} %param.16) | copy-start | bytes 393220
  57.3 21.1 %copy-start.7 = (f32[4096]{0:T(1024)S(1)}, f32[4096]{0:T(1024)}, u32[]{:S(2)}) copy-start(f32[4096]{0:T(1024)} %param.17) | copy-start | bytes 49156
  57.3 20.7 %all-to-all-start.2 = ((bf16[32,16,1024]{2,1,0:T(8,128)(2,1)}), bf16[32,16,1024]{2,1,0:T(8,128)(2,1)S(1)}, u32[]{:S(2)}, u32[]{:S(2)}) async-start(bf16[32,16,1024]{2,1,0:T(8,128)(2,1)} %bitcast.17), calls=%async_computation.2 | async-start | bytes 2097152 | tf_op jit(solution)/shard_map/all_to_all | solution.py:218
  78.1 7.2 %copy-start.3 = (bf16[4,2,8,1024]{3,2,0,1:T(8,128)(2,1)}, bf16[4,2,8,1024]{3,2,0,1:T(8,128)(2,1)S(1)}, u32[]{:S(2)}) copy-start(bf16[4,2,8,1024]{3,2,0,1:T(8,128)(2,1)S(1)} %copy.97) | copy-start | bytes 393220
  78.4 3.6 %collective-permute-start.3 = (bf16[16,4096]{1,0:T(8,128)(2,1)S(1)}, bf16[16,4096]{1,0:T(8,128)(2,1)S(1)}, u32[]{:S(2)}, u32[]{:S(2)}) collective-permute-start(bf16[16,4096]{1,0:T(8,128)(2,1)S(1)} %multiply_convert_fusion), channel_id=1, source_target_pairs={{0,32},{32,0},{1,33},{33,1},{2,34},{34,2},{3,35},{35,3},{4,36},{36... | collective-permute-start | bytes 393224 | tf_op jit(solution)/shard_map/ppermute | solution.py:141
  85.3 60.6 %all-to-all-start.3 = ((bf16[64,8,4096]{2,1,0:T(8,128)(2,1)}), bf16[64,8,4096]{2,1,0:T(8,128)(2,1)}, u32[]{:S(2)}, u32[]{:S(2)}) async-start(bf16[64,8,4096]{2,1,0:T(8,128)(2,1)} %fusion), calls=%async_computation.3 | async-start | bytes 8388608 | tf_op jit(solution)/shard_map/all_to_all | solution.py:233
  164.5 12.0 %copy-start.8 = (f32[16,8]{0,1:T(8,128)S(1)}, f32[16,8]{0,1:T(8,128)}, u32[]{:S(2)}) copy-start(f32[16,8]{0,1:T(8,128)} %param.19) | copy-start | bytes 1540
  164.5 60.4 %all-to-all-start.4 = ((bf16[64,8,4096]{2,1,0:T(8,128)(2,1)}), bf16[64,8,4096]{2,1,0:T(8,128)(2,1)}, u32[]{:S(2)}, u32[]{:S(2)}) async-start(bf16[64,8,4096]{2,1,0:T(8,128)(2,1)} %bitcast.52), calls=%async_computation.4 | async-start | bytes 8388608 | tf_op jit(solution)/shard_map/all_to_all | solution.py:246
  176.5 3.0 %collective-permute-start.2 = (f32[16,8]{0,1:T(8,128)S(1)}, f32[16,8]{0,1:T(8,128)S(1)}, u32[]{:S(2)}, u32[]{:S(2)}) collective-permute-start(f32[16,8]{0,1:T(8,128)S(1)} %broadcast_divide_fusion), channel_id=1, source_target_pairs={{0,32},{32,0},{1,33},{33,1},{2,34},{34,2},{3,35},{35,3},{4,36},{36... | collective-permute-start | bytes 1544 | tf_op jit(solution)/shard_map/ppermute | solution.py:141
  224.9 9.6 %copy-start.1 = (bf16[8192,128]{1,0:T(8,128)(2,1)S(1)}, bf16[8192,128]{1,0:T(8,128)(2,1)}, u32[]{:S(2)}) copy-start(bf16[8192,128]{1,0:T(8,128)(2,1)} %param.20) | copy-start | bytes 6291460
  228.1 5.7 %collective-permute-start.7 = (f32[16,4096]{1,0:T(8,128)S(1)}, f32[16,4096]{1,0:T(8,128)S(1)}, u32[]{:S(2)}, u32[]{:S(2)}) collective-permute-start(f32[16,4096]{1,0:T(8,128)S(1)} %slice.35), channel_id=1, source_target_pairs={{0,32},{32,0},{1,33},{33,1},{2,34},{34,2},{3,35},{35,3},{4,36},{36... | collective-permute-start | bytes 786440 | tf_op jit(solution)/shard_map/ppermute | solution.py:141

commit v2 on v1

v2 whole, which is shorter than its diff:
```python
import functools
import math

import jax
import jax.numpy as jnp
from jax import lax
from jax.experimental import pallas as pl
from jax.experimental.pallas import tpu as pltpu
from jax.sharding import Mesh, PartitionSpec as P

HEADS = 64
KVH = 4
HD = 128
TOP = 8
SLOTS = 4

DP = ("xh", "core")
EP = ("xl", "yh", "yl", "z")
SPLIT = ("yl", "z")
CHIPS = ("xh",) + EP
ALL = DP + EP
SWAP = ((0, 1), (1, 0))
MIB = 1 << 20
BLOCK = 128
WIDE = 512
PIECE = 1024
AHEAD = 8


def attend_kernel(lengths_ref, queries_ref, cache_hbm, fresh_ref, out_ref, cache, heads, sems, *, parts, copies):
    rows = queries_ref.shape[0]
    batch = rows // sems.shape[0]
    span = cache.shape[2]
    moves = []
    for number in range(sems.shape[0]):
        at = pl.ds(number * batch, batch)
        moves.append(pltpu.make_async_copy(cache_hbm.at[at], cache.at[at], sems.at[number]))
        moves[-1].start()
    groups = HEADS // KVH
    scaling = 1.0 / math.sqrt(HD)
    for head in range(HEADS):
        heads[pl.ds(head, rows, stride=HEADS), :] = queries_ref[:, head * HD : (head + 1) * HD].astype(jnp.float32)
    position = lax.broadcasted_iota(jnp.int32, (HEADS, span), 1)
    for row in range(rows):
        if row % batch == 0:
            moves[row // batch].wait()
        at = slice(row * HEADS, (row + 1) * HEADS)
        query = heads[at, :]
        query16 = query.astype(jnp.bfloat16)
        scores = []
        fresh = []
        for k in range(KVH):
            cols = slice(k * HD, (k + 1) * HD)
            own = slice(k * groups, (k + 1) * groups)
            scores.append(
                lax.dot_general(
                    query16[own], cache[row, 0, :, cols], (((1,), (1,)), ((), ())), preferred_element_type=jnp.float32
                )
            )
            key = fresh_ref[row, 0:1, cols].astype(jnp.float32)
            fresh.append(jnp.sum(query[own] * key, axis=1, keepdims=True))
        scores = jnp.concatenate(scores, 0) * scaling
        fresh = jnp.concatenate(fresh, 0) * scaling
        scores = jnp.where(position < lengths_ref[row], scores, -1e30)
        highest = jnp.maximum(jnp.max(scores, axis=1, keepdims=True), fresh)
        scores = jnp.exp(scores - highest)
        fresh = jnp.exp(fresh - highest)
        denominator = jnp.sum(scores, axis=1, keepdims=True) + fresh
        weights = (scores / denominator).astype(jnp.bfloat16)
        fresh = (fresh / denominator).astype(jnp.bfloat16).astype(jnp.float32)
        mixed = []
        for k in range(KVH):
            cols = slice(k * HD, (k + 1) * HD)
            own = slice(k * groups, (k + 1) * groups)
            value = jnp.dot(weights[own], cache[row, 1, :, cols], preferred_element_type=jnp.float32)
            mixed.append(value + fresh[own] * fresh_ref[row, 1:2, cols].astype(jnp.float32))
        heads[at, :] = jnp.concatenate(mixed, 0)
    share = HEADS // parts
    for head in range(HEADS):
        value = heads[pl.ds(head, rows, stride=HEADS), :].astype(jnp.bfloat16)
        cols = slice(head % share * HD, (head % share + 1) * HD)
        for copy in range(copies):
            out_ref[copy * parts + head // share, :, cols] = value

def run_attend(queries, kv_cache, kv_new, lengths, parts, copies):
    rows = queries.shape[0]
    return pl.pallas_call(
        functools.partial(attend_kernel, parts=parts, copies=copies),
        out_shape=jax.ShapeDtypeStruct((copies * parts, rows, HEADS * HD // parts), jnp.bfloat16),
        in_specs=[pl.BlockSpec(memory_space=pltpu.SMEM), pl.BlockSpec(memory_space=pltpu.VMEM), pl.BlockSpec(memory_space=pl.ANY), pl.BlockSpec(memory_space=pltpu.VMEM)],
        out_specs=pl.BlockSpec(memory_space=pltpu.VMEM),
        scratch_shapes=[pltpu.VMEM(kv_cache.shape, jnp.bfloat16), pltpu.VMEM((rows * HEADS, HD), jnp.float32), pltpu.SemaphoreType.DMA((4,))],
        compiler_params=pltpu.CompilerParams(vmem_limit_bytes=24 * MIB),
        cost_estimate=pl.CostEstimate(
            flops=4 * kv_cache.size // 2 * HEADS // KVH,
            bytes_accessed=2 * (kv_cache.size + 5 * queries.size),
            transcendentals=rows * HEADS * kv_cache.shape[2],
        ),
        name="attend",
    )(lengths, queries, kv_cache, kv_new)


def expert_kernel(
    core_ref, rows_hbm, gate_a, up_a, down_a, gate_b, up_b, down_b, out_hbm, rows, gate, up, down, hidden, out, sems, out_sems
):
    mine = core_ref[0]
    depth = rows.shape[1]
    share = gate.shape[2]
    blocks = share // BLOCK
    pieces = depth // PIECE
    moves = []

    def move(source, target):
        moves.append(pltpu.make_async_copy(source, target, sems.at[len(moves)]))
        return len(moves) - 1

    def at(block):
        return pl.ds(block * BLOCK, BLOCK)

    in_gate = ((gate_a, gate.at[0]), (gate_b, gate.at[1]))
    in_up = ((up_a, up.at[0]), (up_b, up.at[1]))
    in_down = ((down_a, down.at[0]), (down_b, down.at[1]))
    first = []
    for piece in range(pieces):
        part = pl.ds(piece * PIECE, PIECE)
        for source, target in (in_gate[0], in_up[0]):
            last = move(source.at[mine, part, at(0)], target.at[part, at(0)])
        last = move(rows_hbm.at[:, part], rows.at[:, part])
        first.append(last)
    later = {}
    for place in range(2):
        for block in range(blocks):
            if place + block > 0:
                for source, target in (in_gate[place], in_up[place]):
                    later[place, block] = move(source.at[mine, :, at(block)], target.at[:, at(block)])
    finals = []
    for block in range(depth // WIDE):
        part = pl.ds(block * WIDE, WIDE)
        for source, target in in_down:
            last = move(source.at[mine, :, part], target.at[:, part])
        finals.append(last)

    state = {"started": 0, "waited": 0}

    def reach(number):
        while state["started"] < min(len(moves), number + 1 + AHEAD):
            moves[state["started"]].start()
            state["started"] += 1
        while state["waited"] <= number:
            moves[state["waited"]].wait()
            state["waited"] += 1

    for place in range(2):
        for block in range(blocks):
            cols = slice(block * BLOCK, (block + 1) * BLOCK)
            if place + block == 0:
                acts = None
                for piece in range(pieces):
                    reach(first[piece])
                    part = slice(piece * PIECE, (piece + 1) * PIECE)
                    both = jnp.concatenate([gate[place, part, cols], up[place, part, cols]], axis=1)
                    term = jnp.dot(rows[:, part], both, preferred_element_type=jnp.float32)
                    acts = term if acts is None else acts + term
            else:
                reach(later[place, block])
                both = jnp.concatenate([gate[place, :, cols], up[place, :, cols]], axis=1)
                acts = jnp.dot(rows[...], both, preferred_element_type=jnp.float32)
            gate_act = acts[:, :BLOCK]
            value = gate_act / (1.0 + jnp.exp(-gate_act)) * acts[:, BLOCK:]
            start = place * share + block * BLOCK
            hidden[:, start : start + BLOCK] = value.astype(jnp.bfloat16)

    stores = []
    for block in range(depth // WIDE):
        reach(finals[block])
        cols = slice(block * WIDE, (block + 1) * WIDE)
        both = jnp.concatenate([down[0, :, cols], down[1, :, cols]], axis=0)
        out[:, cols] = jnp.dot(hidden[...], both, preferred_element_type=jnp.float32).astype(out.dtype)
        part = pl.ds(block * WIDE, WIDE)
        stores.append(pltpu.make_async_copy(out.at[:, part], out_hbm.at[:, part], out_sems.at[block]))
        stores[-1].start()
    for store in stores:
        store.wait()


def run_expert(core, rows, gate_a, up_a, down_a, gate_b, up_b, down_b):
    count, depth = rows.shape
    share = gate_a.shape[2]
    moves = 3 * (depth // PIECE) + 2 * (2 * share // BLOCK - 1) + 2 * (depth // WIDE)
    hbm = pl.BlockSpec(memory_space=pl.ANY)
    return pl.pallas_call(
        expert_kernel,
        out_shape=jax.ShapeDtypeStruct((count, depth), jnp.bfloat16),
        in_specs=[pl.BlockSpec(memory_space=pltpu.SMEM)] + [hbm] * 7,
        out_specs=hbm,
        scratch_shapes=[
            pltpu.VMEM((count, depth), jnp.bfloat16),
            pltpu.VMEM((2, depth, share), jnp.bfloat16),
            pltpu.VMEM((2, depth, share), jnp.bfloat16),
            pltpu.VMEM((2, share, depth), jnp.bfloat16),
            pltpu.VMEM((count, 2 * share), jnp.bfloat16),
            pltpu.VMEM((count, depth), jnp.bfloat16),
            pltpu.SemaphoreType.DMA((moves,)),
            pltpu.SemaphoreType.DMA((depth // WIDE,)),
        ],
        compiler_params=pltpu.CompilerParams(vmem_limit_bytes=48 * MIB),
        cost_estimate=pl.CostEstimate(
            flops=2 * count * depth * share * 6,
            bytes_accessed=2 * (2 * count * depth + 6 * depth * share),
            transcendentals=count * share * 2,
        ),
        name="expert",
    )(core, rows, gate_a, up_a, down_a, gate_b, up_b, down_b)


def project_kernel(core_ref, rows_ref, mine_ref, other_ref, out_ref):
    mine = core_ref[0]
    half = mine_ref.shape[1]
    width = mine_ref.shape[2]
    near = rows_ref[:, pl.ds(pl.multiple_of(mine * half, half), half)]
    far = rows_ref[:, pl.ds(pl.multiple_of((1 - mine) * half, half), half)]
    for block in range(0, mine_ref.shape[0], 2):
        weights = jnp.concatenate([mine_ref[block], mine_ref[block + 1]], axis=1)
        total = jnp.dot(near, weights, preferred_element_type=jnp.float32)
        weights = jnp.concatenate([other_ref[block], other_ref[block + 1]], axis=1)
        total += jnp.dot(far, weights, preferred_element_type=jnp.float32)
        out_ref[:, block * width : (block + 2) * width] = total.astype(out_ref.dtype)


def run_project(core, rows, mine, other):
    count, depth = rows.shape
    width = mine.shape[0] * mine.shape[2]
    vmem = pl.BlockSpec(memory_space=pltpu.VMEM)
    return pl.pallas_call(
        project_kernel,
        out_shape=jax.ShapeDtypeStruct((count, width), jnp.bfloat16),
        in_specs=[pl.BlockSpec(memory_space=pltpu.SMEM)] + [vmem] * 3,
        out_specs=vmem,
        compiler_params=pltpu.CompilerParams(vmem_limit_bytes=16 * MIB),
        cost_estimate=pl.CostEstimate(
            flops=2 * count * depth * width,
            bytes_accessed=2 * (count * depth + count * width + depth * width),
            transcendentals=0,
        ),
        name="project",
    )(core, rows, mine, other)


def norm_kernel(terms_ref, residual_ref, gain_ref, out_ref, normed_ref, *, parts):
    width = terms_ref.shape[2]
    streams = []
    squares = None
    for group in range(terms_ref.shape[0] // parts):
        cols = slice(group * width, (group + 1) * width)
        total = terms_ref[group * parts].astype(jnp.float32)
        for part in range(1, parts):
            total += terms_ref[group * parts + part].astype(jnp.float32)
        total = total.astype(jnp.bfloat16)
        out_ref[:, cols] = total
        stream = residual_ref[:, cols].astype(jnp.float32) + total.astype(jnp.float32)
        square = jnp.sum(stream * stream, axis=1, keepdims=True)
        squares = square if squares is None else squares + square
        streams.append(stream)
    scale = lax.rsqrt(squares / out_ref.shape[1] + 1e-06)
    for group, stream in enumerate(streams):
        cols = slice(group * width, (group + 1) * width)
        normed_ref[:, cols] = (stream * scale * gain_ref[:, cols]).astype(jnp.bfloat16)


def run_norm(terms, residual, gain, parts):
    vmem = pl.BlockSpec(memory_space=pltpu.VMEM)
    return pl.pallas_call(
        functools.partial(norm_kernel, parts=parts),
        out_shape=[jax.ShapeDtypeStruct(residual.shape, jnp.bfloat16)] * 2,
        in_specs=[vmem] * 3,
        out_specs=[vmem] * 2,
        compiler_params=pltpu.CompilerParams(vmem_limit_bytes=16 * MIB),
        cost_estimate=pl.CostEstimate(
            flops=2 * terms.size, bytes_accessed=2 * terms.size, transcendentals=0
        ),
        name="norm",
    )(terms, residual, gain.reshape(1, -1))


def swap(value):
    return lax.ppermute(value, "core", SWAP)


def places(expert_ids, core, expert_total):
    row_count = expert_ids.shape[0]
    pair_ids = expert_ids.reshape(-1)
    member = (pair_ids[:, None] == jnp.arange(expert_total, dtype=jnp.int32)[None, :]).astype(
        jnp.int32
    )
    ranking = jnp.sum((jnp.cumsum(member, 0) - 1) * member, 1)
    here = (pair_ids % 2) == core
    slot = (pair_ids // 2) * (2 * SLOTS) + ranking
    slot = jnp.where(here, slot, -1)
    return slot.reshape(row_count, TOP)


def on_device(
    queries,
    kv_cache,
    kv_new,
    lengths,
    residual,
    norm_gain,
    expert_ids,
    route_probs,
    w_out,
    w_gate,
    w_up,
    w_down,
):
    row_count = queries.shape[0]
    core = lax.axis_index("core")
    core_index = core.astype(jnp.int32).reshape(1)
    ep_size = lax.axis_size(EP)
    parts = lax.axis_size(SPLIT)
    groups = ep_size // parts
    chips = lax.axis_size(CHIPS)
    depth = w_out.shape[0] // parts
    half = depth // 2
    width = w_out.shape[1]

    mine = lax.dynamic_index_in_dim(
        w_out.reshape(parts, 2, half, width), core, axis=1, keepdims=False
    )
    mine = lax.all_to_all(mine, SPLIT, split_axis=0, concat_axis=0, tiled=True)
    other = swap(mine)

    gate_b, up_b, down_b = swap(w_gate), swap(w_up), swap(w_down)

    expert_total = w_gate.shape[0] * ep_size
    slot_total = 2 * SLOTS * ep_size
    gates = route_probs / jnp.sum(route_probs, -1, keepdims=True)
    own_slots = places(expert_ids, core, expert_total)
    other_slots = places(swap(expert_ids), core, expert_total)
    other_slots = jnp.where(other_slots >= 0, other_slots + SLOTS, -1)
    slots = jnp.concatenate([own_slots, other_slots], 0)
    both_gates = jnp.concatenate([gates, swap(gates)], 0)
    chosen = slots[:, :, None] == jnp.arange(slot_total, dtype=jnp.int32)[None, None, :]
    placing = jnp.any(chosen, 1)
    mixing = jnp.sum(jnp.where(chosen, both_gates[:, :, None], 0.0), 1)
    placing = jnp.concatenate([placing, placing], 1).astype(jnp.bfloat16)
    mixing = jnp.concatenate([mixing, mixing], 1)
    mixing_high = mixing.astype(jnp.bfloat16)
    mixing_low = (mixing - mixing_high.astype(jnp.float32)).astype(jnp.bfloat16)
    mixing = jnp.concatenate([mixing_high, mixing_low], 0)

    sent = run_attend(queries, kv_cache, kv_new, lengths, parts, groups)
    gathered = lax.all_to_all(sent, EP, split_axis=0, concat_axis=0, tiled=True)
    columns = run_project(core_index, gathered.reshape(ep_size * row_count, depth), mine, other)
    terms = lax.all_to_all(
        columns.reshape(ep_size, row_count, parts * width), EP, split_axis=0, concat_axis=0, tiled=True
    )
    attn_out, normed = run_norm(terms, residual, norm_gain, parts)

    rows = jnp.concatenate([normed, swap(normed)], 0)
    outgoing = lax.dot_general(
        placing, rows, (((0,), (0,)), ((), ())), preferred_element_type=jnp.float32
    ).astype(jnp.bfloat16)
    arrived = lax.all_to_all(
        outgoing.reshape(chips, 2 * SLOTS, -1), CHIPS, split_axis=0, concat_axis=0, tiled=True
    )
    partial_value = run_expert(
        core_index,
        arrived.reshape(chips * 2 * SLOTS, -1),
        w_gate,
        w_up,
        w_down,
        gate_b,
        up_b,
        down_b,
    )
    returned = lax.all_to_all(
        partial_value.reshape(chips, 2 * SLOTS, -1), CHIPS, split_axis=0, concat_axis=0, tiled=True
    )
    mixed = jnp.dot(
        mixing, returned.reshape(chips * 2 * SLOTS, -1), preferred_element_type=jnp.float32
    )
    mixed = mixed[: 2 * row_count] + mixed[2 * row_count :]
    moe_out = mixed[:row_count] + swap(mixed[row_count:])
    return (attn_out, moe_out.astype(jnp.bfloat16))


def solution(mesh):
    fine = Mesh(mesh.devices.reshape(2, 2, 2, 2, 2, 4), ALL)
    return jax.shard_map(
        on_device,
        mesh=fine,
        in_specs=(
            P(ALL, None),
            P(ALL, None, None, None),
            P(ALL, None, None),
            P(ALL),
            P(ALL, None),
            P(),
            P(ALL, None),
            P(ALL, None),
            P(None, EP),
            P(EP, None, DP),
            P(EP, None, DP),
            P(EP, DP, None),
        ),
        out_specs=(P(ALL, None), P(ALL, None)),
        check_vma=False,
    )
```

time: 237 us -> 249 us (1.051)
  blocking collectives: 0 us -> 21.2 us
  Pallas kernels: 18.5 us -> 37.1 us
  local copies, waits for them, and re-layouts: 19.3 us -> 5.86 us
  matrix products: 14.7 us -> 6.34 us
  starting transfers between devices: 50.3 us -> 43.5 us
    all_to_all x0 -> x1, blocking collectives: none -> 21.2 us  [on_device(): mine = lax.all_to_all(mine, SPLIT, split_axis=0, concat_axis=0, tiled=True)]
    pallas_call x0 -> x3, Pallas kernels: none -> 15.2 us  [the longest x1 10.9 us: run_attend(): pl.pallas_call(functools.partial(attend_kernel, parts=parts, copies=copie...]
    dot_general x4 -> x0, matrix products: 8.23 us -> none  [the longest x1 4.22 us: on_device(): jnp.dot(gathered.reshape(ep_size * row_count, depth), weights, preferred_...]
    all_to_all x1 -> x0, starting transfers between devices: 6.88 us -> none  [on_device(): mine = lax.all_to_all(mine, SPLIT, split_axis=0, concat_axis=0, tiled=True)]
    slice x1 -> x0, local copies, waits for them, and re-layouts: 4.64 us -> none  [attend(): cache_keys = kv_cache[:, 0].reshape(row_count, span_len, KVH, HD)]
    unnamed x26 -> x23, local copies, waits for them, and re-layouts: 9.06 us -> 5.37 us
    pallas_call x1, Pallas kernels: 18.5 us -> 22 us  [run_expert(): pl.pallas_call(expert_kernel, out_shape=jax.ShapeDtypeStruct((count, dept...]
    all_to_all x1, waiting for transfers between devices: 11.2 us -> 14.2 us  [on_device(): gathered = lax.all_to_all(sent, EP, split_axis=0, concat_axis=0, tiled=True)]
  transfers between devices with their start and end apart: 13 -> 12, of which waited for: 8 -> 7; matrix products, arithmetic and copies ran while one was open for 13% -> 2% of each run, Pallas kernels for 0% -> 6%
where the time goes in v2:
time: 249 us; the launch traced here: 246 us
  waiting for transfers between devices  129 us (52%)
  starting transfers between devices  43.5 us (17%)
  Pallas kernels  37.1 us (15%)
  blocking collectives  21.2 us (9%)
  matrix products  6.34 us (3%)
  local copies, waits for them, and re-layouts  5.86 us (2%)
    all_to_all x1, waiting for transfers between devices, on_device(): lax.all_to_all(outgoing.reshape(chips, 2 * SLOTS, -1), CHIPS, split_axis=...  53.2 us
    all_to_all x1, waiting for transfers between devices, on_device(): lax.all_to_all(partial_value.reshape(chips, 2 * SLOTS, -1), CHIPS, split_...  45 us
    pallas_call x1, Pallas kernels, run_expert(): pl.pallas_call(expert_kernel, out_shape=jax.ShapeDtypeStruct((count, dept...  22 us
    all_to_all x1, blocking collectives, on_device(): mine = lax.all_to_all(mine, SPLIT, split_axis=0, concat_axis=0, tiled=True)  21.2 us
    all_to_all x1, waiting for transfers between devices, on_device(): gathered = lax.all_to_all(sent, EP, split_axis=0, concat_axis=0, tiled=True)  14.2 us
    all_to_all x1, waiting for transfers between devices, on_device(): lax.all_to_all(columns.reshape(ep_size, row_count, parts * width), EP, sp...  13.7 us
    ppermute x8, starting transfers between devices, swap(): return lax.ppermute(value, 'core', SWAP)  12.7 us
    all_to_all x1, starting transfers between devices, on_device(): lax.all_to_all(partial_value.reshape(chips, 2 * SLOTS, -1), CHIPS, split_...  12.1 us
  transfers between devices with their start and end apart: 12, of which 7 were waited for; matrix products, arithmetic and copies ran while one was open for 2% of the time, Pallas kernels for 6%

profile of v2, /device:TPU:1, one launch (start us, length us, event | category | flops | bytes accessed | tf_op | source)
XLA Modules:
  0.0 246.0 jit_solution(8610036045648844466)
XLA Ops:
  0.7 1.6 copy-done
  2.2 0.1 dynamic-slice_bitcast_fusion
  2.3 21.2 %all_to_all.25.mine_ref = bf16[8,512,128]{2,1,0:T(8,128)(2,1)S(1)} all-to-all(bf16[8,512,128]{2,1,0:T(8,128)(2,1)S(1)} %dynamic-slice_bitcast_fusion), channel_id=1, replica_groups=mesh['xh'=2,'core'=2,'xl'=2,'yh'=2,'yl'=2,'z'=4] {'yl','z'}, dimensions={0} | all-to-all | bytes 2097152 | tf_op jit(solution)/shard_map/all_to_all | solution.py:330
  23.5 2.4 collective-permute-start
  26.0 0.9 copy-done.4
  26.9 0.8 copy-done.6
  27.7 10.9 %attend.1 = bf16[32,16,1024]{2,1,0:T(8,128)(2,1)} custom-call(s32[16]{0:T(128)S(1)} %copy-done.8, bf16[16,8192]{1,0:T(8,128)(2,1)S(1)} %copy-done.4, bf16[16,2,128,512]{3,2,1,0:T(8,128)(2,1)S(1)} %copy-done.3, bf16[16,2,512]{2,1,0:T(2,128)(2,1)S(1)} %copy-done.6), custom_call_target="tpu_custom_call" | custom-call | flops 67108864 | bytes 5505024 | tf_op jit(solution)/shard_map/attend/pallas_call | solution.py:87
  38.6 5.7 %all-to-all-start = ((bf16[32,16,1024]{2,1,0:T(8,128)(2,1)}), bf16[32,16,1024]{2,1,0:T(8,128)(2,1)S(1)}, u32[]{:S(2)}, u32[]{:S(2)}) async-start(bf16[32,16,1024]{2,1,0:T(8,128)(2,1)} %attend.1), calls=%async_computation | async-start | bytes 2097152 | tf_op jit(solution)/shard_map/all_to_all | solution.py:353
  44.3 0.4 collective-permute-start.4
  44.7 0.2 collective-permute-start.5
  44.9 0.3 collective-permute-start.6
  45.2 0.1 copy.42
  45.3 0.2 collective-permute-start.1
  45.5 0.1 eq.60
  45.6 14.2 %all-to-all-done = bf16[32,16,1024]{2,1,0:T(8,128)(2,1)S(1)} async-done(((bf16[32,16,1024]{2,1,0:T(8,128)(2,1)}), bf16[32,16,1024]{2,1,0:T(8,128)(2,1)S(1)}, u32[]{:S(2)}, u32[]{:S(2)}) %all-to-all-start) | async-done | bytes 1048608 | tf_op jit(solution)/shard_map/all_to_all | solution.py:353
  59.8 3.5 %project.1 = bf16[512,1024]{1,0:T(8,128)(2,1)} custom-call(s32[1]{0:T(128)} %bitcast.core_ref, bf16[512,1024]{1,0:T(8,128)(2,1)S(1)} %bitcast.18, bf16[8,512,128]{2,1,0:T(8,128)(2,1)S(1)} %all_to_all.25.mine_ref, bf16[8,512,128]{2,1,0:T(8,128)(2,1)} %collective-permute-done.other_ref), custom_call_target="tpu_custom_call" | custom-call | flops 1073741824 | bytes 4194304 | tf_op jit(solution)/shard_map/project/pallas_call | solution.py:234
  63.3 5.6 %all-to-all-start.2 = ((bf16[32,16,1024]{2,1,0:T(8,128)(2,1)}), bf16[32,16,1024]{2,1,0:T(8,128)(2,1)S(1)}, u32[]{:S(2)}, u32[]{:S(2)}) async-start(bf16[32,16,1024]{2,1,0:T(8,128)(2,1)} %bitcast.4), calls=%async_computation.2 | async-start | bytes 2097152 | tf_op jit(solution)/shard_map/all_to_all | solution.py:355
  68.9 0.1 fusion.15
  69.0 0.2 reduce_window_sum.17
  69.2 0.2 select_reduce_fusion.2
  69.3 0.1 reduce_sum.41
  69.5 0.1 eq.65
  69.6 0.1 fusion.14
  69.6 0.2 reduce_window_sum.18
  69.8 0.2 select_reduce_fusion.1
  70.0 0.1 reduce_sum.43
  70.1 13.7 %all-to-all-done.2.terms_ref = bf16[32,16,1024]{2,1,0:T(8,128)(2,1)S(1)} async-done(((bf16[32,16,1024]{2,1,0:T(8,128)(2,1)}), bf16[32,16,1024]{2,1,0:T(8,128)(2,1)S(1)}, u32[]{:S(2)}, u32[]{:S(2)}) %all-to-all-start.2) | async-done | bytes 1048608 | tf_op jit(solution)/shard_map/all_to_all | solution.py:355
  83.8 0.8 norm.1
  84.6 2.5 %collective-permute-start.3 = (bf16[16,4096]{1,0:T(8,128)(2,1)S(1)}, bf16[16,4096]{1,0:T(8,128)(2,1)S(1)}, u32[]{:S(2)}, u32[]{:S(2)}) collective-permute-start(bf16[16,4096]{1,0:T(8,128)(2,1)S(1)} %get-tuple-element.5), channel_id=1, source_target_pairs={{0,32},{32,0},{1,33},{33,1},{2,34},{34,2},{3,35},{35,3},{4,36},{36... | collective-permute-start | bytes 393224 | tf_op jit(solution)/shard_map/ppermute | solution.py:286
  87.2 0.2 fusion.7
  87.3 0.8 collective-permute-done.3
  88.1 3.3 %fusion = bf16[64,8,4096]{2,1,0:T(8,128)(2,1)} fusion(bf16[16,4096]{1,0:T(8,128)(2,1)S(1)} %collective-permute-done.3, bf16[16,4096]{1,0:T(8,128)(2,1)S(1)} %get-tuple-element.5, pred[32,256]{1,0:T(8,128)(4,1)S(1)} %fusion.7), kind=kOutput, calls=%fused_computation.1 | convolution fusion | flops 136855552 | bytes 4464640 | tf_op jit(solution)/shard_map/dot_general | solution.py:361
  91.5 7.3 %all-to-all-start.3 = ((bf16[64,8,4096]{2,1,0:T(8,128)(2,1)}), bf16[64,8,4096]{2,1,0:T(8,128)(2,1)}, u32[]{:S(2)}, u32[]{:S(2)}) async-start(bf16[64,8,4096]{2,1,0:T(8,128)(2,1)} %fusion), calls=%async_computation.3 | async-start | bytes 8388608 | tf_op jit(solution)/shard_map/all_to_all | solution.py:364
  98.8 53.2 %all-to-all-done.3 = bf16[64,8,4096]{2,1,0:T(8,128)(2,1)} async-done(((bf16[64,8,4096]{2,1,0:T(8,128)(2,1)}), bf16[64,8,4096]{2,1,0:T(8,128)(2,1)}, u32[]{:S(2)}, u32[]{:S(2)}) %all-to-all-start.3) | async-done | bytes 4194336 | tf_op jit(solution)/shard_map/all_to_all | solution.py:364
  152.0 22.0 %expert.1 = bf16[512,4096]{1,0:T(8,128)(2,1)S(1)} custom-call(s32[1]{0:T(128)} %bitcast.core_ref, bf16[512,4096]{1,0:T(8,128)(2,1)} %bitcast.7.rows_hbm, bf16[2,4096,384]{2,1,0:T(8,128)(2,1)} %gate_a.1, bf16[2,4096,384]{2,1,0:T(8,128)(2,1)} %up_a.1, bf16[2,384,4096]{2,1,0:T(8,128)(2,1)} %down_a.1, bf16[2,4096,384]{2,1,0:T(8,128)(2,1)} %collective-permute-done.4.gate_b, ...), custom_call_target="tpu_custom_call" | custom-call | flops 9663676416 | bytes 27262976 | tf_op jit(solution)/shard_map/expert/pallas_call | solution.py:191
  174.0 2.0 copy-done.2
  176.0 12.1 %all-to-all-start.4 = ((bf16[64,8,4096]{2,1,0:T(8,128)(2,1)}), bf16[64,8,4096]{2,1,0:T(8,128)(2,1)}, u32[]{:S(2)}, u32[]{:S(2)}) async-start(bf16[64,8,4096]{2,1,0:T(8,128)(2,1)} %bitcast.17), calls=%async_computation.4 | async-start | bytes 8388608 | tf_op jit(solution)/shard_map/all_to_all | solution.py:377
  188.2 2.2 collective-permute-start.2
  190.3 0.8 collective-permute-done.2
  191.2 0.1 pad_maximum_fusion.1
  191.2 0.1 copy.48
  191.3 0.2 select_reduce_fusion
  191.5 45.0 %all-to-all-done.4 = bf16[64,8,4096]{2,1,0:T(8,128)(2,1)} async-done(((bf16[64,8,4096]{2,1,0:T(8,128)(2,1)}), bf16[64,8,4096]{2,1,0:T(8,128)(2,1)}, u32[]{:S(2)}, u32[]{:S(2)}) %all-to-all-start.4) | async-done | bytes 4194336 | tf_op jit(solution)/shard_map/all_to_all | solution.py:377
  236.5 3.0 %fusion.1 = f32[64,4096]{1,0:T(8,128)S(1)} fusion(bf16[64,8,4096]{2,1,0:T(8,128)(2,1)} %all-to-all-done.4, bf16[32,512]{1,0:T(8,128)(2,1)S(1)} %fusion.10, bf16[32,512]{1,0:T(8,128)(2,1)S(1)} %fusion.9), kind=kOutput, calls=%fused_computation.2 | convolution fusion | flops 268566528 | bytes 5308416 | tf_op jit(solution)/shard_map/dot_general | solution.py:380
  239.5 0.1 slice_add_fusion
  239.6 4.5 %collective-permute-start.7 = (f32[16,4096]{1,0:T(8,128)S(1)}, f32[16,4096]{1,0:T(8,128)S(1)}, u32[]{:S(2)}, u32[]{:S(2)}) collective-permute-start(f32[16,4096]{1,0:T(8,128)S(1)} %slice.19), channel_id=1, source_target_pairs={{0,32},{32,0},{1,33},{33,1},{2,34},{34,2},{3,35},{35,3},{4,36},{36... | collective-permute-start | bytes 786440 | tf_op jit(solution)/shard_map/ppermute | solution.py:286
  244.1 1.2 collective-permute-done.7
  245.3 0.7 fusion.3
  (31 shorter events, 0.2 us)
Async XLA Ops:
  0.6 1.6 copy-start
  0.6 25.3 %copy-start.8 = (s32[16]{0:T(128)S(1)}, s32[16]{0:T(128)}, u32[]{:S(2)}) copy-start(s32[16]{0:T(128)} %lengths_ref.1) | copy-start | bytes 196
  2.2 23.8 %copy-start.3 = (bf16[16,2,128,512]{3,2,1,0:T(8,128)(2,1)S(1)}, bf16[16,2,128,512]{3,2,1,0:T(8,128)(2,1)}, u32[]{:S(2)}) copy-start(bf16[16,2,128,512]{3,2,1,0:T(8,128)(2,1)} %cache_hbm.1) | copy-start | bytes 12582916
  23.5 36.3 %collective-permute-start = (bf16[8,512,128]{2,1,0:T(8,128)(2,1)S(1)}, bf16[8,512,128]{2,1,0:T(8,128)(2,1)}, u32[]{:S(2)}, u32[]{:S(2)}) collective-permute-start(bf16[8,512,128]{2,1,0:T(8,128)(2,1)S(1)} %all_to_all.25.mine_ref), channel_id=1, source_target_pairs={{0,32},{32,0},{1,33},{33,1},{2,34},{34,2},{3,35},{35,3},{4,36},{36... | collective-permute-start | bytes 3145736 | tf_op jit(solution)/shard_map/ppermute | solution.py:286
  26.0 1.0 copy-start.4
  26.9 0.8 copy-start.6
  27.7 17.5 %copy-start.10 = (s32[16,8]{0,1:T(8,128)S(1)}, s32[16,8]{0,1:T(8,128)}, u32[]{:S(2)}) copy-start(s32[16,8]{0,1:T(8,128)} %param.18) | copy-start | bytes 1540
  38.6 45.2 %copy-start.5 = (bf16[16,4096]{1,0:T(8,128)(2,1)S(1)}, bf16[16,4096]{1,0:T(8,128)(2,1)}, u32[]{:S(2)}) copy-start(bf16[16,4096]{1,0:T(8,128)(2,1)} %residual_ref.1) | copy-start | bytes 393220
  38.6 45.2 %copy-start.7 = (f32[4096]{0:T(1024)S(1)}, f32[4096]{0:T(1024)}, u32[]{:S(2)}) copy-start(f32[4096]{0:T(1024)} %param.17) | copy-start | bytes 49156
  38.6 21.2 %all-to-all-start = ((bf16[32,16,1024]{2,1,0:T(8,128)(2,1)}), bf16[32,16,1024]{2,1,0:T(8,128)(2,1)S(1)}, u32[]{:S(2)}, u32[]{:S(2)}) async-start(bf16[32,16,1024]{2,1,0:T(8,128)(2,1)} %attend.1), calls=%async_computation | async-start | bytes 2097152 | tf_op jit(solution)/shard_map/all_to_all | solution.py:353
  44.3 54.5 %collective-permute-start.4 = (bf16[2,4096,384]{2,1,0:T(8,128)(2,1)}, bf16[2,4096,384]{2,1,0:T(8,128)(2,1)}, u32[]{:S(2)}, u32[]{:S(2)}) collective-permute-start(bf16[2,4096,384]{2,1,0:T(8,128)(2,1)} %gate_a.1), channel_id=1, source_target_pairs={{0,32},{32,0},{1,33},{33,1},{2,34},{34,2},{3,35},{35,3},{4,36},{36... | collective-permute-start | bytes 18874376 | tf_op jit(solution)/shard_map/ppermute | solution.py:286
  44.7 54.1 %collective-permute-start.5 = (bf16[2,4096,384]{2,1,0:T(8,128)(2,1)}, bf16[2,4096,384]{2,1,0:T(8,128)(2,1)}, u32[]{:S(2)}, u32[]{:S(2)}) collective-permute-start(bf16[2,4096,384]{2,1,0:T(8,128)(2,1)} %up_a.1), channel_id=1, source_target_pairs={{0,32},{32,0},{1,33},{33,1},{2,34},{34,2},{3,35},{35,3},{4,36},{36... | collective-permute-start | bytes 18874376 | tf_op jit(solution)/shard_map/ppermute | solution.py:286
  44.9 53.9 %collective-permute-start.6 = (bf16[2,384,4096]{2,1,0:T(8,128)(2,1)}, bf16[2,384,4096]{2,1,0:T(8,128)(2,1)}, u32[]{:S(2)}, u32[]{:S(2)}) collective-permute-start(bf16[2,384,4096]{2,1,0:T(8,128)(2,1)} %down_a.1), channel_id=1, source_target_pairs={{0,32},{32,0},{1,33},{33,1},{2,34},{34,2},{3,35},{35,3},{4,36},{36... | collective-permute-start | bytes 18874376 | tf_op jit(solution)/shard_map/ppermute | solution.py:286
  45.3 24.2 %collective-permute-start.1 = (s32[16,8]{1,0:T(8,128)S(1)}, s32[16,8]{1,0:T(8,128)S(1)}, u32[]{:S(2)}, u32[]{:S(2)}) collective-permute-start(s32[16,8]{1,0:T(8,128)S(1)} %copy.42), channel_id=1, source_target_pairs={{0,32},{32,0},{1,33},{33,1},{2,34},{34,2},{3,35},{35,3},{4,36},{36... | collective-permute-start | bytes 1544 | tf_op jit(solution)/shard_map/ppermute | solution.py:286
  63.3 20.5 %all-to-all-start.2 = ((bf16[32,16,1024]{2,1,0:T(8,128)(2,1)}), bf16[32,16,1024]{2,1,0:T(8,128)(2,1)S(1)}, u32[]{:S(2)}, u32[]{:S(2)}) async-start(bf16[32,16,1024]{2,1,0:T(8,128)(2,1)} %bitcast.4), calls=%async_computation.2 | async-start | bytes 2097152 | tf_op jit(solution)/shard_map/all_to_all | solution.py:355
  84.6 3.5 %collective-permute-start.3 = (bf16[16,4096]{1,0:T(8,128)(2,1)S(1)}, bf16[16,4096]{1,0:T(8,128)(2,1)S(1)}, u32[]{:S(2)}, u32[]{:S(2)}) collective-permute-start(bf16[16,4096]{1,0:T(8,128)(2,1)S(1)} %get-tuple-element.5), channel_id=1, source_target_pairs={{0,32},{32,0},{1,33},{33,1},{2,34},{34,2},{3,35},{35,3},{4,36},{36... | collective-permute-start | bytes 393224 | tf_op jit(solution)/shard_map/ppermute | solution.py:286
  91.5 60.6 %all-to-all-start.3 = ((bf16[64,8,4096]{2,1,0:T(8,128)(2,1)}), bf16[64,8,4096]{2,1,0:T(8,128)(2,1)}, u32[]{:S(2)}, u32[]{:S(2)}) async-start(bf16[64,8,4096]{2,1,0:T(8,128)(2,1)} %fusion), calls=%async_computation.3 | async-start | bytes 8388608 | tf_op jit(solution)/shard_map/all_to_all | solution.py:364
  174.0 2.0 copy-start.2
  176.0 12.1 %copy-start.9 = (f32[16,8]{0,1:T(8,128)S(1)}, f32[16,8]{0,1:T(8,128)}, u32[]{:S(2)}) copy-start(f32[16,8]{0,1:T(8,128)} %param.19) | copy-start | bytes 1540
  176.0 60.5 %all-to-all-start.4 = ((bf16[64,8,4096]{2,1,0:T(8,128)(2,1)}), bf16[64,8,4096]{2,1,0:T(8,128)(2,1)}, u32[]{:S(2)}, u32[]{:S(2)}) async-start(bf16[64,8,4096]{2,1,0:T(8,128)(2,1)} %bitcast.17), calls=%async_computation.4 | async-start | bytes 8388608 | tf_op jit(solution)/shard_map/all_to_all | solution.py:377
  188.1 57.9 %copy-start.1 = (bf16[8192,128]{1,0:T(8,128)(2,1)S(1)}, bf16[8192,128]{1,0:T(8,128)(2,1)}, u32[]{:S(2)}) copy-start(bf16[8192,128]{1,0:T(8,128)(2,1)} %param.20) | copy-start | bytes 6291460
  188.2 3.0 %collective-permute-start.2 = (f32[16,8]{0,1:T(8,128)S(1)}, f32[16,8]{0,1:T(8,128)S(1)}, u32[]{:S(2)}, u32[]{:S(2)}) collective-permute-start(f32[16,8]{0,1:T(8,128)S(1)} %broadcast_divide_fusion), channel_id=1, source_target_pairs={{0,32},{32,0},{1,33},{33,1},{2,34},{34,2},{3,35},{35,3},{4,36},{36... | collective-permute-start | bytes 1544 | tf_op jit(solution)/shard_map/ppermute | solution.py:286
  239.6 5.7 %collective-permute-start.7 = (f32[16,4096]{1,0:T(8,128)S(1)}, f32[16,4096]{1,0:T(8,128)S(1)}, u32[]{:S(2)}, u32[]{:S(2)}) collective-permute-start(f32[16,4096]{1,0:T(8,128)S(1)} %slice.19), channel_id=1, source_target_pairs={{0,32},{32,0},{1,33},{33,1},{2,34},{34,2},{3,35},{35,3},{4,36},{36... | collective-permute-start | bytes 786440 | tf_op jit(solution)/shard_map/ppermute | solution.py:286

commit v3 on v2

--- a/solution.py
+++ b/solution.py
@@ -22,9 +22,7 @@
 SWAP = ((0, 1), (1, 0))
 MIB = 1 << 20
 BLOCK = 128
-WIDE = 512
-PIECE = 1024
-AHEAD = 8
+WIDE = 1024
 
 
 def attend_kernel(lengths_ref, queries_ref, cache_hbm, fresh_ref, out_ref, cache, heads, sems, *, parts, copies):
@@ -86,8 +84,8 @@
     rows = queries.shape[0]
     return pl.pallas_call(
         functools.partial(attend_kernel, parts=parts, copies=copies),
-        out_shape=jax.ShapeDtypeStruct((copies * parts, rows, HEADS * HD // parts), jnp.bfloat16),
-        in_specs=[pl.BlockSpec(memory_space=pltpu.SMEM), pl.BlockSpec(memory_space=pltpu.VMEM), pl.BlockSpec(memory_space=pl.ANY), pl.BlockSpec(memory_space=pltpu.VMEM)],
+        out_shape=pltpu.HBM((copies * parts, rows, HEADS * HD // parts), jnp.bfloat16),
+        in_specs=[pl.BlockSpec(memory_space=pltpu.SMEM), pl.BlockSpec(memory_space=pltpu.VMEM), pl.BlockSpec(memory_space=pltpu.HBM), pl.BlockSpec(memory_space=pltpu.VMEM)],
         out_specs=pl.BlockSpec(memory_space=pltpu.VMEM),
         scratch_shapes=[pltpu.VMEM(kv_cache.shape, jnp.bfloat16), pltpu.VMEM((rows * HEADS, HD), jnp.float32), pltpu.SemaphoreType.DMA((4,))],
         compiler_params=pltpu.CompilerParams(vmem_limit_bytes=24 * MIB),
@@ -97,100 +95,93 @@
             transcendentals=rows * HEADS * kv_cache.shape[2],
         ),
         name="attend",
-    )(lengths, queries, kv_cache, kv_new)
+    )(lengths, queries, pltpu.with_memory_space_constraint(kv_cache, pltpu.HBM), kv_new)
 
 
 def expert_kernel(
     core_ref, rows_hbm, gate_a, up_a, down_a, gate_b, up_b, down_b, out_hbm, rows, gate, up, down, hidden, out, sems, out_sems
 ):
     mine = core_ref[0]
-    depth = rows.shape[1]
+    count, depth = rows.shape
     share = gate.shape[2]
-    blocks = share // BLOCK
-    pieces = depth // PIECE
     moves = []
 
     def move(source, target):
         moves.append(pltpu.make_async_copy(source, target, sems.at[len(moves)]))
-        return len(moves) - 1
-
-    def at(block):
-        return pl.ds(block * BLOCK, BLOCK)
-
-    in_gate = ((gate_a, gate.at[0]), (gate_b, gate.at[1]))
-    in_up = ((up_a, up.at[0]), (up_b, up.at[1]))
-    in_down = ((down_a, down.at[0]), (down_b, down.at[1]))
-    first = []
-    for piece in range(pieces):
-        part = pl.ds(piece * PIECE, PIECE)
-        for source, target in (in_gate[0], in_up[0]):
-            last = move(source.at[mine, part, at(0)], target.at[part, at(0)])
-        last = move(rows_hbm.at[:, part], rows.at[:, part])
-        first.append(last)
-    later = {}
-    for place in range(2):
-        for block in range(blocks):
-            if place + block > 0:
-                for source, target in (in_gate[place], in_up[place]):
-                    later[place, block] = move(source.at[mine, :, at(block)], target.at[:, at(block)])
-    finals = []
-    for block in range(depth // WIDE):
-        part = pl.ds(block * WIDE, WIDE)
-        for source, target in in_down:
-            last = move(source.at[mine, :, part], target.at[:, part])
-        finals.append(last)
-
-    state = {"started": 0, "waited": 0}
-
-    def reach(number):
-        while state["started"] < min(len(moves), number + 1 + AHEAD):
-            moves[state["started"]].start()
-            state["started"] += 1
-        while state["waited"] <= number:
-            moves[state["waited"]].wait()
-            state["waited"] += 1
-
-    for place in range(2):
-        for block in range(blocks):
-            cols = slice(block * BLOCK, (block + 1) * BLOCK)
-            if place + block == 0:
-                acts = None
-                for piece in range(pieces):
-                    reach(first[piece])
-                    part = slice(piece * PIECE, (piece + 1) * PIECE)
-                    both = jnp.concatenate([gate[place, part, cols], up[place, part, cols]], axis=1)
-                    term = jnp.dot(rows[:, part], both, preferred_element_type=jnp.float32)
-                    acts = term if acts is None else acts + term
-            else:
-                reach(later[place, block])
+        return moves[-1:]
+
+    def halves(source, target):
+        size = target.shape[0] // 2
+        found = []
+        for half in range(2):
+            at = pl.ds(half * size, size)
+            found += move(source.at[at], target.at[at])
+        return found
+
+    def block_of(start):
+        at = pl.ds(start, BLOCK)
+        return move(gate_a.at[mine, :, at], gate.at[0, :, at]) + move(up_a.at[mine, :, at], up.at[0, :, at])
+
+    def start_all(copies):
+        for copy in copies:
+            copy.start()
+
+    def wait_all(copies):
+        for copy in copies:
+            copy.wait()
+
+    def step(*places):
+        @pl.when(mine >= 0)
+        def _():
+            for place, start in places:
+                cols = slice(start, start + BLOCK)
                 both = jnp.concatenate([gate[place, :, cols], up[place, :, cols]], axis=1)
                 acts = jnp.dot(rows[...], both, preferred_element_type=jnp.float32)
-            gate_act = acts[:, :BLOCK]
-            value = gate_act / (1.0 + jnp.exp(-gate_act)) * acts[:, BLOCK:]
-            start = place * share + block * BLOCK
-            hidden[:, start : start + BLOCK] = value.astype(jnp.bfloat16)
-
-    stores = []
-    for block in range(depth // WIDE):
-        reach(finals[block])
-        cols = slice(block * WIDE, (block + 1) * WIDE)
-        both = jnp.concatenate([down[0, :, cols], down[1, :, cols]], axis=0)
-        out[:, cols] = jnp.dot(hidden[...], both, preferred_element_type=jnp.float32).astype(out.dtype)
-        part = pl.ds(block * WIDE, WIDE)
-        stores.append(pltpu.make_async_copy(out.at[:, part], out_hbm.at[:, part], out_sems.at[block]))
-        stores[-1].start()
-    for store in stores:
-        store.wait()
+                gate_act = acts[:, :BLOCK]
+                value = gate_act / (1.0 + jnp.exp(-gate_act)) * acts[:, BLOCK:]
+                at = place * share + start
+                hidden[:, at : at + BLOCK] = value.astype(jnp.bfloat16)
+
+    blocks = range(0, share, BLOCK)
+    quarter = count // 4
+    first = block_of(0)
+    for part in range(4):
+        at = pl.ds(part * quarter, quarter)
+        first += move(rows_hbm.at[at], rows.at[at])
+    second = [copy for start in blocks[1:] for copy in block_of(start)]
+    third = halves(gate_b.at[mine], gate.at[1]) + halves(up_b.at[mine], up.at[1])
+    last = halves(down_a.at[mine], down.at[0]) + halves(down_b.at[mine], down.at[1])
+    start_all(first)
+    wait_all(first)
+    start_all(second + third)
+    step((0, 0))
+    wait_all(second)
+    start_all(last)
+    step(*((0, start) for start in blocks[1:]))
+    wait_all(third)
+    step(*((1, start) for start in blocks))
+    wait_all(last)
+
+    @pl.when(mine >= 0)
+    def _():
+        stores = []
+        for start in range(0, depth, WIDE):
+            cols = slice(start, start + WIDE)
+            both = jnp.concatenate([down[0, :, cols], down[1, :, cols]], axis=0)
+            out[:, cols] = jnp.dot(hidden[...], both, preferred_element_type=jnp.float32).astype(out.dtype)
+            at = pl.ds(start, WIDE)
+            stores.append(pltpu.make_async_copy(out.at[:, at], out_hbm.at[:, at], out_sems.at[start // WIDE]))
+            stores[-1].start()
+        wait_all(stores)
 
 
 def run_expert(core, rows, gate_a, up_a, down_a, gate_b, up_b, down_b):
     count, depth = rows.shape
     share = gate_a.shape[2]
-    moves = 3 * (depth // PIECE) + 2 * (2 * share // BLOCK - 1) + 2 * (depth // WIDE)
-    hbm = pl.BlockSpec(memory_space=pl.ANY)
+    hbm = pl.BlockSpec(memory_space=pltpu.HBM)
     return pl.pallas_call(
         expert_kernel,
-        out_shape=jax.ShapeDtypeStruct((count, depth), jnp.bfloat16),
+        out_shape=pltpu.HBM((count, depth), jnp.bfloat16),
         in_specs=[pl.BlockSpec(memory_space=pltpu.SMEM)] + [hbm] * 7,
         out_specs=hbm,
         scratch_shapes=[
@@ -200,7 +191,7 @@
             pltpu.VMEM((2, share, depth), jnp.bfloat16),
             pltpu.VMEM((count, 2 * share), jnp.bfloat16),
             pltpu.VMEM((count, depth), jnp.bfloat16),
-            pltpu.SemaphoreType.DMA((moves,)),
+            pltpu.SemaphoreType.DMA((4 + 2 * (share // BLOCK) + 8,)),
             pltpu.SemaphoreType.DMA((depth // WIDE,)),
         ],
         compiler_params=pltpu.CompilerParams(vmem_limit_bytes=48 * MIB),
@@ -280,6 +271,44 @@
         ),
         name="norm",
     )(terms, residual, gain.reshape(1, -1))
+
+
+def place_kernel(placing_ref, own_ref, other_ref, out_hbm, out, sems):
+    count = placing_ref.shape[0]
+    step = count // 4
+    rows = jnp.concatenate([own_ref[...], other_ref[...]], axis=0)
+    stores = []
+    for start in range(0, count, step):
+        value = jnp.dot(placing_ref[start : start + step, :], rows, preferred_element_type=jnp.float32)
+        out[start : start + step, :] = value.astype(out.dtype)
+        for copy in range(2):
+            stores.append(
+                pltpu.make_async_copy(
+                    out.at[pl.ds(start, step)],
+                    out_hbm.at[pl.ds(copy * count + start, step)],
+                    sems.at[len(stores)],
+                )
+            )
+            stores[-1].start()
+    for store in stores:
+        store.wait()
+
+
+def run_place(placing, own, other):
+    vmem = pl.BlockSpec(memory_space=pltpu.VMEM)
+    count, depth = placing.shape[0], own.shape[1]
+    return pl.pallas_call(
+        place_kernel,
+        out_shape=pltpu.HBM((2 * count, depth), jnp.bfloat16),
+        in_specs=[vmem] * 3,
+        out_specs=pl.BlockSpec(memory_space=pltpu.HBM),
+        scratch_shapes=[pltpu.VMEM((count, depth), jnp.bfloat16), pltpu.SemaphoreType.DMA((8,))],
+        compiler_params=pltpu.CompilerParams(vmem_limit_bytes=16 * MIB),
+        cost_estimate=pl.CostEstimate(
+            flops=2 * placing.size * depth, bytes_accessed=4 * count * depth, transcendentals=0
+        ),
+        name="place",
+    )(placing, own, other)
 
 
 def swap(value):
@@ -328,7 +357,6 @@
         w_out.reshape(parts, 2, half, width), core, axis=1, keepdims=False
     )
     mine = lax.all_to_all(mine, SPLIT, split_axis=0, concat_axis=0, tiled=True)
-    other = swap(mine)
 
     gate_b, up_b, down_b = swap(w_gate), swap(w_up), swap(w_down)
 
@@ -343,24 +371,23 @@
     chosen = slots[:, :, None] == jnp.arange(slot_total, dtype=jnp.int32)[None, None, :]
     placing = jnp.any(chosen, 1)
     mixing = jnp.sum(jnp.where(chosen, both_gates[:, :, None], 0.0), 1)
-    placing = jnp.concatenate([placing, placing], 1).astype(jnp.bfloat16)
+    placing = placing.astype(jnp.bfloat16).T
     mixing = jnp.concatenate([mixing, mixing], 1)
     mixing_high = mixing.astype(jnp.bfloat16)
     mixing_low = (mixing - mixing_high.astype(jnp.float32)).astype(jnp.bfloat16)
     mixing = jnp.concatenate([mixing_high, mixing_low], 0)
 
     sent = run_attend(queries, kv_cache, kv_new, lengths, parts, groups)
+    sent, mine = lax.optimization_barrier((sent, mine))
     gathered = lax.all_to_all(sent, EP, split_axis=0, concat_axis=0, tiled=True)
+    other = swap(mine)
     columns = run_project(core_index, gathered.reshape(ep_size * row_count, depth), mine, other)
     terms = lax.all_to_all(
         columns.reshape(ep_size, row_count, parts * width), EP, split_axis=0, concat_axis=0, tiled=True
     )
     attn_out, normed = run_norm(terms, residual, norm_gain, parts)
 
-    rows = jnp.concatenate([normed, swap(normed)], 0)
-    outgoing = lax.dot_general(
-        placing, rows, (((0,), (0,)), ((), ())), preferred_element_type=jnp.float32
-    ).astype(jnp.bfloat16)
+    outgoing = run_place(placing, normed, swap(normed))
     arrived = lax.all_to_all(
         outgoing.reshape(chips, 2 * SLOTS, -1), CHIPS, split_axis=0, concat_axis=0, tiled=True
     )
@@ -381,7 +408,7 @@
         mixing, returned.reshape(chips * 2 * SLOTS, -1), preferred_element_type=jnp.float32
     )
     mixed = mixed[: 2 * row_count] + mixed[2 * row_count :]
-    moe_out = mixed[:row_count] + swap(mixed[row_count:])
+    moe_out = mixed[:row_count] + swap(mixed[row_count:].astype(jnp.bfloat16)).astype(jnp.float32)
     return (attn_out, moe_out.astype(jnp.bfloat16))
 
 

time: 249 us -> 226 us (0.908)
  blocking collectives: 21.2 us -> 0 us
  starting transfers between devices: 43.5 us -> 49.4 us
  Pallas kernels: 37.1 us -> 32.3 us
  matrix products: 6.34 us -> 3.03 us
  waiting for transfers between devices: 129 us -> 132 us
  local copies, waits for them, and re-layouts: 5.86 us -> 3.25 us
    all_to_all x1 -> x0, blocking collectives: 21.2 us -> none  [on_device(): mine = lax.all_to_all(mine, SPLIT, split_axis=0, concat_axis=0, tiled=True)]
    all_to_all x0 -> x1, starting transfers between devices: none -> 6.88 us  [on_device(): mine = lax.all_to_all(mine, SPLIT, split_axis=0, concat_axis=0, tiled=True)]
    pallas_call x1 -> x2, Pallas kernels: 22 us -> 17.8 us  [the longest x1 15.5 us: run_expert(): pl.pallas_call(expert_kernel, out_shape=pltpu.HBM((count, depth), jnp.bfl...]
    unnamed x23 -> x19, local copies, waits for them, and re-layouts: 5.37 us -> 1.67 us
    all_to_all x0 -> x1, waiting for transfers between devices: none -> 3.45 us  [on_device(): mine = lax.all_to_all(mine, SPLIT, split_axis=0, concat_axis=0, tiled=True)]
    dot_general x1 -> x0, matrix products: 3.31 us -> none  [on_device(): lax.dot_general(placing, rows, (((0,), (0,)), ((), ())), preferred_elemen...]
  transfers between devices with their start and end apart: 12 -> 13, of which waited for: 7 -> 8; matrix products, arithmetic and copies ran while one was open for 2% -> 1% of each run, Pallas kernels for 6% -> 8%
where the time goes in v3:
time: 226 us; the launch traced here: 223 us
  waiting for transfers between devices  132 us (58%)
  starting transfers between devices  49.4 us (22%)
  Pallas kernels  32.3 us (14%)
  local copies, waits for them, and re-layouts  3.25 us (1%)
  matrix products  3.03 us (1%)
    all_to_all x1, waiting for transfers between devices, on_device(): lax.all_to_all(outgoing.reshape(chips, 2 * SLOTS, -1), CHIPS, split_axis=...  53.2 us
    all_to_all x1, waiting for transfers between devices, on_device(): lax.all_to_all(partial_value.reshape(chips, 2 * SLOTS, -1), CHIPS, split_...  45 us
    pallas_call x1, Pallas kernels, run_expert(): pl.pallas_call(expert_kernel, out_shape=pltpu.HBM((count, depth), jnp.bfl...  15.5 us
    all_to_all x1, waiting for transfers between devices, on_device(): gathered = lax.all_to_all(sent, EP, split_axis=0, concat_axis=0, tiled=True)  14.2 us
    all_to_all x1, waiting for transfers between devices, on_device(): lax.all_to_all(columns.reshape(ep_size, row_count, parts * width), EP, sp...  13.7 us
    all_to_all x1, starting transfers between devices, on_device(): lax.all_to_all(partial_value.reshape(chips, 2 * SLOTS, -1), CHIPS, split_...  12.2 us
    pallas_call x1, Pallas kernels, run_attend(): pl.pallas_call(functools.partial(attend_kernel, parts=parts, copies=copie...  11.4 us
    ppermute x8, starting transfers between devices, swap(): return lax.ppermute(value, 'core', SWAP)  11.1 us
  transfers between devices with their start and end apart: 13, of which 8 were waited for; matrix products, arithmetic and copies ran while one was open for 1% of the time, Pallas kernels for 8%

profile of v3, /device:TPU:1, one launch (start us, length us, event | category | flops | bytes accessed | tf_op | source)
XLA Modules:
  0.0 223.0 jit_solution(11645697790147468111)
XLA Ops:
  0.6 0.0 copy-start
  0.7 1.5 copy-done
  2.2 1.0 dynamic-slice_bitcast_fusion
  3.3 6.9 %all-to-all-start = ((bf16[8,512,128]{2,1,0:T(8,128)(2,1)}), bf16[8,512,128]{2,1,0:T(8,128)(2,1)S(1)}, u32[]{:S(2)}, u32[]{:S(2)}) async-start(bf16[8,512,128]{2,1,0:T(8,128)(2,1)} %dynamic-slice_bitcast_fusion), calls=%async_computation | async-start | bytes 2097152 | tf_op jit(solution)/shard_map/all_to_all | solution.py:359
  10.2 11.4 %attend.1 = bf16[32,16,1024]{2,1,0:T(8,128)(2,1)} custom-call(s32[16]{0:T(128)S(1)} %copy-done.6, bf16[16,8192]{1,0:T(8,128)(2,1)S(1)} %copy-done.2, bf16[16,2,128,512]{3,2,1,0:T(8,128)(2,1)} %cache_hbm.1, bf16[16,2,512]{2,1,0:T(2,128)(2,1)S(1)} %copy-done.4), custom_call_target="tpu_custom_call" | custom-call | flops 67108864 | bytes 5505024 | tf_op jit(solution)/shard_map/attend/pallas_call | solution.py:85
  21.6 3.4 %all-to-all-done.mine_ref = bf16[8,512,128]{2,1,0:T(8,128)(2,1)S(1)} async-done(((bf16[8,512,128]{2,1,0:T(8,128)(2,1)}), bf16[8,512,128]{2,1,0:T(8,128)(2,1)S(1)}, u32[]{:S(2)}, u32[]{:S(2)}) %all-to-all-start) | async-done | bytes 1048608 | tf_op jit(solution)/shard_map/all_to_all | solution.py:359
  25.1 0.8 collective-permute-start
  25.9 6.5 %all-to-all-start.1 = ((bf16[32,16,1024]{2,1,0:T(8,128)(2,1)}), bf16[32,16,1024]{2,1,0:T(8,128)(2,1)S(1)}, u32[]{:S(2)}, u32[]{:S(2)}) async-start(bf16[32,16,1024]{2,1,0:T(8,128)(2,1)} %attend.1), calls=%async_computation.1 | async-start | bytes 2097152 | tf_op jit(solution)/shard_map/all_to_all | solution.py:382
  32.4 0.4 collective-permute-start.4
  32.7 0.2 collective-permute-start.5
  33.0 0.3 collective-permute-start.6
  33.2 0.1 copy.51
  33.3 0.2 collective-permute-start.1
  33.5 0.1 eq.60
  33.6 14.2 %all-to-all-done.1 = bf16[32,16,1024]{2,1,0:T(8,128)(2,1)S(1)} async-done(((bf16[32,16,1024]{2,1,0:T(8,128)(2,1)}), bf16[32,16,1024]{2,1,0:T(8,128)(2,1)S(1)}, u32[]{:S(2)}, u32[]{:S(2)}) %all-to-all-start.1) | async-done | bytes 1048608 | tf_op jit(solution)/shard_map/all_to_all | solution.py:382
  47.8 2.2 %project.1 = bf16[512,1024]{1,0:T(8,128)(2,1)} custom-call(s32[1]{0:T(128)} %bitcast.core_ref, bf16[512,1024]{1,0:T(8,128)(2,1)S(1)} %bitcast.17, bf16[8,512,128]{2,1,0:T(8,128)(2,1)S(1)} %all-to-all-done.mine_ref, bf16[8,512,128]{2,1,0:T(8,128)(2,1)S(1)} %collective-permute-done.other_ref), custom_call_target="tpu_custom_call" | custom-call | flops 1073741824 | bytes 4194304 | tf_op jit(solution)/shard_map/project/pallas_call | solution.py:225
  50.1 5.6 %all-to-all-start.2 = ((bf16[32,16,1024]{2,1,0:T(8,128)(2,1)}), bf16[32,16,1024]{2,1,0:T(8,128)(2,1)S(1)}, u32[]{:S(2)}, u32[]{:S(2)}) async-start(bf16[32,16,1024]{2,1,0:T(8,128)(2,1)} %bitcast.4), calls=%async_computation.2 | async-start | bytes 2097152 | tf_op jit(solution)/shard_map/all_to_all | solution.py:385
  55.7 0.1 fusion.11
  55.8 0.2 reduce_window_sum.17
  56.0 0.2 select_reduce_fusion.2
  56.2 0.1 reduce_sum.41
  56.3 0.1 eq.65
  56.4 0.1 fusion.10
  56.5 0.2 reduce_window_sum.18
  56.6 0.2 select_reduce_fusion.1
  56.8 0.1 reduce_sum.43
  56.9 13.7 %all-to-all-done.2.terms_ref = bf16[32,16,1024]{2,1,0:T(8,128)(2,1)S(1)} async-done(((bf16[32,16,1024]{2,1,0:T(8,128)(2,1)}), bf16[32,16,1024]{2,1,0:T(8,128)(2,1)S(1)}, u32[]{:S(2)}, u32[]{:S(2)}) %all-to-all-start.2) | async-done | bytes 1048608 | tf_op jit(solution)/shard_map/all_to_all | solution.py:385
  70.6 0.8 norm.1
  71.5 2.5 %collective-permute-start.3 = (bf16[16,4096]{1,0:T(8,128)(2,1)S(1)}, bf16[16,4096]{1,0:T(8,128)(2,1)S(1)}, u32[]{:S(2)}, u32[]{:S(2)}) collective-permute-start(bf16[16,4096]{1,0:T(8,128)(2,1)S(1)} %get-tuple-element.9.own_ref), channel_id=1, source_target_pairs={{0,32},{32,0},{1,33},{33,1},{2,34},{34,2},{3,35},{35,3},{4,36},{36... | collective-permute-start | bytes 393224 | tf_op jit(solution)/shard_map/ppermute | solution.py:315
  74.0 0.2 fusion.3
  74.2 0.1 copy.58
  74.3 0.7 collective-permute-done.3.other_ref
  75.0 2.3 %place.1 = bf16[512,4096]{1,0:T(8,128)(2,1)} custom-call(bf16[256,32]{1,0:T(8,128)(2,1)S(1)} %bitcast.18, bf16[16,4096]{1,0:T(8,128)(2,1)S(1)} %get-tuple-element.9.own_ref, bf16[16,4096]{1,0:T(8,128)(2,1)S(1)} %collective-permute-done.3.other_ref), custom_call_target="tpu_custom_call" | custom-call | flops 67108864 | bytes 4194304 | tf_op jit(solution)/shard_map/place/pallas_call | solution.py:300
  77.3 7.1 %all-to-all-start.3 = ((bf16[64,8,4096]{2,1,0:T(8,128)(2,1)}), bf16[64,8,4096]{2,1,0:T(8,128)(2,1)}, u32[]{:S(2)}, u32[]{:S(2)}) async-start(bf16[64,8,4096]{2,1,0:T(8,128)(2,1)} %bitcast.21), calls=%async_computation.3 | async-start | bytes 8388608 | tf_op jit(solution)/shard_map/all_to_all | solution.py:391
  84.4 53.2 %all-to-all-done.3 = bf16[64,8,4096]{2,1,0:T(8,128)(2,1)} async-done(((bf16[64,8,4096]{2,1,0:T(8,128)(2,1)}), bf16[64,8,4096]{2,1,0:T(8,128)(2,1)}, u32[]{:S(2)}, u32[]{:S(2)}) %all-to-all-start.3) | async-done | bytes 4194336 | tf_op jit(solution)/shard_map/all_to_all | solution.py:391
  137.6 15.5 %expert.1 = bf16[512,4096]{1,0:T(8,128)(2,1)} custom-call(s32[1]{0:T(128)} %bitcast.core_ref, bf16[512,4096]{1,0:T(8,128)(2,1)} %bitcast.8.rows_hbm, bf16[2,4096,384]{2,1,0:T(8,128)(2,1)} %gate_a.1, bf16[2,4096,384]{2,1,0:T(8,128)(2,1)} %up_a.1, bf16[2,384,4096]{2,1,0:T(8,128)(2,1)} %down_a.1, bf16[2,4096,384]{2,1,0:T(8,128)(2,1)} %collective-permute-done.4.gate_b, ...), custom_call_target="tpu_custom_call" | custom-call | flops 9663676416 | bytes 27262976 | tf_op jit(solution)/shard_map/expert/pallas_call | solution.py:182
  153.1 12.2 %all-to-all-start.4 = ((bf16[64,8,4096]{2,1,0:T(8,128)(2,1)}), bf16[64,8,4096]{2,1,0:T(8,128)(2,1)}, u32[]{:S(2)}, u32[]{:S(2)}) async-start(bf16[64,8,4096]{2,1,0:T(8,128)(2,1)} %bitcast.20), calls=%async_computation.4 | async-start | bytes 8388608 | tf_op jit(solution)/shard_map/all_to_all | solution.py:404
  165.4 2.2 collective-permute-start.2
  167.5 0.8 collective-permute-done.2
  168.3 0.1 pad_maximum_fusion.1
  168.4 0.1 copy.57
  168.5 0.2 select_reduce_fusion
  168.7 45.0 %all-to-all-done.4 = bf16[64,8,4096]{2,1,0:T(8,128)(2,1)} async-done(((bf16[64,8,4096]{2,1,0:T(8,128)(2,1)}), bf16[64,8,4096]{2,1,0:T(8,128)(2,1)}, u32[]{:S(2)}, u32[]{:S(2)}) %all-to-all-start.4) | async-done | bytes 4194336 | tf_op jit(solution)/shard_map/all_to_all | solution.py:404
  213.7 3.0 %fusion = f32[64,4096]{1,0:T(8,128)S(1)} fusion(bf16[64,8,4096]{2,1,0:T(8,128)(2,1)} %all-to-all-done.4, bf16[32,512]{1,0:T(8,128)(2,1)S(1)} %fusion.6, bf16[32,512]{1,0:T(8,128)(2,1)S(1)} %fusion.5), kind=kOutput, calls=%fused_computation | convolution fusion | flops 268566528 | bytes 5308416 | tf_op jit(solution)/shard_map/dot_general | solution.py:407
  216.7 0.1 slice_add_fusion
  216.8 4.5 %collective-permute-start.7 = (bf16[16,4096]{1,0:T(8,128)(2,1)S(1)}, bf16[16,4096]{1,0:T(8,128)(2,1)S(1)}, u32[]{:S(2)}, u32[]{:S(2)}) collective-permute-start(bf16[16,4096]{1,0:T(8,128)(2,1)S(1)} %slice.27), channel_id=1, source_target_pairs={{0,32},{32,0},{1,33},{33,1},{2,34},{34,2},{3,35},{35,3},{4,36},{36... | collective-permute-start | bytes 393224 | tf_op jit(solution)/shard_map/ppermute | solution.py:315
  221.3 1.0 collective-permute-done.7
  222.3 0.7 fusion.2
  (30 shorter events, 0.2 us)
Async XLA Ops:
  0.6 1.6 copy-start
  0.6 9.5 %copy-start.6 = (s32[16]{0:T(128)S(1)}, s32[16]{0:T(128)}, u32[]{:S(2)}) copy-start(s32[16]{0:T(128)} %lengths_ref.1) | copy-start | bytes 196
  0.7 9.5 %copy-start.2 = (bf16[16,8192]{1,0:T(8,128)(2,1)S(1)}, bf16[16,8192]{1,0:T(8,128)(2,1)}, u32[]{:S(2)}) copy-start(bf16[16,8192]{1,0:T(8,128)(2,1)} %queries_ref.1) | copy-start | bytes 786436
  0.7 9.5 %copy-start.4 = (bf16[16,2,512]{2,1,0:T(2,128)(2,1)S(1)}, bf16[16,2,512]{2,1,0:T(2,128)(2,1)}, u32[]{:S(2)}) copy-start(bf16[16,2,512]{2,1,0:T(2,128)(2,1)} %fresh_ref.1) | copy-start | bytes 98308
  3.3 21.8 %all-to-all-start = ((bf16[8,512,128]{2,1,0:T(8,128)(2,1)}), bf16[8,512,128]{2,1,0:T(8,128)(2,1)S(1)}, u32[]{:S(2)}, u32[]{:S(2)}) async-start(bf16[8,512,128]{2,1,0:T(8,128)(2,1)} %dynamic-slice_bitcast_fusion), calls=%async_computation | async-start | bytes 2097152 | tf_op jit(solution)/shard_map/all_to_all | solution.py:359
  10.2 23.1 %copy-start.8 = (s32[16,8]{0,1:T(8,128)S(1)}, s32[16,8]{0,1:T(8,128)}, u32[]{:S(2)}) copy-start(s32[16,8]{0,1:T(8,128)} %param.18) | copy-start | bytes 1540
  21.6 49.0 %copy-start.3 = (bf16[16,4096]{1,0:T(8,128)(2,1)S(1)}, bf16[16,4096]{1,0:T(8,128)(2,1)}, u32[]{:S(2)}) copy-start(bf16[16,4096]{1,0:T(8,128)(2,1)} %residual_ref.1) | copy-start | bytes 393220
  21.6 49.0 %copy-start.5 = (f32[4096]{0:T(1024)S(1)}, f32[4096]{0:T(1024)}, u32[]{:S(2)}) copy-start(f32[4096]{0:T(1024)} %param.17) | copy-start | bytes 49156
  25.1 22.8 %collective-permute-start = (bf16[8,512,128]{2,1,0:T(8,128)(2,1)S(1)}, bf16[8,512,128]{2,1,0:T(8,128)(2,1)S(1)}, u32[]{:S(2)}, u32[]{:S(2)}) collective-permute-start(bf16[8,512,128]{2,1,0:T(8,128)(2,1)S(1)} %all-to-all-done.mine_ref), channel_id=1, source_target_pairs={{0,32},{32,0},{1,33},{33,1},{2,34},{34,2},{3,35},{35,3},{4,36},{36... | collective-permute-start | bytes 3145736 | tf_op jit(solution)/shard_map/ppermute | solution.py:315
  25.9 21.9 %all-to-all-start.1 = ((bf16[32,16,1024]{2,1,0:T(8,128)(2,1)}), bf16[32,16,1024]{2,1,0:T(8,128)(2,1)S(1)}, u32[]{:S(2)}, u32[]{:S(2)}) async-start(bf16[32,16,1024]{2,1,0:T(8,128)(2,1)} %attend.1), calls=%async_computation.1 | async-start | bytes 2097152 | tf_op jit(solution)/shard_map/all_to_all | solution.py:382
  32.4 52.1 %collective-permute-start.4 = (bf16[2,4096,384]{2,1,0:T(8,128)(2,1)}, bf16[2,4096,384]{2,1,0:T(8,128)(2,1)}, u32[]{:S(2)}, u32[]{:S(2)}) collective-permute-start(bf16[2,4096,384]{2,1,0:T(8,128)(2,1)} %gate_a.1), channel_id=1, source_target_pairs={{0,32},{32,0},{1,33},{33,1},{2,34},{34,2},{3,35},{35,3},{4,36},{36... | collective-permute-start | bytes 18874376 | tf_op jit(solution)/shard_map/ppermute | solution.py:315
  32.7 51.7 %collective-permute-start.5 = (bf16[2,4096,384]{2,1,0:T(8,128)(2,1)}, bf16[2,4096,384]{2,1,0:T(8,128)(2,1)}, u32[]{:S(2)}, u32[]{:S(2)}) collective-permute-start(bf16[2,4096,384]{2,1,0:T(8,128)(2,1)} %up_a.1), channel_id=1, source_target_pairs={{0,32},{32,0},{1,33},{33,1},{2,34},{34,2},{3,35},{35,3},{4,36},{36... | collective-permute-start | bytes 18874376 | tf_op jit(solution)/shard_map/ppermute | solution.py:315
  33.0 51.5 %collective-permute-start.6 = (bf16[2,384,4096]{2,1,0:T(8,128)(2,1)}, bf16[2,384,4096]{2,1,0:T(8,128)(2,1)}, u32[]{:S(2)}, u32[]{:S(2)}) collective-permute-start(bf16[2,384,4096]{2,1,0:T(8,128)(2,1)} %down_a.1), channel_id=1, source_target_pairs={{0,32},{32,0},{1,33},{33,1},{2,34},{34,2},{3,35},{35,3},{4,36},{36... | collective-permute-start | bytes 18874376 | tf_op jit(solution)/shard_map/ppermute | solution.py:315
  33.3 23.0 %collective-permute-start.1 = (s32[16,8]{1,0:T(8,128)S(1)}, s32[16,8]{1,0:T(8,128)S(1)}, u32[]{:S(2)}, u32[]{:S(2)}) collective-permute-start(s32[16,8]{1,0:T(8,128)S(1)} %copy.51), channel_id=1, source_target_pairs={{0,32},{32,0},{1,33},{33,1},{2,34},{34,2},{3,35},{35,3},{4,36},{36... | collective-permute-start | bytes 1544 | tf_op jit(solution)/shard_map/ppermute | solution.py:315
  50.1 20.5 %all-to-all-start.2 = ((bf16[32,16,1024]{2,1,0:T(8,128)(2,1)}), bf16[32,16,1024]{2,1,0:T(8,128)(2,1)S(1)}, u32[]{:S(2)}, u32[]{:S(2)}) async-start(bf16[32,16,1024]{2,1,0:T(8,128)(2,1)} %bitcast.4), calls=%async_computation.2 | async-start | bytes 2097152 | tf_op jit(solution)/shard_map/all_to_all | solution.py:385
  71.5 3.5 %collective-permute-start.3 = (bf16[16,4096]{1,0:T(8,128)(2,1)S(1)}, bf16[16,4096]{1,0:T(8,128)(2,1)S(1)}, u32[]{:S(2)}, u32[]{:S(2)}) collective-permute-start(bf16[16,4096]{1,0:T(8,128)(2,1)S(1)} %get-tuple-element.9.own_ref), channel_id=1, source_target_pairs={{0,32},{32,0},{1,33},{33,1},{2,34},{34,2},{3,35},{35,3},{4,36},{36... | collective-permute-start | bytes 393224 | tf_op jit(solution)/shard_map/ppermute | solution.py:315
  77.3 60.4 %all-to-all-start.3 = ((bf16[64,8,4096]{2,1,0:T(8,128)(2,1)}), bf16[64,8,4096]{2,1,0:T(8,128)(2,1)}, u32[]{:S(2)}, u32[]{:S(2)}) async-start(bf16[64,8,4096]{2,1,0:T(8,128)(2,1)} %bitcast.21), calls=%async_computation.3 | async-start | bytes 8388608 | tf_op jit(solution)/shard_map/all_to_all | solution.py:391
  153.1 12.2 %copy-start.7 = (f32[16,8]{0,1:T(8,128)S(1)}, f32[16,8]{0,1:T(8,128)}, u32[]{:S(2)}) copy-start(f32[16,8]{0,1:T(8,128)} %param.19) | copy-start | bytes 1540
  153.1 60.6 %all-to-all-start.4 = ((bf16[64,8,4096]{2,1,0:T(8,128)(2,1)}), bf16[64,8,4096]{2,1,0:T(8,128)(2,1)}, u32[]{:S(2)}, u32[]{:S(2)}) async-start(bf16[64,8,4096]{2,1,0:T(8,128)(2,1)} %bitcast.20), calls=%async_computation.4 | async-start | bytes 8388608 | tf_op jit(solution)/shard_map/all_to_all | solution.py:404
  165.3 57.7 %copy-start.1 = (bf16[8192,128]{1,0:T(8,128)(2,1)S(1)}, bf16[8192,128]{1,0:T(8,128)(2,1)}, u32[]{:S(2)}) copy-start(bf16[8192,128]{1,0:T(8,128)(2,1)} %param.20) | copy-start | bytes 6291460
  165.4 3.0 %collective-permute-start.2 = (f32[16,8]{0,1:T(8,128)S(1)}, f32[16,8]{0,1:T(8,128)S(1)}, u32[]{:S(2)}, u32[]{:S(2)}) collective-permute-start(f32[16,8]{0,1:T(8,128)S(1)} %broadcast_divide_fusion), channel_id=1, source_target_pairs={{0,32},{32,0},{1,33},{33,1},{2,34},{34,2},{3,35},{35,3},{4,36},{36... | collective-permute-start | bytes 1544 | tf_op jit(solution)/shard_map/ppermute | solution.py:315
  216.8 5.5 %collective-permute-start.7 = (bf16[16,4096]{1,0:T(8,128)(2,1)S(1)}, bf16[16,4096]{1,0:T(8,128)(2,1)S(1)}, u32[]{:S(2)}, u32[]{:S(2)}) collective-permute-start(bf16[16,4096]{1,0:T(8,128)(2,1)S(1)} %slice.27), channel_id=1, source_target_pairs={{0,32},{32,0},{1,33},{33,1},{2,34},{34,2},{3,35},{35,3},{4,36},{36... | collective-permute-start | bytes 393224 | tf_op jit(solution)/shard_map/ppermute | solution.py:315

commit v4 on v3

v4 whole, which is shorter than its diff:
```python
import functools
import math

import jax
import jax.numpy as jnp
from jax import lax
from jax.experimental import pallas as pl
from jax.experimental.pallas import tpu as pltpu
from jax.sharding import Mesh, PartitionSpec as P

HEADS = 64
KVH = 4
HD = 128
TOP = 8
SLOTS = 4

DP = ("xh", "core")
EP = ("xl", "yh", "yl", "z")
PLANE = ("xh", "xl", "yh", "yl")
CHIPS = ("xh",) + EP
ALL = DP + EP
SWAP = ((0, 1), (1, 0))
MIB = 1 << 20
BLOCK = 128
WIDE = 1024


def attend_kernel(
    lengths_ref, queries_hbm, cache_hbm, fresh_hbm, out_ref, queries_ref, cache, fresh_ref, heads, sems, *, parts, copies
):
    rows = queries_ref.shape[0]
    batches = sems.shape[0] - 2
    batch = rows // batches
    span = cache.shape[2]
    others = [
        pltpu.make_async_copy(queries_hbm, queries_ref, sems.at[batches]),
        pltpu.make_async_copy(fresh_hbm, fresh_ref, sems.at[batches + 1]),
    ]
    for other in others:
        other.start()
    moves = []
    for number in range(batches):
        at = pl.ds(number * batch, batch)
        moves.append(pltpu.make_async_copy(cache_hbm.at[at], cache.at[at], sems.at[number]))
        moves[-1].start()
    groups = HEADS // KVH
    scaling = 1.0 / math.sqrt(HD)
    for other in others:
        other.wait()
    for head in range(HEADS):
        query = queries_ref[:, head * HD : (head + 1) * HD].astype(jnp.float32)
        heads[pl.ds(head, rows, stride=HEADS), :] = query
    position = lax.broadcasted_iota(jnp.int32, (HEADS, span), 1)
    for number, move in enumerate(moves):
        move.wait()
        those = range(number * batch, (number + 1) * batch)
        at = slice(number * batch * HEADS, (number + 1) * batch * HEADS)
        query = heads[at, :]
        rounded = query.astype(jnp.bfloat16)
        blocks = [
            (row, kv, slice(kv * HD, (kv + 1) * HD), slice(place * groups, (place + 1) * groups))
            for place, (row, kv) in enumerate((row, kv) for row in those for kv in range(KVH))
        ]
        scores = jnp.concatenate(
            [
                lax.dot_general(
                    rounded[own], cache[row, 0, :, cols], (((1,), (1,)), ((), ())), preferred_element_type=jnp.float32
                )
                for row, kv, cols, own in blocks
            ],
            axis=0,
        )
        keys = [
            jnp.broadcast_to(fresh_ref[row, 0:1, cols].astype(jnp.float32), (groups, HD)) for row, kv, cols, own in blocks
        ]
        fresh = jnp.sum(query * jnp.concatenate(keys, axis=0), axis=1, keepdims=True) * scaling
        live = jnp.concatenate([position < lengths_ref[row] for row in those], axis=0)
        scores = jnp.where(live, scores * scaling, -1e30)
        highest = jnp.maximum(jnp.max(scores, axis=1, keepdims=True), fresh)
        scores = jnp.exp(scores - highest)
        fresh = jnp.exp(fresh - highest)
        denominator = jnp.sum(scores, axis=1, keepdims=True) + fresh
        weights = (scores / denominator).astype(jnp.bfloat16)
        fresh = (fresh / denominator).astype(jnp.bfloat16).astype(jnp.float32)
        mixed = [
            jnp.dot(weights[own], cache[row, 1, :, cols], preferred_element_type=jnp.float32)
            + fresh[own] * fresh_ref[row, 1:2, cols].astype(jnp.float32)
            for row, kv, cols, own in blocks
        ]
        heads[at, :] = jnp.concatenate(mixed, axis=0)
    share = HEADS // parts
    for head in range(HEADS):
        value = heads[pl.ds(head, rows, stride=HEADS), :].astype(jnp.bfloat16)
        cols = slice(head % share * HD, (head % share + 1) * HD)
        outer, inner = divmod(head // share, 2)
        for copy in range(copies):
            out_ref[(outer * copies + copy) * 2 + inner, :, cols] = value

def run_attend(queries, kv_cache, kv_new, lengths, parts, copies):
    rows = queries.shape[0]
    hbm = pl.BlockSpec(memory_space=pltpu.HBM)
    operands = [pltpu.with_memory_space_constraint(value, pltpu.HBM) for value in (queries, kv_cache, kv_new)]
    return pl.pallas_call(
        functools.partial(attend_kernel, parts=parts, copies=copies),
        out_shape=pltpu.HBM((copies * parts, rows, HEADS * HD // parts), jnp.bfloat16),
        in_specs=[pl.BlockSpec(memory_space=pltpu.SMEM)] + [hbm] * 3,
        out_specs=pl.BlockSpec(memory_space=pltpu.VMEM),
        scratch_shapes=[
            pltpu.VMEM(queries.shape, jnp.bfloat16),
            pltpu.VMEM(kv_cache.shape, jnp.bfloat16),
            pltpu.VMEM(kv_new.shape, jnp.bfloat16),
            pltpu.VMEM((rows * HEADS, HD), jnp.float32),
            pltpu.SemaphoreType.DMA((6,)),
        ],
        compiler_params=pltpu.CompilerParams(vmem_limit_bytes=24 * MIB),
        cost_estimate=pl.CostEstimate(
            flops=4 * kv_cache.size // 2 * HEADS // KVH,
            bytes_accessed=2 * (kv_cache.size + 5 * queries.size),
            transcendentals=rows * HEADS * kv_cache.shape[2],
        ),
        name="attend",
    )(lengths, *operands)


def expert_kernel(
    core_ref, rows, gate_a, up_a, down_a, gate_b, up_b, down_b, out_hbm, gate, up, down, hidden, out, sems, out_sems
):
    mine = core_ref[0]
    depth = rows.shape[1]
    share = gate.shape[1]
    moves = []
    for source, target in ((gate_a, gate), (up_a, up), (down_a, down)):
        size = target.shape[0] // 2
        for half in range(2):
            at = pl.ds(half * size, size)
            moves.append(pltpu.make_async_copy(source.at[mine, at], target.at[at], sems.at[len(moves)]))
            moves[-1].start()

    def step(gate_of, up_of, base):
        @pl.when(mine >= 0)
        def _():
            for start in range(0, share, BLOCK):
                cols = slice(start, start + BLOCK)
                both = jnp.concatenate([gate_of(cols), up_of(cols)], axis=1)
                acts = jnp.dot(rows[...], both, preferred_element_type=jnp.float32)
                gate_act = acts[:, :BLOCK]
                value = gate_act / (1.0 + jnp.exp(-gate_act)) * acts[:, BLOCK:]
                hidden[:, base + start : base + start + BLOCK] = value.astype(jnp.bfloat16)

    step(lambda cols: gate_b[mine, :, cols], lambda cols: up_b[mine, :, cols], 0)
    for move in moves[:4]:
        move.wait()
    step(lambda cols: gate[:, cols], lambda cols: up[:, cols], share)
    for move in moves[4:]:
        move.wait()

    @pl.when(mine >= 0)
    def _():
        stores = []
        for start in range(0, depth, WIDE):
            cols = slice(start, start + WIDE)
            both = jnp.concatenate([down_b[mine, :, cols], down[:, cols]], axis=0)
            out[:, cols] = jnp.dot(hidden[...], both, preferred_element_type=jnp.float32).astype(out.dtype)
            at = pl.ds(start, WIDE)
            stores.append(pltpu.make_async_copy(out.at[:, at], out_hbm.at[:, at], out_sems.at[start // WIDE]))
            stores[-1].start()
        for store in stores:
            store.wait()


def run_expert(core, rows, gate_a, up_a, down_a, gate_b, up_b, down_b):
    count, depth = rows.shape
    share = gate_a.shape[2]
    hbm = pl.BlockSpec(memory_space=pl.ANY)
    vmem = pl.BlockSpec(memory_space=pltpu.VMEM)
    rows, gate_b, up_b, down_b = (
        pltpu.with_memory_space_constraint(value, pltpu.VMEM) for value in (rows, gate_b, up_b, down_b)
    )
    return pl.pallas_call(
        expert_kernel,
        out_shape=pltpu.HBM((count, depth), jnp.bfloat16),
        in_specs=[pl.BlockSpec(memory_space=pltpu.SMEM), vmem] + [hbm] * 3 + [vmem] * 3,
        out_specs=hbm,
        scratch_shapes=[
            pltpu.VMEM((depth, share), jnp.bfloat16),
            pltpu.VMEM((depth, share), jnp.bfloat16),
            pltpu.VMEM((share, depth), jnp.bfloat16),
            pltpu.VMEM((count, 2 * share), jnp.bfloat16),
            pltpu.VMEM((count, depth), jnp.bfloat16),
            pltpu.SemaphoreType.DMA((6,)),
            pltpu.SemaphoreType.DMA((depth // WIDE,)),
        ],
        compiler_params=pltpu.CompilerParams(vmem_limit_bytes=24 * MIB),
        cost_estimate=pl.CostEstimate(
            flops=2 * count * depth * share * 6,
            bytes_accessed=2 * (2 * count * depth + 6 * depth * share),
            transcendentals=count * share * 2,
        ),
        name="expert",
    )(core, rows, gate_a, up_a, down_a, gate_b, up_b, down_b)


def project_kernel(place_ref, rows_ref, *refs):
    *weights, out_ref = refs
    half, width = weights[0].shape[1:]
    ring = len(weights) // 2
    pair, turn, core = place_ref[0], place_ref[1], place_ref[2]
    near = rows_ref[:, pl.ds(pl.multiple_of(core * half, half), half)]
    far = rows_ref[:, pl.ds(pl.multiple_of((1 - core) * half, half), half)]
    for step in range(ring):
        total = None
        for rows, weight in ((near, weights[step]), (far, weights[ring + step])):
            both = jnp.concatenate([weight[0], weight[1]], axis=1)
            term = jnp.dot(rows, both, preferred_element_type=jnp.float32)
            total = term if total is None else total + term
        total = total.astype(out_ref.dtype)
        for which in range(2):
            owner = (pair + which) % 2 * ring + (turn + ring - step) % ring
            cols = pl.ds(pl.multiple_of(owner * width, width), width)
            out_ref[:, cols] = total[:, which * width : (which + 1) * width]


def run_project(place, rows, weights):
    count, depth = rows.shape
    width = len(weights) * weights[0].shape[2]
    vmem = pl.BlockSpec(memory_space=pltpu.VMEM)
    return pl.pallas_call(
        project_kernel,
        out_shape=pltpu.HBM((count, width), jnp.bfloat16),
        in_specs=[pl.BlockSpec(memory_space=pltpu.SMEM)] + [vmem] * (1 + len(weights)),
        out_specs=vmem,
        compiler_params=pltpu.CompilerParams(vmem_limit_bytes=16 * MIB),
        cost_estimate=pl.CostEstimate(
            flops=2 * count * depth * width,
            bytes_accessed=2 * (count * depth + count * width + depth * width),
            transcendentals=0,
        ),
        name="project",
    )(place, rows, *weights)


def norm_kernel(terms_ref, residual_ref, gain_ref, out_ref, normed_ref, *, parts):
    width = terms_ref.shape[2]
    streams = []
    squares = None
    groups = terms_ref.shape[0] // parts
    outer = parts // 2
    for group in range(groups):
        cols = slice(group * width, (group + 1) * width)
        total = None
        for part in range(outer):
            for inner in range(2):
                term = terms_ref[(part * groups + group) * 2 + inner].astype(jnp.float32)
                total = term if total is None else total + term
        total = total.astype(jnp.bfloat16)
        out_ref[:, cols] = total
        stream = residual_ref[:, cols].astype(jnp.float32) + total.astype(jnp.float32)
        square = jnp.sum(stream * stream, axis=1, keepdims=True)
        squares = square if squares is None else squares + square
        streams.append(stream)
    scale = lax.rsqrt(squares / out_ref.shape[1] + 1e-06)
    for group, stream in enumerate(streams):
        cols = slice(group * width, (group + 1) * width)
        normed_ref[:, cols] = (stream * scale * gain_ref[:, cols]).astype(jnp.bfloat16)


def run_norm(terms, residual, gain, parts):
    vmem = pl.BlockSpec(memory_space=pltpu.VMEM)
    return pl.pallas_call(
        functools.partial(norm_kernel, parts=parts),
        out_shape=[jax.ShapeDtypeStruct(residual.shape, jnp.bfloat16)] * 2,
        in_specs=[vmem] * 3,
        out_specs=[vmem] * 2,
        compiler_params=pltpu.CompilerParams(vmem_limit_bytes=16 * MIB),
        cost_estimate=pl.CostEstimate(
            flops=2 * terms.size, bytes_accessed=2 * terms.size, transcendentals=0
        ),
        name="norm",
    )(terms, residual, gain.reshape(1, -1))


def place_kernel(placing_ref, own_ref, other_ref, out_hbm, out, sems):
    count = placing_ref.shape[0]
    step = count // 4
    rows = jnp.concatenate([own_ref[...], other_ref[...]], axis=0)
    stores = []
    for start in range(0, count, step):
        value = jnp.dot(placing_ref[start : start + step, :], rows, preferred_element_type=jnp.float32)
        out[start : start + step, :] = value.astype(out.dtype)
        for copy in range(2):
            stores.append(
                pltpu.make_async_copy(
                    out.at[pl.ds(start, step)],
                    out_hbm.at[pl.ds(copy * count + start, step)],
                    sems.at[len(stores)],
                )
            )
            stores[-1].start()
    for store in stores:
        store.wait()


def run_place(placing, own, other):
    vmem = pl.BlockSpec(memory_space=pltpu.VMEM)
    count, depth = placing.shape[0], own.shape[1]
    return pl.pallas_call(
        place_kernel,
        out_shape=pltpu.HBM((2 * count, depth), jnp.bfloat16),
        in_specs=[vmem] * 3,
        out_specs=pl.BlockSpec(memory_space=pltpu.HBM),
        scratch_shapes=[pltpu.VMEM((count, depth), jnp.bfloat16), pltpu.SemaphoreType.DMA((8,))],
        compiler_params=pltpu.CompilerParams(vmem_limit_bytes=16 * MIB),
        cost_estimate=pl.CostEstimate(
            flops=2 * placing.size * depth, bytes_accessed=4 * count * depth, transcendentals=0
        ),
        name="place",
    )(placing, own, other)


def swap(value):
    return lax.ppermute(value, "core", SWAP)


def places(expert_ids, core, expert_total):
    row_count = expert_ids.shape[0]
    pair_ids = expert_ids.reshape(-1)
    member = (pair_ids[:, None] == jnp.arange(expert_total, dtype=jnp.int32)[None, :]).astype(
        jnp.int32
    )
    ranking = jnp.sum((jnp.cumsum(member, 0) - 1) * member, 1)
    here = (pair_ids % 2) == core
    slot = (pair_ids // 2) * (2 * SLOTS) + ranking
    slot = jnp.where(here, slot, -1)
    return slot.reshape(row_count, TOP)


def on_device(
    queries,
    kv_cache,
    kv_new,
    lengths,
    residual,
    norm_gain,
    expert_ids,
    route_probs,
    w_out,
    w_gate,
    w_up,
    w_down,
):
    row_count = queries.shape[0]
    core = lax.axis_index("core")
    core_index = core.astype(jnp.int32).reshape(1)
    ep_size = lax.axis_size(EP)
    plane = lax.axis_size(PLANE)
    chips = lax.axis_size(CHIPS)
    ring = lax.axis_size("z")
    parts = 2 * lax.axis_size("xh")
    depth = w_out.shape[0] // parts
    half = depth // 2

    pair = lax.axis_index("yl")
    quarter = lax.axis_index("xh") * 2
    kept = lax.dynamic_slice_in_dim(w_out, (quarter + pair) * depth + core * half, half, axis=0)
    given = lax.dynamic_slice_in_dim(w_out, (quarter + 1 - pair) * depth + core * half, half, axis=0)
    taken = lax.ppermute(given, "yl", SWAP)
    sent = run_attend(queries, kv_cache, kv_new, lengths, parts, plane // parts)
    sent, taken, expert_ids, route_probs = lax.optimization_barrier((sent, taken, expert_ids, route_probs))
    weights = [jnp.stack([kept, taken])]
    for step in range(1, ring):
        turn = [(place, (place + step) % ring) for place in range(ring)]
        weights.append(lax.ppermute(weights[0], "z", turn))
    weights += [swap(value) for value in weights]
    place = jnp.stack([pair, lax.axis_index("z"), core]).astype(jnp.int32)

    expert_total = w_gate.shape[0] * ep_size
    slot_total = 2 * SLOTS * ep_size
    gates = route_probs / jnp.sum(route_probs, -1, keepdims=True)
    own_slots = places(expert_ids, core, expert_total)
    other_slots = places(swap(expert_ids), core, expert_total)
    other_slots = jnp.where(other_slots >= 0, other_slots + SLOTS, -1)
    slots = jnp.concatenate([own_slots, other_slots], 0)
    both_gates = jnp.concatenate([gates, swap(gates)], 0)
    chosen = slots[:, :, None] == jnp.arange(slot_total, dtype=jnp.int32)[None, None, :]
    placing = jnp.any(chosen, 1)
    mixing = jnp.sum(jnp.where(chosen, both_gates[:, :, None], 0.0), 1)
    placing = placing.astype(jnp.bfloat16).T
    mixing = jnp.concatenate([mixing, mixing], 1)
    mixing_high = mixing.astype(jnp.bfloat16)
    mixing_low = (mixing - mixing_high.astype(jnp.float32)).astype(jnp.bfloat16)
    mixing = jnp.concatenate([mixing_high, mixing_low], 0)

    gathered = lax.all_to_all(sent, PLANE, split_axis=0, concat_axis=0, tiled=True)
    columns = run_project(place, gathered.reshape(plane * row_count, depth), weights)
    columns, placing, mixing = lax.optimization_barrier((columns, placing, mixing))
    terms = lax.all_to_all(
        columns.reshape(plane, row_count, -1), PLANE, split_axis=0, concat_axis=0, tiled=True
    )
    attn_out, normed = run_norm(terms, residual, norm_gain, parts)

    other_normed = swap(normed)
    other_normed, w_gate, w_up, w_down = lax.optimization_barrier((other_normed, w_gate, w_up, w_down))
    gate_b, up_b, down_b = swap(w_gate), swap(w_up), swap(w_down)
    outgoing = run_place(placing, normed, other_normed)
    arrived = lax.all_to_all(
        outgoing.reshape(chips, 2 * SLOTS, -1), CHIPS, split_axis=0, concat_axis=0, tiled=True
    )
    partial_value = run_expert(
        core_index,
        arrived.reshape(chips * 2 * SLOTS, -1),
        w_gate,
        w_up,
        w_down,
        gate_b,
        up_b,
        down_b,
    )
    returned = lax.all_to_all(
        partial_value.reshape(chips, 2 * SLOTS, -1), CHIPS, split_axis=0, concat_axis=0, tiled=True
    )
    mixed = jnp.dot(
        mixing, returned.reshape(chips * 2 * SLOTS, -1), preferred_element_type=jnp.float32
    )
    mixed = mixed[: 2 * row_count] + mixed[2 * row_count :]
    moe_out = mixed[:row_count] + swap(mixed[row_count:].astype(jnp.bfloat16)).astype(jnp.float32)
    return (attn_out, moe_out.astype(jnp.bfloat16))


def solution(mesh):
    fine = Mesh(mesh.devices.reshape(2, 2, 2, 2, 2, 4), ALL)
    return jax.shard_map(
        on_device,
        mesh=fine,
        in_specs=(
            P(ALL, None),
            P(ALL, None, None, None),
            P(ALL, None, None),
            P(ALL),
            P(ALL, None),
            P(),
            P(ALL, None),
            P(ALL, None),
            P(None, EP),
            P(EP, None, DP),
            P(EP, None, DP),
            P(EP, DP, None),
        ),
        out_specs=(P(ALL, None), P(ALL, None)),
        check_vma=False,
    )
```

time: 226 us -> 204 us (0.903)
  blocking collectives: 0 us -> 129 us
  waiting for transfers between devices: 132 us -> 17.8 us
  starting transfers between devices: 49.4 us -> 25.1 us
  Pallas kernels: 32.3 us -> 24.7 us
    all_to_all x5 -> x1, waiting for transfers between devices: 130 us -> 0.01 us  [on_device(): lax.all_to_all(sent, PLANE, split_axis=0, concat_axis=0, tiled=True)]
    all_to_all x0 -> x3, blocking collectives: none -> 129 us  [the longest x1 56.4 us: on_device(): lax.all_to_all(partial_value.reshape(chips, 2 * SLOTS, -1), CHIPS, split_...]
    all_to_all x5 -> x1, starting transfers between devices: 38.2 us -> 6.54 us  [on_device(): lax.all_to_all(sent, PLANE, split_axis=0, concat_axis=0, tiled=True)]
    ppermute x0 -> x4, waiting for transfers between devices: none -> 14.5 us  [the longest x3 14.5 us: on_device(): weights.append(lax.ppermute(weights[0], 'z', turn))]
    ppermute x0 -> x4, starting transfers between devices: none -> 6.73 us  [the longest x3 4.52 us: on_device(): weights.append(lax.ppermute(weights[0], 'z', turn))]
    pallas_call x1, Pallas kernels: 11.4 us -> 5.94 us  [run_attend(): pl.pallas_call(functools.partial(attend_kernel, parts=parts, copies=copie...]
    pallas_call x1, Pallas kernels: 15.5 us -> 11.8 us  [run_expert(): pl.pallas_call(expert_kernel, out_shape=pltpu.HBM((count, depth), jnp.bfl...]
    ppermute x8 -> x11, starting transfers between devices: 11.1 us -> 11.8 us  [swap(): return lax.ppermute(value, 'core', SWAP)]
  transfers between devices with their start and end apart: 13 -> 16, of which waited for: 8 -> 5; matrix products, arithmetic and copies ran while one was open for 1% -> 1% of each run, Pallas kernels for 8% -> 4%
where the time goes in v4:
time: 204 us; the launch traced here: 203 us
  blocking collectives  129 us (63%)
  starting transfers between devices  25.1 us (12%)
  Pallas kernels  24.7 us (12%)
  waiting for transfers between devices  17.8 us (9%)
  local copies, waits for them, and re-layouts  2.38 us (1%)
  other arithmetic  2.24 us (1%)
    all_to_all x1, blocking collectives, on_device(): lax.all_to_all(partial_value.reshape(chips, 2 * SLOTS, -1), CHIPS, split_...  56.4 us
    all_to_all x1, blocking collectives, on_device(): lax.all_to_all(outgoing.reshape(chips, 2 * SLOTS, -1), CHIPS, split_axis=...  55.8 us
    all_to_all x1, blocking collectives, on_device(): lax.all_to_all(columns.reshape(plane, row_count, -1), PLANE, split_axis=0...  16.9 us
    ppermute x3, waiting for transfers between devices, on_device(): weights.append(lax.ppermute(weights[0], 'z', turn))  14.5 us
    pallas_call x1, Pallas kernels, run_expert(): pl.pallas_call(expert_kernel, out_shape=pltpu.HBM((count, depth), jnp.bfl...  11.8 us
    ppermute x11, starting transfers between devices, swap(): return lax.ppermute(value, 'core', SWAP)  11.8 us
    all_to_all x1, starting transfers between devices, on_device(): lax.all_to_all(sent, PLANE, split_axis=0, concat_axis=0, tiled=True)  6.54 us
    pallas_call x1, Pallas kernels, run_attend(): pl.pallas_call(functools.partial(attend_kernel, parts=parts, copies=copie...  5.94 us
  transfers between devices with their start and end apart: 16, of which 5 were waited for; matrix products, arithmetic and copies ran while one was open for 1% of the time, Pallas kernels for 4%

profile of v4, /device:TPU:1, one launch (start us, length us, event | category | flops | bytes accessed | tf_op | source)
XLA Modules:
  0.0 203.1 jit_solution(545690538765315146)
XLA Ops:
  0.7 1.1 dynamic-slice_bitcast_fusion
  1.7 2.2 %collective-permute-start = (bf16[1024,128]{1,0:T(8,128)(2,1)S(1)}, bf16[1024,128]{1,0:T(8,128)(2,1)S(1)}, u32[]{:S(2)}, u32[]{:S(2)}) collective-permute-start(bf16[1024,128]{1,0:T(8,128)(2,1)S(1)} %get-tuple-element.29), channel_id=1, source_target_pairs={{0,4},{4,0},{1,5},{5,1},{2,6},{6,2},{3,7},{7,3},{8,12},{12,8},{9,1... | collective-permute-start | bytes 786440 | tf_op jit(solution)/shard_map/ppermute | solution.py:366
  3.9 0.7 copy-done.2
  4.6 5.9 %attend.1 = bf16[16,16,2048]{2,1,0:T(8,128)(2,1)} custom-call(s32[16]{0:T(128)S(1)} %copy-done.2, bf16[16,8192]{1,0:T(8,128)(2,1)} %queries_hbm.1, bf16[16,2,128,512]{3,2,1,0:T(8,128)(2,1)} %cache_hbm.1, bf16[16,2,512]{2,1,0:T(2,128)(2,1)} %fresh_hbm.1), custom_call_target="tpu_custom_call" | custom-call | flops 67108864 | bytes 5505024 | tf_op jit(solution)/shard_map/attend/pallas_call | solution.py:103
  10.5 0.1 pad_add_fusion.1.place_ref
  10.6 0.1 copy.46
  10.7 0.1 eq.60
  10.8 1.0 collective-permute-start.8
  11.9 0.1 collective-permute-start.4
  12.0 3.8 %collective-permute-start.3 = (bf16[2,1024,128]{2,1,0:T(8,128)(2,1)S(1)}, bf16[2,1024,128]{2,1,0:T(8,128)(2,1)S(1)}, u32[]{:S(2)}, u32[]{:S(2)}) collective-permute-start(bf16[2,1024,128]{2,1,0:T(8,128)(2,1)S(1)} %pad_maximum_fusion.refs_0_), channel_id=1, source_target_pairs={{0,3},{1,0},{2,1},{3,2},{4,7},{5,4},{6,5},{7,6},{8,11},{9,8},{10,9... | collective-permute-start | bytes 1572872 | tf_op jit(solution)/shard_map/ppermute | solution.py:372
  15.8 0.7 collective-permute-start.1
  16.5 6.5 %all-to-all-start = ((bf16[16,16,2048]{2,1,0:T(8,128)(2,1)}), bf16[16,16,2048]{2,1,0:T(8,128)(2,1)S(1)}, u32[]{:S(2)}, u32[]{:S(2)}) async-start(bf16[16,16,2048]{2,1,0:T(8,128)(2,1)} %attend.1), calls=%async_computation | async-start | bytes 2097152 | tf_op jit(solution)/shard_map/all_to_all | solution.py:393
  23.1 0.1 fusion.8
  23.2 0.2 reduce_window_sum.17
  23.4 0.2 select_reduce_fusion.2
  23.6 0.1 reduce_sum.41
  23.7 1.6 collective-permute-start.9
  25.3 0.1 eq.65
  25.4 0.1 fusion.7
  25.5 0.2 reduce_window_sum.18
  25.7 0.2 select_reduce_fusion.1
  25.8 0.1 reduce_sum.43
  26.0 0.2 fusion.3
  26.1 11.8 %collective-permute-done.3.refs_3_ = bf16[2,1024,128]{2,1,0:T(8,128)(2,1)S(1)} collective-permute-done((bf16[2,1024,128]{2,1,0:T(8,128)(2,1)S(1)}, bf16[2,1024,128]{2,1,0:T(8,128)(2,1)S(1)}, u32[]{:S(2)}, u32[]{:S(2)}) %collective-permute-start.3) | collective-permute-done | bytes 524320 | tf_op jit(solution)/shard_map/ppermute | solution.py:372
  37.9 1.3 collective-permute-start.7
  39.2 2.7 %collective-permute-done.1.refs_1_ = bf16[2,1024,128]{2,1,0:T(8,128)(2,1)} collective-permute-done((bf16[2,1024,128]{2,1,0:T(8,128)(2,1)S(1)}, bf16[2,1024,128]{2,1,0:T(8,128)(2,1)}, u32[]{:S(2)}, u32[]{:S(2)}) %collective-permute-start.1) | collective-permute-done | bytes 524320 | tf_op jit(solution)/shard_map/ppermute | solution.py:372
  41.9 0.8 collective-permute-start.5
  42.7 0.1 pad_maximum_fusion.3
  42.8 0.1 copy.53
  42.9 0.1 copy.52
  43.0 0.2 select_reduce_fusion
  43.2 1.3 collective-permute-done.5.refs_5_
  44.6 3.7 %project.1 = bf16[256,1024]{1,0:T(8,128)(2,1)} custom-call(s32[3]{0:T(128)S(1)} %pad_add_fusion.1.place_ref, bf16[256,2048]{1,0:T(8,128)(2,1)S(1)} %bitcast.20, bf16[2,1024,128]{2,1,0:T(8,128)(2,1)S(1)} %pad_maximum_fusion.refs_0_, bf16[2,1024,128]{2,1,0:T(8,128)(2,1)} %collective-permute-done.1.refs_1_, ...), custom_call_target="tpu_custom_call" | custom-call | flops 1073741824 | bytes 5767168 | tf_op jit(solution)/shard_map/project/pallas_call | solution.py:227
  48.3 16.9 %all_to_all.20.terms_ref = bf16[16,16,1024]{2,1,0:T(8,128)(2,1)S(1)} all-to-all(bf16[16,16,1024]{2,1,0:T(8,128)(2,1)} %bitcast.25), channel_id=1, replica_groups=mesh['xh'=2,'core'=2,'xl'=2,'yh'=2,'yl'=2,'z'=4] {'xh','xl','yh','yl'}, dimensions={0} | all-to-all | bytes 1048576 | tf_op jit(solution)/shard_map/all_to_all | solution.py:396
  65.2 0.8 norm.1
  65.9 2.1 %collective-permute-start.10 = (bf16[16,4096]{1,0:T(8,128)(2,1)S(1)}, bf16[16,4096]{1,0:T(8,128)(2,1)S(1)}, u32[]{:S(2)}, u32[]{:S(2)}) collective-permute-start(bf16[16,4096]{1,0:T(8,128)(2,1)S(1)} %get-tuple-element.23.own_ref), channel_id=1, source_target_pairs={{0,32},{32,0},{1,33},{33,1},{2,34},{34,2},{3,35},{35,3},{4,36},{36... | collective-permute-start | bytes 393224 | tf_op jit(solution)/shard_map/ppermute | solution.py:321
  68.0 1.0 collective-permute-done.10.other_ref
  69.0 0.4 collective-permute-start.11
  69.4 0.1 collective-permute-start.12
  69.5 0.4 collective-permute-start.13
  69.9 2.5 %place.1 = bf16[512,4096]{1,0:T(8,128)(2,1)} custom-call(bf16[256,32]{1,0:T(8,128)(2,1)S(1)} %bitcast.21, bf16[16,4096]{1,0:T(8,128)(2,1)S(1)} %get-tuple-element.23.own_ref, bf16[16,4096]{1,0:T(8,128)(2,1)S(1)} %collective-permute-done.10.other_ref), custom_call_target="tpu_custom_call" | custom-call | flops 67108864 | bytes 4194304 | tf_op jit(solution)/shard_map/place/pallas_call | solution.py:306
  72.4 55.8 %all_to_all.21 = bf16[64,8,4096]{2,1,0:T(8,128)(2,1)S(1)} all-to-all(bf16[64,8,4096]{2,1,0:T(8,128)(2,1)} %bitcast.24), channel_id=1, replica_groups=mesh['xh'=2,'core'=2,'xl'=2,'yh'=2,'yl'=2,'z'=4] {'xh','xl','yh','yl','z'}, dimensions={0} | all-to-all | bytes 8388608 | tf_op jit(solution)/shard_map/all_to_all | solution.py:405
  128.2 11.8 %expert.1 = bf16[512,4096]{1,0:T(8,128)(2,1)} custom-call(s32[1]{0:T(128)} %bitcast.2.core_ref, bf16[512,4096]{1,0:T(8,128)(2,1)S(1)} %bitcast.17, bf16[2,4096,384]{2,1,0:T(8,128)(2,1)S(1)} %bitcast.19, bf16[2,4096,384]{2,1,0:T(8,128)(2,1)} %up_a, bf16[2,384,4096]{2,1,0:T(8,128)(2,1)} %down_a, bf16[2,4096,384]{2,1,0:T(8,128)(2,1)S(1)} %collective-permute-done.11.gate_b, ...), custom_call_target="tpu_custom_call" | custom-call | flops 9663676416 | bytes 27262976 | tf_op jit(solution)/shard_map/expert/pallas_call | solution.py:179
  140.0 56.4 %all_to_all.22 = bf16[64,8,4096]{2,1,0:T(8,128)(2,1)S(1)} all-to-all(bf16[64,8,4096]{2,1,0:T(8,128)(2,1)} %bitcast.23), channel_id=1, replica_groups=mesh['xh'=2,'core'=2,'xl'=2,'yh'=2,'yl'=2,'z'=4] {'xh','xl','yh','yl','z'}, dimensions={0} | all-to-all | bytes 8388608 | tf_op jit(solution)/shard_map/all_to_all | solution.py:418
  196.5 0.8 fusion
  197.4 4.0 %collective-permute-start.14 = (bf16[16,4096]{1,0:T(8,128)(2,1)S(1)}, bf16[16,4096]{1,0:T(8,128)(2,1)S(1)}, u32[]{:S(2)}, u32[]{:S(2)}) collective-permute-start(bf16[16,4096]{1,0:T(8,128)(2,1)S(1)} %slice.27), channel_id=1, source_target_pairs={{0,32},{32,0},{1,33},{33,1},{2,34},{34,2},{3,35},{35,3},{4,36},{36... | collective-permute-start | bytes 393224 | tf_op jit(solution)/shard_map/ppermute | solution.py:321
  201.4 1.0 collective-permute-done.14
  202.4 0.7 fusion.2
  (39 shorter events, 0.3 us)
Async XLA Ops:
  0.6 15.9 %copy-start.3 = (f32[16,8]{0,1:T(8,128)S(1)}, f32[16,8]{0,1:T(8,128)}, u32[]{:S(2)}) copy-start(f32[16,8]{0,1:T(8,128)} %param.19) | copy-start | bytes 1540
  0.6 10.0 %copy-start.4 = (s32[16,8]{0,1:T(8,128)S(1)}, s32[16,8]{0,1:T(8,128)}, u32[]{:S(2)}) copy-start(s32[16,8]{0,1:T(8,128)} %param.18) | copy-start | bytes 1540
  1.7 8.9 %collective-permute-start = (bf16[1024,128]{1,0:T(8,128)(2,1)S(1)}, bf16[1024,128]{1,0:T(8,128)(2,1)S(1)}, u32[]{:S(2)}, u32[]{:S(2)}) collective-permute-start(bf16[1024,128]{1,0:T(8,128)(2,1)S(1)} %get-tuple-element.29), channel_id=1, source_target_pairs={{0,4},{4,0},{1,5},{5,1},{2,6},{6,2},{3,7},{7,3},{8,12},{12,8},{9,1... | collective-permute-start | bytes 786440 | tf_op jit(solution)/shard_map/ppermute | solution.py:366
  3.9 0.7 copy-start.2
  10.8 12.9 %collective-permute-start.8 = (s32[16,8]{1,0:T(8,128)S(1)}, s32[16,8]{1,0:T(8,128)S(1)}, u32[]{:S(2)}, u32[]{:S(2)}) collective-permute-start(s32[16,8]{1,0:T(8,128)S(1)} %copy.46), channel_id=1, source_target_pairs={{0,32},{32,0},{1,33},{33,1},{2,34},{34,2},{3,35},{35,3},{4,36},{36... | collective-permute-start | bytes 1544 | tf_op jit(solution)/shard_map/ppermute | solution.py:321
  11.9 31.3 %collective-permute-start.4 = (bf16[2,1024,128]{2,1,0:T(8,128)(2,1)S(1)}, bf16[2,1024,128]{2,1,0:T(8,128)(2,1)S(1)}, u32[]{:S(2)}, u32[]{:S(2)}) collective-permute-start(bf16[2,1024,128]{2,1,0:T(8,128)(2,1)S(1)} %pad_maximum_fusion.refs_0_), channel_id=1, source_target_pairs={{0,32},{32,0},{1,33},{33,1},{2,34},{34,2},{3,35},{35,3},{4,36},{36... | collective-permute-start | bytes 1572872 | tf_op jit(solution)/shard_map/ppermute | solution.py:321
  12.0 25.9 %collective-permute-start.3 = (bf16[2,1024,128]{2,1,0:T(8,128)(2,1)S(1)}, bf16[2,1024,128]{2,1,0:T(8,128)(2,1)S(1)}, u32[]{:S(2)}, u32[]{:S(2)}) collective-permute-start(bf16[2,1024,128]{2,1,0:T(8,128)(2,1)S(1)} %pad_maximum_fusion.refs_0_), channel_id=1, source_target_pairs={{0,3},{1,0},{2,1},{3,2},{4,7},{5,4},{6,5},{7,6},{8,11},{9,8},{10,9... | collective-permute-start | bytes 1572872 | tf_op jit(solution)/shard_map/ppermute | solution.py:372
  15.8 23.4 %collective-permute-start.2 = (bf16[2,1024,128]{2,1,0:T(8,128)(2,1)S(1)}, bf16[2,1024,128]{2,1,0:T(8,128)(2,1)S(1)}, u32[]{:S(2)}, u32[]{:S(2)}) collective-permute-start(bf16[2,1024,128]{2,1,0:T(8,128)(2,1)S(1)} %pad_maximum_fusion.refs_0_), channel_id=1, source_target_pairs={{0,2},{1,3},{2,0},{3,1},{4,6},{5,7},{6,4},{7,5},{8,10},{9,11},{10,... | collective-permute-start | bytes 1572872 | tf_op jit(solution)/shard_map/ppermute | solution.py:372
  15.8 26.1 %collective-permute-start.1 = (bf16[2,1024,128]{2,1,0:T(8,128)(2,1)S(1)}, bf16[2,1024,128]{2,1,0:T(8,128)(2,1)}, u32[]{:S(2)}, u32[]{:S(2)}) collective-permute-start(bf16[2,1024,128]{2,1,0:T(8,128)(2,1)S(1)} %pad_maximum_fusion.refs_0_), channel_id=1, source_target_pairs={{0,1},{1,2},{2,3},{3,0},{4,5},{5,6},{6,7},{7,4},{8,9},{9,10},{10,1... | collective-permute-start | bytes 1572872 | tf_op jit(solution)/shard_map/ppermute | solution.py:372
  16.5 26.7 %all-to-all-start = ((bf16[16,16,2048]{2,1,0:T(8,128)(2,1)}), bf16[16,16,2048]{2,1,0:T(8,128)(2,1)S(1)}, u32[]{:S(2)}, u32[]{:S(2)}) async-start(bf16[16,16,2048]{2,1,0:T(8,128)(2,1)} %attend.1), calls=%async_computation | async-start | bytes 2097152 | tf_op jit(solution)/shard_map/all_to_all | solution.py:393
  23.1 42.1 %copy-start = (bf16[16,4096]{1,0:T(8,128)(2,1)S(1)}, bf16[16,4096]{1,0:T(8,128)(2,1)}, u32[]{:S(2)}) copy-start(bf16[16,4096]{1,0:T(8,128)(2,1)} %residual_ref.1) | copy-start | bytes 393220
  23.1 42.1 %copy-start.1 = (f32[4096]{0:T(1024)S(1)}, f32[4096]{0:T(1024)}, u32[]{:S(2)}) copy-start(f32[4096]{0:T(1024)} %param.17) | copy-start | bytes 49156
  23.7 19.0 %collective-permute-start.9 = (f32[16,8]{0,1:T(8,128)S(1)}, f32[16,8]{0,1:T(8,128)S(1)}, u32[]{:S(2)}, u32[]{:S(2)}) collective-permute-start(f32[16,8]{0,1:T(8,128)S(1)} %broadcast_divide_fusion), channel_id=1, source_target_pairs={{0,32},{32,0},{1,33},{33,1},{2,34},{34,2},{3,35},{35,3},{4,36},{36... | collective-permute-start | bytes 1544 | tf_op jit(solution)/shard_map/ppermute | solution.py:321
  37.9 5.3 %collective-permute-start.7 = (bf16[2,1024,128]{2,1,0:T(8,128)(2,1)S(1)}, bf16[2,1024,128]{2,1,0:T(8,128)(2,1)}, u32[]{:S(2)}, u32[]{:S(2)}) collective-permute-start(bf16[2,1024,128]{2,1,0:T(8,128)(2,1)S(1)} %collective-permute-done.3.refs_3_), channel_id=1, source_target_pairs={{0,32},{32,0},{1,33},{33,1},{2,34},{34,2},{3,35},{35,3},{4,36},{36... | collective-permute-start | bytes 1572872 | tf_op jit(solution)/shard_map/ppermute | solution.py:321
  39.2 4.1 %collective-permute-start.6 = (bf16[2,1024,128]{2,1,0:T(8,128)(2,1)S(1)}, bf16[2,1024,128]{2,1,0:T(8,128)(2,1)}, u32[]{:S(2)}, u32[]{:S(2)}) collective-permute-start(bf16[2,1024,128]{2,1,0:T(8,128)(2,1)S(1)} %collective-permute-done.2.refs_2_), channel_id=1, source_target_pairs={{0,32},{32,0},{1,33},{33,1},{2,34},{34,2},{3,35},{35,3},{4,36},{36... | collective-permute-start | bytes 1572872 | tf_op jit(solution)/shard_map/ppermute | solution.py:321
  41.9 2.7 %collective-permute-start.5 = (bf16[2,1024,128]{2,1,0:T(8,128)(2,1)}, bf16[2,1024,128]{2,1,0:T(8,128)(2,1)}, u32[]{:S(2)}, u32[]{:S(2)}) collective-permute-start(bf16[2,1024,128]{2,1,0:T(8,128)(2,1)} %collective-permute-done.1.refs_1_), channel_id=1, source_target_pairs={{0,32},{32,0},{1,33},{33,1},{2,34},{34,2},{3,35},{35,3},{4,36},{36... | collective-permute-start | bytes 1572872 | tf_op jit(solution)/shard_map/ppermute | solution.py:321
  65.9 3.1 %collective-permute-start.10 = (bf16[16,4096]{1,0:T(8,128)(2,1)S(1)}, bf16[16,4096]{1,0:T(8,128)(2,1)S(1)}, u32[]{:S(2)}, u32[]{:S(2)}) collective-permute-start(bf16[16,4096]{1,0:T(8,128)(2,1)S(1)} %get-tuple-element.23.own_ref), channel_id=1, source_target_pairs={{0,32},{32,0},{1,33},{33,1},{2,34},{34,2},{3,35},{35,3},{4,36},{36... | collective-permute-start | bytes 393224 | tf_op jit(solution)/shard_map/ppermute | solution.py:321
  69.0 59.2 %collective-permute-start.11 = (bf16[2,4096,384]{2,1,0:T(8,128)(2,1)}, bf16[2,4096,384]{2,1,0:T(8,128)(2,1)S(1)}, u32[]{:S(2)}, u32[]{:S(2)}) collective-permute-start(bf16[2,4096,384]{2,1,0:T(8,128)(2,1)} %gate_a), channel_id=1, source_target_pairs={{0,32},{32,0},{1,33},{33,1},{2,34},{34,2},{3,35},{35,3},{4,36},{36... | collective-permute-start | bytes 18874376 | tf_op jit(solution)/shard_map/ppermute | solution.py:321
  69.4 58.8 %collective-permute-start.12 = (bf16[2,4096,384]{2,1,0:T(8,128)(2,1)}, bf16[2,4096,384]{2,1,0:T(8,128)(2,1)S(1)}, u32[]{:S(2)}, u32[]{:S(2)}) collective-permute-start(bf16[2,4096,384]{2,1,0:T(8,128)(2,1)} %up_a), channel_id=1, source_target_pairs={{0,32},{32,0},{1,33},{33,1},{2,34},{34,2},{3,35},{35,3},{4,36},{36... | collective-permute-start | bytes 18874376 | tf_op jit(solution)/shard_map/ppermute | solution.py:321
  69.5 58.6 %collective-permute-start.13 = (bf16[2,384,4096]{2,1,0:T(8,128)(2,1)}, bf16[2,384,4096]{2,1,0:T(8,128)(2,1)S(1)}, u32[]{:S(2)}, u32[]{:S(2)}) collective-permute-start(bf16[2,384,4096]{2,1,0:T(8,128)(2,1)} %down_a), channel_id=1, source_target_pairs={{0,32},{32,0},{1,33},{33,1},{2,34},{34,2},{3,35},{35,3},{4,36},{36... | collective-permute-start | bytes 18874376 | tf_op jit(solution)/shard_map/ppermute | solution.py:321
  69.9 58.3 %slice-start = ((s8[6291456]{0:T(1024)(128)(4,1)}), s8[4194304]{0:T(1024)(128)(4,1)S(1)}, s32[]{:S(2)}) async-start(s8[6291456]{0:T(1024)(128)(4,1)} %bitcast.18), calls=%async_computation.4 | async-start | bytes 8388608
  72.4 55.8 %slice-start.1 = ((s8[6291456]{0:T(1024)(128)(4,1)}), s8[2097152]{0:T(1024)(128)(4,1)S(1)}, s32[]{:S(2)}) async-start(s8[6291456]{0:T(1024)(128)(4,1)} %bitcast.18), calls=%async_computation.5 | async-start | bytes 4194304
  197.4 5.0 %collective-permute-start.14 = (bf16[16,4096]{1,0:T(8,128)(2,1)S(1)}, bf16[16,4096]{1,0:T(8,128)(2,1)S(1)}, u32[]{:S(2)}, u32[]{:S(2)}) collective-permute-start(bf16[16,4096]{1,0:T(8,128)(2,1)S(1)} %slice.27), channel_id=1, source_target_pairs={{0,32},{32,0},{1,33},{33,1},{2,34},{34,2},{3,35},{35,3},{4,36},{36... | collective-permute-start | bytes 393224 | tf_op jit(solution)/shard_map/ppermute | solution.py:321

commit v5 on v4

--- a/solution.py
+++ b/solution.py
@@ -26,15 +26,16 @@
 
 
 def attend_kernel(
-    lengths_ref, queries_hbm, cache_hbm, fresh_hbm, out_ref, queries_ref, cache, fresh_ref, heads, sems, *, parts, copies
+    lengths_hbm, queries_hbm, cache_hbm, fresh_hbm, out_ref, lengths_ref, queries_ref, cache, fresh_ref, heads, sems, *, parts, copies
 ):
     rows = queries_ref.shape[0]
-    batches = sems.shape[0] - 2
+    batches = sems.shape[0] - 3
     batch = rows // batches
     span = cache.shape[2]
     others = [
         pltpu.make_async_copy(queries_hbm, queries_ref, sems.at[batches]),
         pltpu.make_async_copy(fresh_hbm, fresh_ref, sems.at[batches + 1]),
+        pltpu.make_async_copy(lengths_hbm, lengths_ref, sems.at[batches + 2]),
     ]
     for other in others:
         other.start()
@@ -99,18 +100,19 @@
 def run_attend(queries, kv_cache, kv_new, lengths, parts, copies):
     rows = queries.shape[0]
     hbm = pl.BlockSpec(memory_space=pltpu.HBM)
-    operands = [pltpu.with_memory_space_constraint(value, pltpu.HBM) for value in (queries, kv_cache, kv_new)]
+    operands = [pltpu.with_memory_space_constraint(value, pltpu.HBM) for value in (lengths, queries, kv_cache, kv_new)]
     return pl.pallas_call(
         functools.partial(attend_kernel, parts=parts, copies=copies),
         out_shape=pltpu.HBM((copies * parts, rows, HEADS * HD // parts), jnp.bfloat16),
-        in_specs=[pl.BlockSpec(memory_space=pltpu.SMEM)] + [hbm] * 3,
+        in_specs=[hbm] * 4,
         out_specs=pl.BlockSpec(memory_space=pltpu.VMEM),
         scratch_shapes=[
+            pltpu.SMEM(lengths.shape, jnp.int32),
             pltpu.VMEM(queries.shape, jnp.bfloat16),
             pltpu.VMEM(kv_cache.shape, jnp.bfloat16),
             pltpu.VMEM(kv_new.shape, jnp.bfloat16),
             pltpu.VMEM((rows * HEADS, HD), jnp.float32),
-            pltpu.SemaphoreType.DMA((6,)),
+            pltpu.SemaphoreType.DMA((7,)),
         ],
         compiler_params=pltpu.CompilerParams(vmem_limit_bytes=24 * MIB),
         cost_estimate=pl.CostEstimate(
@@ -119,11 +121,11 @@
             transcendentals=rows * HEADS * kv_cache.shape[2],
         ),
         name="attend",
-    )(lengths, *operands)
+    )(*operands)
 
 
 def expert_kernel(
-    core_ref, rows, gate_a, up_a, down_a, gate_b, up_b, down_b, out_hbm, gate, up, down, hidden, out, sems, out_sems
+    core_ref, rows, gate_a, up_a, down_a, gate_b, up_b, down_b, out, gate, up, down, hidden, sems
 ):
     mine = core_ref[0]
     depth = rows.shape[1]
@@ -156,16 +158,10 @@
 
     @pl.when(mine >= 0)
     def _():
-        stores = []
         for start in range(0, depth, WIDE):
             cols = slice(start, start + WIDE)
             both = jnp.concatenate([down_b[mine, :, cols], down[:, cols]], axis=0)
             out[:, cols] = jnp.dot(hidden[...], both, preferred_element_type=jnp.float32).astype(out.dtype)
-            at = pl.ds(start, WIDE)
-            stores.append(pltpu.make_async_copy(out.at[:, at], out_hbm.at[:, at], out_sems.at[start // WIDE]))
-            stores[-1].start()
-        for store in stores:
-            store.wait()
 
 
 def run_expert(core, rows, gate_a, up_a, down_a, gate_b, up_b, down_b):
@@ -178,17 +174,15 @@
     )
     return pl.pallas_call(
         expert_kernel,
-        out_shape=pltpu.HBM((count, depth), jnp.bfloat16),
+        out_shape=pltpu.VMEM((count, depth), jnp.bfloat16),
         in_specs=[pl.BlockSpec(memory_space=pltpu.SMEM), vmem] + [hbm] * 3 + [vmem] * 3,
-        out_specs=hbm,
+        out_specs=vmem,
         scratch_shapes=[
             pltpu.VMEM((depth, share), jnp.bfloat16),
             pltpu.VMEM((depth, share), jnp.bfloat16),
             pltpu.VMEM((share, depth), jnp.bfloat16),
             pltpu.VMEM((count, 2 * share), jnp.bfloat16),
-            pltpu.VMEM((count, depth), jnp.bfloat16),
             pltpu.SemaphoreType.DMA((6,)),
-            pltpu.SemaphoreType.DMA((depth // WIDE,)),
         ],
         compiler_params=pltpu.CompilerParams(vmem_limit_bytes=24 * MIB),
         cost_estimate=pl.CostEstimate(
@@ -202,15 +196,20 @@
 
 def project_kernel(place_ref, rows_ref, *refs):
     *weights, out_ref = refs
+    kinds = len(weights) // 2
     half, width = weights[0].shape[1:]
-    ring = len(weights) // 2
+    ring = kinds - 1
     pair, turn, core = place_ref[0], place_ref[1], place_ref[2]
     near = rows_ref[:, pl.ds(pl.multiple_of(core * half, half), half)]
     far = rows_ref[:, pl.ds(pl.multiple_of((1 - core) * half, half), half)]
     for step in range(ring):
         total = None
-        for rows, weight in ((near, weights[step]), (far, weights[ring + step])):
-            both = jnp.concatenate([weight[0], weight[1]], axis=1)
+        for rows, (own, before, after, first, second) in ((near, weights[:kinds]), (far, weights[kinds:])):
+            if step == 2:
+                both = jnp.concatenate([first[...], second[...]], axis=1)
+            else:
+                weight = {0: own, 1: before, 3: after}[step]
+                both = jnp.concatenate([weight[0], weight[1]], axis=1)
             term = jnp.dot(rows, both, preferred_element_type=jnp.float32)
             total = term if total is None else total + term
         total = total.astype(out_ref.dtype)
@@ -222,11 +221,12 @@
 
 def run_project(place, rows, weights):
     count, depth = rows.shape
-    width = len(weights) * weights[0].shape[2]
+    width = 8 * weights[0].shape[2]
     vmem = pl.BlockSpec(memory_space=pltpu.VMEM)
+    weights = [pltpu.with_memory_space_constraint(value, pltpu.VMEM) for value in weights]
     return pl.pallas_call(
         project_kernel,
-        out_shape=pltpu.HBM((count, width), jnp.bfloat16),
+        out_shape=pltpu.VMEM((count, width), jnp.bfloat16),
         in_specs=[pl.BlockSpec(memory_space=pltpu.SMEM)] + [vmem] * (1 + len(weights)),
         out_specs=vmem,
         compiler_params=pltpu.CompilerParams(vmem_limit_bytes=16 * MIB),
@@ -279,25 +279,15 @@
     )(terms, residual, gain.reshape(1, -1))
 
 
-def place_kernel(placing_ref, own_ref, other_ref, out_hbm, out, sems):
+def place_kernel(placing_ref, own_ref, other_ref, out_ref):
     count = placing_ref.shape[0]
     step = count // 4
     rows = jnp.concatenate([own_ref[...], other_ref[...]], axis=0)
-    stores = []
     for start in range(0, count, step):
         value = jnp.dot(placing_ref[start : start + step, :], rows, preferred_element_type=jnp.float32)
-        out[start : start + step, :] = value.astype(out.dtype)
+        value = value.astype(out_ref.dtype)
         for copy in range(2):
-            stores.append(
-                pltpu.make_async_copy(
-                    out.at[pl.ds(start, step)],
-                    out_hbm.at[pl.ds(copy * count + start, step)],
-                    sems.at[len(stores)],
-                )
-            )
-            stores[-1].start()
-    for store in stores:
-        store.wait()
+            out_ref[copy * count + start : copy * count + start + step, :] = value
 
 
 def run_place(placing, own, other):
@@ -305,10 +295,9 @@
     count, depth = placing.shape[0], own.shape[1]
     return pl.pallas_call(
         place_kernel,
-        out_shape=pltpu.HBM((2 * count, depth), jnp.bfloat16),
+        out_shape=pltpu.VMEM((2 * count, depth), jnp.bfloat16),
         in_specs=[vmem] * 3,
-        out_specs=pl.BlockSpec(memory_space=pltpu.HBM),
-        scratch_shapes=[pltpu.VMEM((count, depth), jnp.bfloat16), pltpu.SemaphoreType.DMA((8,))],
+        out_specs=vmem,
         compiler_params=pltpu.CompilerParams(vmem_limit_bytes=16 * MIB),
         cost_estimate=pl.CostEstimate(
             flops=2 * placing.size * depth, bytes_accessed=4 * count * depth, transcendentals=0
@@ -361,18 +350,17 @@
 
     pair = lax.axis_index("yl")
     quarter = lax.axis_index("xh") * 2
-    kept = lax.dynamic_slice_in_dim(w_out, (quarter + pair) * depth + core * half, half, axis=0)
     given = lax.dynamic_slice_in_dim(w_out, (quarter + 1 - pair) * depth + core * half, half, axis=0)
+    given, w_rest = lax.optimization_barrier((given, w_out))
+    kept = lax.dynamic_slice_in_dim(w_rest, (quarter + pair) * depth + core * half, half, axis=0)
     taken = lax.ppermute(given, "yl", SWAP)
     sent = run_attend(queries, kv_cache, kv_new, lengths, parts, plane // parts)
     sent, taken, expert_ids, route_probs = lax.optimization_barrier((sent, taken, expert_ids, route_probs))
-    weights = [jnp.stack([kept, taken])]
-    for step in range(1, ring):
-        turn = [(place, (place + step) % ring) for place in range(ring)]
-        weights.append(lax.ppermute(weights[0], "z", turn))
-    weights += [swap(value) for value in weights]
-    place = jnp.stack([pair, lax.axis_index("z"), core]).astype(jnp.int32)
-
+    own = jnp.stack([kept, taken])
+    forth = [(at, (at + 1) % ring) for at in range(ring)]
+    back = [(at, (at + ring - 1) % ring) for at in range(ring)]
+    before = lax.ppermute(own, "z", forth)
+    after = lax.ppermute(own, "z", back)
     expert_total = w_gate.shape[0] * ep_size
     slot_total = 2 * SLOTS * ep_size
     gates = route_probs / jnp.sum(route_probs, -1, keepdims=True)
@@ -390,9 +378,13 @@
     mixing_low = (mixing - mixing_high.astype(jnp.float32)).astype(jnp.bfloat16)
     mixing = jnp.concatenate([mixing_high, mixing_low], 0)
 
+    passed, placing, mixing = lax.optimization_barrier((before[0], placing, mixing))
+    weights = [own, before, after, lax.ppermute(passed, "z", forth), lax.ppermute(after[1], "z", back)]
+    given = lax.optimization_barrier(weights[:4])
+    weights += [swap(value) for value in given + weights[4:]]
+    place = jnp.stack([pair, lax.axis_index("z"), core]).astype(jnp.int32)
     gathered = lax.all_to_all(sent, PLANE, split_axis=0, concat_axis=0, tiled=True)
     columns = run_project(place, gathered.reshape(plane * row_count, depth), weights)
-    columns, placing, mixing = lax.optimization_barrier((columns, placing, mixing))
     terms = lax.all_to_all(
         columns.reshape(plane, row_count, -1), PLANE, split_axis=0, concat_axis=0, tiled=True
     )

time: 204 us -> 199 us (0.975)
  Pallas kernels: 24.7 us -> 20.3 us
  waiting for transfers between devices: 17.8 us -> 14.5 us
  starting transfers between devices: 25.1 us -> 27.4 us
    ppermute x3 -> x4, waiting for transfers between devices: 14.5 us -> 9.55 us  [the longest x1 5.12 us: on_device(): lax.ppermute(passed, 'z', forth)]
    pallas_call x3, Pallas kernels: 18 us -> 14.1 us  [the longest x1 10.6 us: run_expert(): pl.pallas_call(expert_kernel, out_shape=pltpu.VMEM((count, depth), jnp.bf...]
    ppermute x3 -> x4, starting transfers between devices: 4.52 us -> 6.79 us  [the longest x1 3.99 us: on_device(): after = lax.ppermute(own, 'z', back)]
    ppermute x11 -> x12, waiting for transfers between devices: 3.33 us -> 4.8 us  [swap(): return lax.ppermute(value, 'core', SWAP)]
    ppermute x11 -> x12, starting transfers between devices: 11.8 us -> 11.6 us  [swap(): return lax.ppermute(value, 'core', SWAP)]
  transfers between devices with their start and end apart: 16 -> 18, of which waited for: 5 -> 7; matrix products, arithmetic and copies ran while one was open for 1% -> 1% of each run, Pallas kernels for 4% -> 3%
where the time goes in v5:
time: 199 us; the launch traced here: 198 us
  blocking collectives  129 us (65%)
  starting transfers between devices  27.4 us (14%)
  Pallas kernels  20.3 us (10%)
  waiting for transfers between devices  14.5 us (7%)
  other arithmetic  2.86 us (1%)
  local copies, waits for them, and re-layouts  2.3 us (1%)
    all_to_all x1, blocking collectives, on_device(): lax.all_to_all(partial_value.reshape(chips, 2 * SLOTS, -1), CHIPS, split_...  57.5 us
    all_to_all x1, blocking collectives, on_device(): lax.all_to_all(outgoing.reshape(chips, 2 * SLOTS, -1), CHIPS, split_axis=...  54.7 us
    all_to_all x1, blocking collectives, on_device(): lax.all_to_all(columns.reshape(plane, row_count, -1), PLANE, split_axis=0...  16.9 us
    ppermute x12, starting transfers between devices, swap(): return lax.ppermute(value, 'core', SWAP)  11.6 us
    pallas_call x1, Pallas kernels, run_expert(): pl.pallas_call(expert_kernel, out_shape=pltpu.VMEM((count, depth), jnp.bf...  10.6 us
    all_to_all x1, starting transfers between devices, on_device(): lax.all_to_all(sent, PLANE, split_axis=0, concat_axis=0, tiled=True)  6.77 us
    pallas_call x1, Pallas kernels, run_attend(): pl.pallas_call(functools.partial(attend_kernel, parts=parts, copies=copie...  5.44 us
    ppermute x1, waiting for transfers between devices, on_device(): lax.ppermute(passed, 'z', forth)  5.12 us
  transfers between devices with their start and end apart: 18, of which 7 were waited for; matrix products, arithmetic and copies ran while one was open for 1% of the time, Pallas kernels for 3%

profile of v5, /device:TPU:1, one launch (start us, length us, event | category | flops | bytes accessed | tf_op | source)
XLA Modules:
  0.0 198.2 jit_solution(14467005733393216242)
XLA Ops:
  0.7 1.6 copy-done
  2.3 2.2 %collective-permute-start = (bf16[1024,128]{1,0:T(8,128)(2,1)S(1)}, bf16[1024,128]{1,0:T(8,128)(2,1)S(1)}, u32[]{:S(2)}, u32[]{:S(2)}) collective-permute-start(bf16[1024,128]{1,0:T(8,128)(2,1)S(1)} %constant_dynamic-slice_fusion), channel_id=1, source_target_pairs={{0,4},{4,0},{1,5},{5,1},{2,6},{6,2},{3,7},{7,3},{8,12},{12,8},{9,1... | collective-permute-start | bytes 786440 | tf_op jit(solution)/shard_map/ppermute | solution.py:356
  4.5 5.4 %attend.1 = bf16[16,16,2048]{2,1,0:T(8,128)(2,1)} custom-call(s32[16]{0:T(128)} %lengths_hbm.1, bf16[16,8192]{1,0:T(8,128)(2,1)} %queries_hbm.1, bf16[16,2,128,512]{3,2,1,0:T(8,128)(2,1)} %cache_hbm.1, bf16[16,2,512]{2,1,0:T(2,128)(2,1)} %fresh_hbm.1), custom_call_target="tpu_custom_call" | custom-call | flops 67108864 | bytes 5505024 | tf_op jit(solution)/shard_map/attend/pallas_call | solution.py:104
  10.0 0.1 collective-permute-done
  10.2 0.1 eq.60
  10.3 1.7 collective-permute-start.3
  12.0 4.0 %collective-permute-start.2 = (bf16[2,1024,128]{2,1,0:T(8,128)(2,1)S(1)}, bf16[2,1024,128]{2,1,0:T(8,128)(2,1)S(1)}, u32[]{:S(2)}, u32[]{:S(2)}) collective-permute-start(bf16[2,1024,128]{2,1,0:T(8,128)(2,1)S(1)} %pad_maximum_fusion.refs_0_), channel_id=1, source_target_pairs={{0,3},{1,0},{2,1},{3,2},{4,7},{5,4},{6,5},{7,6},{8,11},{9,8},{10,9... | collective-permute-start | bytes 1572872 | tf_op jit(solution)/shard_map/ppermute | solution.py:363
  16.1 6.8 %all-to-all-start = ((bf16[16,16,2048]{2,1,0:T(8,128)(2,1)}), bf16[16,16,2048]{2,1,0:T(8,128)(2,1)S(1)}, u32[]{:S(2)}, u32[]{:S(2)}) async-start(bf16[16,16,2048]{2,1,0:T(8,128)(2,1)} %attend.1), calls=%async_computation | async-start | bytes 2097152 | tf_op jit(solution)/shard_map/all_to_all | solution.py:386
  22.8 0.7 collective-permute-start.4
  23.5 0.1 fusion.8
  23.6 0.2 reduce_window_sum.17
  23.7 0.2 select_reduce_fusion.2
  23.9 0.1 reduce_sum.41
  24.1 0.1 eq.65
  24.1 0.1 fusion.7
  24.2 0.2 reduce_window_sum.18
  24.4 0.2 select_reduce_fusion.1
  24.6 0.1 reduce_sum.43
  24.7 0.2 fusion.3
  24.9 0.1 pad_maximum_fusion.3
  25.0 0.1 copy.53
  25.1 0.2 select_reduce_fusion
  25.3 0.1 copy.52
  25.4 0.6 pad_maximum_fusion.2
  26.0 4.4 %collective-permute-done.1.refs_1_ = bf16[2,1024,128]{2,1,0:T(8,128)(2,1)S(1)} collective-permute-done((bf16[2,1024,128]{2,1,0:T(8,128)(2,1)S(1)}, bf16[2,1024,128]{2,1,0:T(8,128)(2,1)S(1)}, u32[]{:S(2)}, u32[]{:S(2)}) %collective-permute-start.1) | collective-permute-done | bytes 524320 | tf_op jit(solution)/shard_map/ppermute | solution.py:362
  30.6 2.7 %collective-permute-start.6 = (bf16[1024,128]{1,0:T(8,128)(2,1)S(1)}, bf16[1024,128]{1,0:T(8,128)(2,1)}, u32[]{:S(2)}, u32[]{:S(2)}) collective-permute-start(bf16[1024,128]{1,0:T(8,128)(2,1)S(1)} %slice_bitcast_fusion), channel_id=1, source_target_pairs={{0,3},{1,0},{2,1},{3,2},{4,7},{5,4},{6,5},{7,6},{8,11},{9,8},{10,9... | collective-permute-start | bytes 786440 | tf_op jit(solution)/shard_map/ppermute | solution.py:382
  33.3 5.1 %collective-permute-done.5.refs_3_ = bf16[1024,128]{1,0:T(8,128)(2,1)S(1)} collective-permute-done((bf16[1024,128]{1,0:T(8,128)(2,1)S(1)}, bf16[1024,128]{1,0:T(8,128)(2,1)S(1)}, u32[]{:S(2)}, u32[]{:S(2)}) %collective-permute-start.5) | collective-permute-done | bytes 262176 | tf_op jit(solution)/shard_map/ppermute | solution.py:382
  38.4 2.0 %collective-permute-start.7 = (bf16[2,1024,128]{2,1,0:T(8,128)(2,1)S(1)}, bf16[2,1024,128]{2,1,0:T(8,128)(2,1)S(1)}, u32[]{:S(2)}, u32[]{:S(2)}) collective-permute-start(bf16[2,1024,128]{2,1,0:T(8,128)(2,1)S(1)} %pad_maximum_fusion.refs_0_), channel_id=1, source_target_pairs={{0,32},{32,0},{1,33},{33,1},{2,34},{34,2},{3,35},{35,3},{4,36},{36... | collective-permute-start | bytes 1572872 | tf_op jit(solution)/shard_map/ppermute | solution.py:310
  40.5 0.5 collective-permute-start.9
  41.0 0.5 collective-permute-start.10
  41.6 2.2 %collective-permute-done.11.refs_9_ = bf16[1024,128]{1,0:T(8,128)(2,1)} collective-permute-done((bf16[1024,128]{1,0:T(8,128)(2,1)}, bf16[1024,128]{1,0:T(8,128)(2,1)}, u32[]{:S(2)}, u32[]{:S(2)}) %collective-permute-start.11) | collective-permute-done | bytes 262176 | tf_op jit(solution)/shard_map/ppermute | solution.py:310
  43.8 0.6 collective-permute-done.10.refs_8_
  44.4 2.8 %project.1 = bf16[256,1024]{1,0:T(8,128)(2,1)S(1)} custom-call(s32[3]{0:T(128)S(1)} %pad_add_fusion.1.place_ref, bf16[256,2048]{1,0:T(8,128)(2,1)S(1)} %bitcast.24, bf16[2,1024,128]{2,1,0:T(8,128)(2,1)S(1)} %pad_maximum_fusion.refs_0_, bf16[2,1024,128]{2,1,0:T(8,128)(2,1)S(1)} %collective-permute-done.1.refs_1_, ...), custom_call_target="tpu_custom_call" | custom-call | flops 1073741824 | bytes 5767168 | tf_op jit(solution)/shard_map/project/pallas_call | solution.py:227
  47.2 16.9 %all_to_all.20.terms_ref = bf16[16,16,1024]{2,1,0:T(8,128)(2,1)S(1)} all-to-all(bf16[16,16,1024]{2,1,0:T(8,128)(2,1)S(1)} %bitcast.25), channel_id=1, replica_groups=mesh['xh'=2,'core'=2,'xl'=2,'yh'=2,'yl'=2,'z'=4] {'xh','xl','yh','yl'}, dimensions={0} | all-to-all | bytes 1048576 | tf_op jit(solution)/shard_map/all_to_all | solution.py:388
  64.1 0.8 norm.1
  64.9 2.1 %collective-permute-start.12 = (bf16[16,4096]{1,0:T(8,128)(2,1)S(1)}, bf16[16,4096]{1,0:T(8,128)(2,1)S(1)}, u32[]{:S(2)}, u32[]{:S(2)}) collective-permute-start(bf16[16,4096]{1,0:T(8,128)(2,1)S(1)} %get-tuple-element.35.own_ref), channel_id=1, source_target_pairs={{0,32},{32,0},{1,33},{33,1},{2,34},{34,2},{3,35},{35,3},{4,36},{36... | collective-permute-start | bytes 393224 | tf_op jit(solution)/shard_map/ppermute | solution.py:310
  67.0 1.0 collective-permute-done.12.other_ref
  68.0 0.4 collective-permute-start.13
  68.3 0.1 collective-permute-start.14
  68.5 0.4 collective-permute-start.15
  68.8 0.7 place.1
  69.5 54.7 %all_to_all.21 = bf16[64,8,4096]{2,1,0:T(8,128)(2,1)S(1)} all-to-all(bf16[64,8,4096]{2,1,0:T(8,128)(2,1)S(1)} %bitcast.23), channel_id=1, replica_groups=mesh['xh'=2,'core'=2,'xl'=2,'yh'=2,'yl'=2,'z'=4] {'xh','xl','yh','yl','z'}, dimensions={0} | all-to-all | bytes 8388608 | tf_op jit(solution)/shard_map/all_to_all | solution.py:397
  124.3 10.6 %expert.1 = bf16[512,4096]{1,0:T(8,128)(2,1)S(1)} custom-call(s32[1]{0:T(128)} %bitcast.2.core_ref, bf16[512,4096]{1,0:T(8,128)(2,1)S(1)} %bitcast.21, bf16[2,4096,384]{2,1,0:T(8,128)(2,1)} %gate_a, bf16[2,4096,384]{2,1,0:T(8,128)(2,1)} %up_a, bf16[2,384,4096]{2,1,0:T(8,128)(2,1)} %down_a, bf16[2,4096,384]{2,1,0:T(8,128)(2,1)S(1)} %collective-permute-done.13.gate_b, ...), custom_call_target="tpu_custom_call" | custom-call | flops 9663676416 | bytes 27262976 | tf_op jit(solution)/shard_map/expert/pallas_call | solution.py:175
  134.9 57.5 %all_to_all.22 = bf16[64,8,4096]{2,1,0:T(8,128)(2,1)S(1)} all-to-all(bf16[64,8,4096]{2,1,0:T(8,128)(2,1)S(1)} %bitcast.22), channel_id=1, replica_groups=mesh['xh'=2,'core'=2,'xl'=2,'yh'=2,'yl'=2,'z'=4] {'xh','xl','yh','yl','z'}, dimensions={0} | all-to-all | bytes 8388608 | tf_op jit(solution)/shard_map/all_to_all | solution.py:410
  192.4 0.8 fusion
  193.3 3.2 %collective-permute-start.16 = (bf16[16,4096]{1,0:T(8,128)(2,1)S(1)}, bf16[16,4096]{1,0:T(8,128)(2,1)S(1)}, u32[]{:S(2)}, u32[]{:S(2)}) collective-permute-start(bf16[16,4096]{1,0:T(8,128)(2,1)S(1)} %slice.39), channel_id=1, source_target_pairs={{0,32},{32,0},{1,33},{33,1},{2,34},{34,2},{3,35},{35,3},{4,36},{36... | collective-permute-start | bytes 393224 | tf_op jit(solution)/shard_map/ppermute | solution.py:310
  196.5 1.0 collective-permute-done.16
  197.5 0.7 fusion.2
  (45 shorter events, 0.6 us)
Async XLA Ops:
  0.6 1.6 copy-start
  0.6 15.4 %copy-start.5 = (f32[16,8]{0,1:T(8,128)S(1)}, f32[16,8]{0,1:T(8,128)}, u32[]{:S(2)}) copy-start(f32[16,8]{0,1:T(8,128)} %param.19) | copy-start | bytes 1540
  0.7 9.4 %copy-start.6 = (s32[16,8]{0,1:T(8,128)S(1)}, s32[16,8]{0,1:T(8,128)}, u32[]{:S(2)}) copy-start(s32[16,8]{0,1:T(8,128)} %param.18) | copy-start | bytes 1540
  2.3 7.8 %collective-permute-start = (bf16[1024,128]{1,0:T(8,128)(2,1)S(1)}, bf16[1024,128]{1,0:T(8,128)(2,1)S(1)}, u32[]{:S(2)}, u32[]{:S(2)}) collective-permute-start(bf16[1024,128]{1,0:T(8,128)(2,1)S(1)} %constant_dynamic-slice_fusion), channel_id=1, source_target_pairs={{0,4},{4,0},{1,5},{5,1},{2,6},{6,2},{3,7},{7,3},{8,12},{12,8},{9,1... | collective-permute-start | bytes 786440 | tf_op jit(solution)/shard_map/ppermute | solution.py:356
  10.3 13.8 %collective-permute-start.3 = (s32[16,8]{1,0:T(8,128)S(1)}, s32[16,8]{1,0:T(8,128)S(1)}, u32[]{:S(2)}, u32[]{:S(2)}) collective-permute-start(s32[16,8]{1,0:T(8,128)S(1)} %copy.46), channel_id=1, source_target_pairs={{0,32},{32,0},{1,33},{33,1},{2,34},{34,2},{3,35},{35,3},{4,36},{36... | collective-permute-start | bytes 1544 | tf_op jit(solution)/shard_map/ppermute | solution.py:310
  12.0 18.5 %collective-permute-start.2 = (bf16[2,1024,128]{2,1,0:T(8,128)(2,1)S(1)}, bf16[2,1024,128]{2,1,0:T(8,128)(2,1)S(1)}, u32[]{:S(2)}, u32[]{:S(2)}) collective-permute-start(bf16[2,1024,128]{2,1,0:T(8,128)(2,1)S(1)} %pad_maximum_fusion.refs_0_), channel_id=1, source_target_pairs={{0,3},{1,0},{2,1},{3,2},{4,7},{5,4},{6,5},{7,6},{8,11},{9,8},{10,9... | collective-permute-start | bytes 1572872 | tf_op jit(solution)/shard_map/ppermute | solution.py:363
  16.0 14.4 %collective-permute-start.1 = (bf16[2,1024,128]{2,1,0:T(8,128)(2,1)S(1)}, bf16[2,1024,128]{2,1,0:T(8,128)(2,1)S(1)}, u32[]{:S(2)}, u32[]{:S(2)}) collective-permute-start(bf16[2,1024,128]{2,1,0:T(8,128)(2,1)S(1)} %pad_maximum_fusion.refs_0_), channel_id=1, source_target_pairs={{0,1},{1,2},{2,3},{3,0},{4,5},{5,6},{6,7},{7,4},{8,9},{9,10},{10,1... | collective-permute-start | bytes 1572872 | tf_op jit(solution)/shard_map/ppermute | solution.py:362
  16.1 25.5 %all-to-all-start = ((bf16[16,16,2048]{2,1,0:T(8,128)(2,1)}), bf16[16,16,2048]{2,1,0:T(8,128)(2,1)S(1)}, u32[]{:S(2)}, u32[]{:S(2)}) async-start(bf16[16,16,2048]{2,1,0:T(8,128)(2,1)} %attend.1), calls=%async_computation | async-start | bytes 2097152 | tf_op jit(solution)/shard_map/all_to_all | solution.py:386
  22.8 2.1 %collective-permute-start.4 = (f32[16,8]{0,1:T(8,128)S(1)}, f32[16,8]{0,1:T(8,128)S(1)}, u32[]{:S(2)}, u32[]{:S(2)}) collective-permute-start(f32[16,8]{0,1:T(8,128)S(1)} %broadcast_divide_fusion), channel_id=1, source_target_pairs={{0,32},{32,0},{1,33},{33,1},{2,34},{34,2},{3,35},{35,3},{4,36},{36... | collective-permute-start | bytes 1544 | tf_op jit(solution)/shard_map/ppermute | solution.py:310
  24.7 39.4 %copy-start.3 = (f32[4096]{0:T(1024)S(1)}, f32[4096]{0:T(1024)}, u32[]{:S(2)}) copy-start(f32[4096]{0:T(1024)} %param.17) | copy-start | bytes 49156
  30.5 8.0 %collective-permute-start.5 = (bf16[1024,128]{1,0:T(8,128)(2,1)S(1)}, bf16[1024,128]{1,0:T(8,128)(2,1)S(1)}, u32[]{:S(2)}, u32[]{:S(2)}) collective-permute-start(bf16[1024,128]{1,0:T(8,128)(2,1)S(1)} %slice_bitcast_fusion.1), channel_id=1, source_target_pairs={{0,1},{1,2},{2,3},{3,0},{4,5},{5,6},{6,7},{7,4},{8,9},{9,10},{10,1... | collective-permute-start | bytes 786440 | tf_op jit(solution)/shard_map/ppermute | solution.py:382
  30.6 10.4 %collective-permute-start.6 = (bf16[1024,128]{1,0:T(8,128)(2,1)S(1)}, bf16[1024,128]{1,0:T(8,128)(2,1)}, u32[]{:S(2)}, u32[]{:S(2)}) collective-permute-start(bf16[1024,128]{1,0:T(8,128)(2,1)S(1)} %slice_bitcast_fusion), channel_id=1, source_target_pairs={{0,3},{1,0},{2,1},{3,2},{4,7},{5,4},{6,5},{7,6},{8,11},{9,8},{10,9... | collective-permute-start | bytes 786440 | tf_op jit(solution)/shard_map/ppermute | solution.py:382
  38.4 6.0 %collective-permute-start.7 = (bf16[2,1024,128]{2,1,0:T(8,128)(2,1)S(1)}, bf16[2,1024,128]{2,1,0:T(8,128)(2,1)S(1)}, u32[]{:S(2)}, u32[]{:S(2)}) collective-permute-start(bf16[2,1024,128]{2,1,0:T(8,128)(2,1)S(1)} %pad_maximum_fusion.refs_0_), channel_id=1, source_target_pairs={{0,32},{32,0},{1,33},{33,1},{2,34},{34,2},{3,35},{35,3},{4,36},{36... | collective-permute-start | bytes 1572872 | tf_op jit(solution)/shard_map/ppermute | solution.py:310
  40.5 3.9 %collective-permute-start.8 = (bf16[2,1024,128]{2,1,0:T(8,128)(2,1)S(1)}, bf16[2,1024,128]{2,1,0:T(8,128)(2,1)}, u32[]{:S(2)}, u32[]{:S(2)}) collective-permute-start(bf16[2,1024,128]{2,1,0:T(8,128)(2,1)S(1)} %collective-permute-done.1.refs_1_), channel_id=1, source_target_pairs={{0,32},{32,0},{1,33},{33,1},{2,34},{34,2},{3,35},{35,3},{4,36},{36... | collective-permute-start | bytes 1572872 | tf_op jit(solution)/shard_map/ppermute | solution.py:310
  40.5 3.9 %collective-permute-start.9 = (bf16[2,1024,128]{2,1,0:T(8,128)(2,1)S(1)}, bf16[2,1024,128]{2,1,0:T(8,128)(2,1)}, u32[]{:S(2)}, u32[]{:S(2)}) collective-permute-start(bf16[2,1024,128]{2,1,0:T(8,128)(2,1)S(1)} %collective-permute-done.2.refs_2_), channel_id=1, source_target_pairs={{0,32},{32,0},{1,33},{33,1},{2,34},{34,2},{3,35},{35,3},{4,36},{36... | collective-permute-start | bytes 1572872 | tf_op jit(solution)/shard_map/ppermute | solution.py:310
  41.0 2.8 %collective-permute-start.11 = (bf16[1024,128]{1,0:T(8,128)(2,1)}, bf16[1024,128]{1,0:T(8,128)(2,1)}, u32[]{:S(2)}, u32[]{:S(2)}) collective-permute-start(bf16[1024,128]{1,0:T(8,128)(2,1)} %collective-permute-done.6.refs_4_), channel_id=1, source_target_pairs={{0,32},{32,0},{1,33},{33,1},{2,34},{34,2},{3,35},{35,3},{4,36},{36... | collective-permute-start | bytes 786440 | tf_op jit(solution)/shard_map/ppermute | solution.py:310
  41.0 3.4 %collective-permute-start.10 = (bf16[1024,128]{1,0:T(8,128)(2,1)S(1)}, bf16[1024,128]{1,0:T(8,128)(2,1)}, u32[]{:S(2)}, u32[]{:S(2)}) collective-permute-start(bf16[1024,128]{1,0:T(8,128)(2,1)S(1)} %collective-permute-done.5.refs_3_), channel_id=1, source_target_pairs={{0,32},{32,0},{1,33},{33,1},{2,34},{34,2},{3,35},{35,3},{4,36},{36... | collective-permute-start | bytes 786440 | tf_op jit(solution)/shard_map/ppermute | solution.py:310
  41.6 22.5 %copy-start.2 = (bf16[16,4096]{1,0:T(8,128)(2,1)S(1)}, bf16[16,4096]{1,0:T(8,128)(2,1)}, u32[]{:S(2)}) copy-start(bf16[16,4096]{1,0:T(8,128)(2,1)} %residual_ref.1) | copy-start | bytes 393220
  64.9 3.1 %collective-permute-start.12 = (bf16[16,4096]{1,0:T(8,128)(2,1)S(1)}, bf16[16,4096]{1,0:T(8,128)(2,1)S(1)}, u32[]{:S(2)}, u32[]{:S(2)}) collective-permute-start(bf16[16,4096]{1,0:T(8,128)(2,1)S(1)} %get-tuple-element.35.own_ref), channel_id=1, source_target_pairs={{0,32},{32,0},{1,33},{33,1},{2,34},{34,2},{3,35},{35,3},{4,36},{36... | collective-permute-start | bytes 393224 | tf_op jit(solution)/shard_map/ppermute | solution.py:310
  68.0 56.3 %collective-permute-start.13 = (bf16[2,4096,384]{2,1,0:T(8,128)(2,1)}, bf16[2,4096,384]{2,1,0:T(8,128)(2,1)S(1)}, u32[]{:S(2)}, u32[]{:S(2)}) collective-permute-start(bf16[2,4096,384]{2,1,0:T(8,128)(2,1)} %gate_a), channel_id=1, source_target_pairs={{0,32},{32,0},{1,33},{33,1},{2,34},{34,2},{3,35},{35,3},{4,36},{36... | collective-permute-start | bytes 18874376 | tf_op jit(solution)/shard_map/ppermute | solution.py:310
  68.3 55.9 %collective-permute-start.14 = (bf16[2,4096,384]{2,1,0:T(8,128)(2,1)}, bf16[2,4096,384]{2,1,0:T(8,128)(2,1)S(1)}, u32[]{:S(2)}, u32[]{:S(2)}) collective-permute-start(bf16[2,4096,384]{2,1,0:T(8,128)(2,1)} %up_a), channel_id=1, source_target_pairs={{0,32},{32,0},{1,33},{33,1},{2,34},{34,2},{3,35},{35,3},{4,36},{36... | collective-permute-start | bytes 18874376 | tf_op jit(solution)/shard_map/ppermute | solution.py:310
  68.5 55.8 %collective-permute-start.15 = (bf16[2,384,4096]{2,1,0:T(8,128)(2,1)}, bf16[2,384,4096]{2,1,0:T(8,128)(2,1)S(1)}, u32[]{:S(2)}, u32[]{:S(2)}) collective-permute-start(bf16[2,384,4096]{2,1,0:T(8,128)(2,1)} %down_a), channel_id=1, source_target_pairs={{0,32},{32,0},{1,33},{33,1},{2,34},{34,2},{3,35},{35,3},{4,36},{36... | collective-permute-start | bytes 18874376 | tf_op jit(solution)/shard_map/ppermute | solution.py:310
  134.9 57.5 %copy-start.4 = (bf16[64,512]{1,0:T(8,128)(2,1)S(1)}, bf16[64,512]{1,0:T(8,128)(2,1)}, u32[]{:S(2)}) copy-start(bf16[64,512]{1,0:T(8,128)(2,1)} %pad_maximum_fusion.2) | copy-start | bytes 196612
  134.9 63.3 %copy-start.1 = (bf16[8192,128]{1,0:T(8,128)(2,1)S(1)}, bf16[8192,128]{1,0:T(8,128)(2,1)}, u32[]{:S(2)}) copy-start(bf16[8192,128]{1,0:T(8,128)(2,1)} %param.20) | copy-start | bytes 6291460
  193.3 4.2 %collective-permute-start.16 = (bf16[16,4096]{1,0:T(8,128)(2,1)S(1)}, bf16[16,4096]{1,0:T(8,128)(2,1)S(1)}, u32[]{:S(2)}, u32[]{:S(2)}) collective-permute-start(bf16[16,4096]{1,0:T(8,128)(2,1)S(1)} %slice.39), channel_id=1, source_target_pairs={{0,32},{32,0},{1,33},{33,1},{2,34},{34,2},{3,35},{35,3},{4,36},{36... | collective-permute-start | bytes 393224 | tf_op jit(solution)/shard_map/ppermute | solution.py:310

commit v6 on v5

--- a/solution.py
+++ b/solution.py
@@ -17,10 +17,11 @@
 DP = ("xh", "core")
 EP = ("xl", "yh", "yl", "z")
 PLANE = ("xh", "xl", "yh", "yl")
-CHIPS = ("xh",) + EP
+CHIPS = ("yh", "yl", "xl", "xh", "z")
 ALL = DP + EP
 SWAP = ((0, 1), (1, 0))
 MIB = 1 << 20
+RUN = 8 * SLOTS
 BLOCK = 128
 WIDE = 1024
 
@@ -286,8 +287,10 @@
     for start in range(0, count, step):
         value = jnp.dot(placing_ref[start : start + step, :], rows, preferred_element_type=jnp.float32)
         value = value.astype(out_ref.dtype)
-        for copy in range(2):
-            out_ref[copy * count + start : copy * count + start + step, :] = value
+        for part in range(0, step, RUN):
+            for copy in range(2):
+                at = 2 * (start + part) + copy * RUN
+                out_ref[at : at + RUN, :] = value[part : part + RUN, :]
 
 
 def run_place(placing, own, other):
@@ -318,7 +321,9 @@
     )
     ranking = jnp.sum((jnp.cumsum(member, 0) - 1) * member, 1)
     here = (pair_ids % 2) == core
-    slot = (pair_ids // 2) * (2 * SLOTS) + ranking
+    chip = pair_ids // 2
+    chip = (chip // 4 % 4 * 2 + chip // 16) * 4 + chip % 4
+    slot = chip * (2 * SLOTS) + ranking
     slot = jnp.where(here, slot, -1)
     return slot.reshape(row_count, TOP)
 
@@ -373,15 +378,16 @@
     placing = jnp.any(chosen, 1)
     mixing = jnp.sum(jnp.where(chosen, both_gates[:, :, None], 0.0), 1)
     placing = placing.astype(jnp.bfloat16).T
-    mixing = jnp.concatenate([mixing, mixing], 1)
+    mixing = mixing.reshape(2 * row_count, -1, 1, RUN)
+    mixing = jnp.concatenate([mixing, mixing], 2).reshape(2 * row_count, 2 * slot_total)
     mixing_high = mixing.astype(jnp.bfloat16)
     mixing_low = (mixing - mixing_high.astype(jnp.float32)).astype(jnp.bfloat16)
     mixing = jnp.concatenate([mixing_high, mixing_low], 0)
 
     passed, placing, mixing = lax.optimization_barrier((before[0], placing, mixing))
     weights = [own, before, after, lax.ppermute(passed, "z", forth), lax.ppermute(after[1], "z", back)]
-    given = lax.optimization_barrier(weights[:4])
-    weights += [swap(value) for value in given + weights[4:]]
+    first = lax.optimization_barrier(weights[:3])
+    weights += [swap(value) for value in first + weights[3:]]
     place = jnp.stack([pair, lax.axis_index("z"), core]).astype(jnp.int32)
     gathered = lax.all_to_all(sent, PLANE, split_axis=0, concat_axis=0, tiled=True)
     columns = run_project(place, gathered.reshape(plane * row_count, depth), weights)

time: 199 us -> 196 us (0.985)
  waiting for transfers between devices: 14.5 us -> 8.88 us
  starting transfers between devices: 27.4 us -> 30.3 us
    ppermute x1, waiting for transfers between devices: 4.43 us -> 0.01 us  [on_device(): before = lax.ppermute(own, 'z', forth)]
    ppermute x1, waiting for transfers between devices: 5.12 us -> 1.61 us  [on_device(): lax.ppermute(passed, 'z', forth)]
    ppermute x1, waiting for transfers between devices: 0.01 us -> 3.05 us  [on_device(): lax.ppermute(after[1], 'z', back)]
    ppermute x12, starting transfers between devices: 11.6 us -> 13.8 us  [swap(): return lax.ppermute(value, 'core', SWAP)]
  transfers between devices with their start and end apart: 18 -> 18, of which waited for: 7 -> 8; matrix products, arithmetic and copies ran while one was open for 1% -> 2% of each run, Pallas kernels for 3% -> 3%
where the time goes in v6:
time: 196 us; the launch traced here: 195 us
  blocking collectives  128 us (65%)
  starting transfers between devices  30.3 us (15%)
  Pallas kernels  20.1 us (10%)
  waiting for transfers between devices  8.88 us (5%)
  other arithmetic  3.15 us (2%)
  local copies, waits for them, and re-layouts  2.7 us (1%)
    all_to_all x1, blocking collectives, on_device(): lax.all_to_all(partial_value.reshape(chips, 2 * SLOTS, -1), CHIPS, split_...  56.3 us
    all_to_all x1, blocking collectives, on_device(): lax.all_to_all(outgoing.reshape(chips, 2 * SLOTS, -1), CHIPS, split_axis=...  55.1 us
    all_to_all x1, blocking collectives, on_device(): lax.all_to_all(columns.reshape(plane, row_count, -1), PLANE, split_axis=0...  16.9 us
    ppermute x12, starting transfers between devices, swap(): return lax.ppermute(value, 'core', SWAP)  13.8 us
    pallas_call x1, Pallas kernels, run_expert(): pl.pallas_call(expert_kernel, out_shape=pltpu.VMEM((count, depth), jnp.bf...  10.4 us
    all_to_all x1, starting transfers between devices, on_device(): lax.all_to_all(sent, PLANE, split_axis=0, concat_axis=0, tiled=True)  6.77 us
    pallas_call x1, Pallas kernels, run_attend(): pl.pallas_call(functools.partial(attend_kernel, parts=parts, copies=copie...  5.44 us
    ppermute x1, starting transfers between devices, on_device(): after = lax.ppermute(own, 'z', back)  3.99 us
  transfers between devices with their start and end apart: 18, of which 8 were waited for; matrix products, arithmetic and copies ran while one was open for 2% of the time, Pallas kernels for 3%

profile of v6, /device:TPU:1, one launch (start us, length us, event | category | flops | bytes accessed | tf_op | source)
XLA Modules:
  0.0 195.1 jit_solution(11765721191620893899)
XLA Ops:
  0.7 1.6 copy-done
  2.3 2.2 %collective-permute-start = (bf16[1024,128]{1,0:T(8,128)(2,1)S(1)}, bf16[1024,128]{1,0:T(8,128)(2,1)S(1)}, u32[]{:S(2)}, u32[]{:S(2)}) collective-permute-start(bf16[1024,128]{1,0:T(8,128)(2,1)S(1)} %constant_dynamic-slice_fusion), channel_id=1, source_target_pairs={{0,4},{4,0},{1,5},{5,1},{2,6},{6,2},{3,7},{7,3},{8,12},{12,8},{9,1... | collective-permute-start | bytes 786440 | tf_op jit(solution)/shard_map/ppermute | solution.py:361
  4.5 5.4 %attend.1 = bf16[16,16,2048]{2,1,0:T(8,128)(2,1)} custom-call(s32[16]{0:T(128)} %lengths_hbm.1, bf16[16,8192]{1,0:T(8,128)(2,1)} %queries_hbm.1, bf16[16,2,128,512]{3,2,1,0:T(8,128)(2,1)} %cache_hbm.1, bf16[16,2,512]{2,1,0:T(2,128)(2,1)} %fresh_hbm.1), custom_call_target="tpu_custom_call" | custom-call | flops 67108864 | bytes 5505024 | tf_op jit(solution)/shard_map/attend/pallas_call | solution.py:105
  10.0 0.1 collective-permute-done
  10.2 0.1 eq.64
  10.3 1.7 collective-permute-start.3
  12.0 4.0 %collective-permute-start.2 = (bf16[2,1024,128]{2,1,0:T(8,128)(2,1)S(1)}, bf16[2,1024,128]{2,1,0:T(8,128)(2,1)S(1)}, u32[]{:S(2)}, u32[]{:S(2)}) collective-permute-start(bf16[2,1024,128]{2,1,0:T(8,128)(2,1)S(1)} %pad_maximum_fusion.refs_0_), channel_id=1, source_target_pairs={{0,3},{1,0},{2,1},{3,2},{4,7},{5,4},{6,5},{7,6},{8,11},{9,8},{10,9... | collective-permute-start | bytes 1572872 | tf_op jit(solution)/shard_map/ppermute | solution.py:368
  16.1 6.8 %all-to-all-start = ((bf16[16,16,2048]{2,1,0:T(8,128)(2,1)}), bf16[16,16,2048]{2,1,0:T(8,128)(2,1)S(1)}, u32[]{:S(2)}, u32[]{:S(2)}) async-start(bf16[16,16,2048]{2,1,0:T(8,128)(2,1)} %attend.1), calls=%async_computation | async-start | bytes 2097152 | tf_op jit(solution)/shard_map/all_to_all | solution.py:392
  22.8 0.7 collective-permute-start.4
  23.6 0.2 reduce_window_sum.17
  23.7 0.2 select_reduce_fusion.2
  24.1 0.2 collective-permute-done.4
  24.5 0.1 eq.69
  24.6 0.1 fusion.4
  24.6 0.2 reduce_window_sum.18
  24.8 0.2 select_reduce_fusion.1
  25.2 0.2 fusion.3
  25.3 0.1 copy.54
  25.4 0.2 select_reduce_fusion
  25.7 0.3 pad_maximum_fusion.1
  26.0 0.3 reshape.45
  26.3 0.6 pad_maximum_fusion.2
  26.9 0.4 collective-permute-done.2.refs_2_
  27.4 3.5 %collective-permute-start.6 = (bf16[1024,128]{1,0:T(8,128)(2,1)S(1)}, bf16[1024,128]{1,0:T(8,128)(2,1)S(1)}, u32[]{:S(2)}, u32[]{:S(2)}) collective-permute-start(bf16[1024,128]{1,0:T(8,128)(2,1)S(1)} %slice_bitcast_fusion), channel_id=1, source_target_pairs={{0,3},{1,0},{2,1},{3,2},{4,7},{5,4},{6,5},{7,6},{8,11},{9,8},{10,9... | collective-permute-start | bytes 786440 | tf_op jit(solution)/shard_map/ppermute | solution.py:388
  31.0 1.2 collective-permute-start.7
  32.1 0.1 collective-permute-start.8
  32.2 0.4 collective-permute-start.9
  32.6 3.0 %collective-permute-done.6.refs_4_ = bf16[1024,128]{1,0:T(8,128)(2,1)S(1)} collective-permute-done((bf16[1024,128]{1,0:T(8,128)(2,1)S(1)}, bf16[1024,128]{1,0:T(8,128)(2,1)S(1)}, u32[]{:S(2)}, u32[]{:S(2)}) %collective-permute-start.6) | collective-permute-done | bytes 262176 | tf_op jit(solution)/shard_map/ppermute | solution.py:388
  35.7 1.7 collective-permute-start.11
  37.4 1.6 collective-permute-done.5.refs_3_
  39.0 2.0 %collective-permute-start.10 = (bf16[1024,128]{1,0:T(8,128)(2,1)}, bf16[1024,128]{1,0:T(8,128)(2,1)}, u32[]{:S(2)}, u32[]{:S(2)}) collective-permute-start(bf16[1024,128]{1,0:T(8,128)(2,1)} %collective-permute-done.5.refs_3_), channel_id=1, source_target_pairs={{0,32},{32,0},{1,33},{33,1},{2,34},{34,2},{3,35},{35,3},{4,36},{36... | collective-permute-start | bytes 786440 | tf_op jit(solution)/shard_map/ppermute | solution.py:313
  41.1 1.4 collective-permute-done.10.refs_8_
  42.5 2.8 %project.1 = bf16[256,1024]{1,0:T(8,128)(2,1)S(1)} custom-call(s32[3]{0:T(128)S(1)} %pad_add_fusion.1.place_ref, bf16[256,2048]{1,0:T(8,128)(2,1)S(1)} %bitcast.26, bf16[2,1024,128]{2,1,0:T(8,128)(2,1)S(1)} %pad_maximum_fusion.refs_0_, bf16[2,1024,128]{2,1,0:T(8,128)(2,1)S(1)} %collective-permute-done.1.refs_1_, ...), custom_call_target="tpu_custom_call" | custom-call | flops 1073741824 | bytes 5767168 | tf_op jit(solution)/shard_map/project/pallas_call | solution.py:228
  45.3 16.9 %all_to_all.20.terms_ref = bf16[16,16,1024]{2,1,0:T(8,128)(2,1)S(1)} all-to-all(bf16[16,16,1024]{2,1,0:T(8,128)(2,1)S(1)} %bitcast.27), channel_id=1, replica_groups=mesh['xh'=2,'core'=2,'xl'=2,'yh'=2,'yl'=2,'z'=4] {'xh','xl','yh','yl'}, dimensions={0} | all-to-all | bytes 1048576 | tf_op jit(solution)/shard_map/all_to_all | solution.py:394
  62.2 0.8 norm.1
  63.0 2.1 %collective-permute-start.12 = (bf16[16,4096]{1,0:T(8,128)(2,1)S(1)}, bf16[16,4096]{1,0:T(8,128)(2,1)S(1)}, u32[]{:S(2)}, u32[]{:S(2)}) collective-permute-start(bf16[16,4096]{1,0:T(8,128)(2,1)S(1)} %get-tuple-element.33.own_ref), channel_id=1, source_target_pairs={{0,32},{32,0},{1,33},{33,1},{2,34},{34,2},{3,35},{35,3},{4,36},{36... | collective-permute-start | bytes 393224 | tf_op jit(solution)/shard_map/ppermute | solution.py:313
  65.1 1.0 collective-permute-done.12.other_ref
  66.1 0.4 collective-permute-start.13
  66.4 0.1 collective-permute-start.14
  66.6 0.4 collective-permute-start.15
  66.9 0.7 place.1
  67.6 55.1 %all_to_all.21 = bf16[64,8,4096]{2,1,0:T(8,128)(2,1)S(1)} all-to-all(bf16[64,8,4096]{2,1,0:T(8,128)(2,1)S(1)} %bitcast.25), channel_id=1, replica_groups=mesh['xh'=2,'core'=2,'xl'=2,'yh'=2,'yl'=2,'z'=4] {'yh','yl','xl','xh','z'}, dimensions={0} | all-to-all | bytes 8388608 | tf_op jit(solution)/shard_map/all_to_all | solution.py:403
  122.8 10.4 %expert.1 = bf16[512,4096]{1,0:T(8,128)(2,1)S(1)} custom-call(s32[1]{0:T(128)} %bitcast.2.core_ref, bf16[512,4096]{1,0:T(8,128)(2,1)S(1)} %bitcast.23, bf16[2,4096,384]{2,1,0:T(8,128)(2,1)} %gate_a, bf16[2,4096,384]{2,1,0:T(8,128)(2,1)} %up_a, bf16[2,384,4096]{2,1,0:T(8,128)(2,1)} %down_a, bf16[2,4096,384]{2,1,0:T(8,128)(2,1)S(1)} %collective-permute-done.13.gate_b, ...), custom_call_target="tpu_custom_call" | custom-call | flops 9663676416 | bytes 27262976 | tf_op jit(solution)/shard_map/expert/pallas_call | solution.py:176
  133.2 56.3 %all_to_all.22 = bf16[64,8,4096]{2,1,0:T(8,128)(2,1)S(1)} all-to-all(bf16[64,8,4096]{2,1,0:T(8,128)(2,1)S(1)} %bitcast.24), channel_id=1, replica_groups=mesh['xh'=2,'core'=2,'xl'=2,'yh'=2,'yl'=2,'z'=4] {'yh','yl','xl','xh','z'}, dimensions={0} | all-to-all | bytes 8388608 | tf_op jit(solution)/shard_map/all_to_all | solution.py:416
  189.5 0.8 fusion
  190.4 3.1 %collective-permute-start.16 = (bf16[16,4096]{1,0:T(8,128)(2,1)S(1)}, bf16[16,4096]{1,0:T(8,128)(2,1)S(1)}, u32[]{:S(2)}, u32[]{:S(2)}) collective-permute-start(bf16[16,4096]{1,0:T(8,128)(2,1)S(1)} %slice.39), channel_id=1, source_target_pairs={{0,32},{32,0},{1,33},{33,1},{2,34},{34,2},{3,35},{35,3},{4,36},{36... | collective-permute-start | bytes 393224 | tf_op jit(solution)/shard_map/ppermute | solution.py:313
  193.5 1.0 collective-permute-done.16
  194.5 0.7 fusion.2
  (47 shorter events, 1.1 us)
Async XLA Ops:
  0.6 1.6 copy-start
  0.6 15.4 %copy-start.5 = (f32[16,8]{0,1:T(8,128)S(1)}, f32[16,8]{0,1:T(8,128)}, u32[]{:S(2)}) copy-start(f32[16,8]{0,1:T(8,128)} %param.19) | copy-start | bytes 1540
  0.7 9.4 %copy-start.6 = (s32[16,8]{0,1:T(8,128)S(1)}, s32[16,8]{0,1:T(8,128)}, u32[]{:S(2)}) copy-start(s32[16,8]{0,1:T(8,128)} %param.18) | copy-start | bytes 1540
  2.3 7.8 %collective-permute-start = (bf16[1024,128]{1,0:T(8,128)(2,1)S(1)}, bf16[1024,128]{1,0:T(8,128)(2,1)S(1)}, u32[]{:S(2)}, u32[]{:S(2)}) collective-permute-start(bf16[1024,128]{1,0:T(8,128)(2,1)S(1)} %constant_dynamic-slice_fusion), channel_id=1, source_target_pairs={{0,4},{4,0},{1,5},{5,1},{2,6},{6,2},{3,7},{7,3},{8,12},{12,8},{9,1... | collective-permute-start | bytes 786440 | tf_op jit(solution)/shard_map/ppermute | solution.py:361
  10.3 14.2 %collective-permute-start.3 = (s32[16,8]{1,0:T(8,128)S(1)}, s32[16,8]{1,0:T(8,128)S(1)}, u32[]{:S(2)}, u32[]{:S(2)}) collective-permute-start(s32[16,8]{1,0:T(8,128)S(1)} %copy.48), channel_id=1, source_target_pairs={{0,32},{32,0},{1,33},{33,1},{2,34},{34,2},{3,35},{35,3},{4,36},{36... | collective-permute-start | bytes 1544 | tf_op jit(solution)/shard_map/ppermute | solution.py:313
  12.0 15.3 %collective-permute-start.2 = (bf16[2,1024,128]{2,1,0:T(8,128)(2,1)S(1)}, bf16[2,1024,128]{2,1,0:T(8,128)(2,1)S(1)}, u32[]{:S(2)}, u32[]{:S(2)}) collective-permute-start(bf16[2,1024,128]{2,1,0:T(8,128)(2,1)S(1)} %pad_maximum_fusion.refs_0_), channel_id=1, source_target_pairs={{0,3},{1,0},{2,1},{3,2},{4,7},{5,4},{6,5},{7,6},{8,11},{9,8},{10,9... | collective-permute-start | bytes 1572872 | tf_op jit(solution)/shard_map/ppermute | solution.py:368
  16.0 14.8 %collective-permute-start.1 = (bf16[2,1024,128]{2,1,0:T(8,128)(2,1)S(1)}, bf16[2,1024,128]{2,1,0:T(8,128)(2,1)S(1)}, u32[]{:S(2)}, u32[]{:S(2)}) collective-permute-start(bf16[2,1024,128]{2,1,0:T(8,128)(2,1)S(1)} %pad_maximum_fusion.refs_0_), channel_id=1, source_target_pairs={{0,1},{1,2},{2,3},{3,0},{4,5},{5,6},{6,7},{7,4},{8,9},{9,10},{10,1... | collective-permute-start | bytes 1572872 | tf_op jit(solution)/shard_map/ppermute | solution.py:367
  16.1 25.0 %all-to-all-start = ((bf16[16,16,2048]{2,1,0:T(8,128)(2,1)}), bf16[16,16,2048]{2,1,0:T(8,128)(2,1)S(1)}, u32[]{:S(2)}, u32[]{:S(2)}) async-start(bf16[16,16,2048]{2,1,0:T(8,128)(2,1)} %attend.1), calls=%async_computation | async-start | bytes 2097152 | tf_op jit(solution)/shard_map/all_to_all | solution.py:392
  22.8 1.5 collective-permute-start.4
  26.0 36.3 %copy-start.3 = (f32[4096]{0:T(1024)S(1)}, f32[4096]{0:T(1024)}, u32[]{:S(2)}) copy-start(f32[4096]{0:T(1024)} %param.17) | copy-start | bytes 49156
  27.4 8.3 %collective-permute-start.6 = (bf16[1024,128]{1,0:T(8,128)(2,1)S(1)}, bf16[1024,128]{1,0:T(8,128)(2,1)S(1)}, u32[]{:S(2)}, u32[]{:S(2)}) collective-permute-start(bf16[1024,128]{1,0:T(8,128)(2,1)S(1)} %slice_bitcast_fusion), channel_id=1, source_target_pairs={{0,3},{1,0},{2,1},{3,2},{4,7},{5,4},{6,5},{7,6},{8,11},{9,8},{10,9... | collective-permute-start | bytes 786440 | tf_op jit(solution)/shard_map/ppermute | solution.py:388
  30.9 8.1 %collective-permute-start.5 = (bf16[1024,128]{1,0:T(8,128)(2,1)S(1)}, bf16[1024,128]{1,0:T(8,128)(2,1)}, u32[]{:S(2)}, u32[]{:S(2)}) collective-permute-start(bf16[1024,128]{1,0:T(8,128)(2,1)S(1)} %slice_bitcast_fusion.1), channel_id=1, source_target_pairs={{0,1},{1,2},{2,3},{3,0},{4,5},{5,6},{6,7},{7,4},{8,9},{9,10},{10,1... | collective-permute-start | bytes 786440 | tf_op jit(solution)/shard_map/ppermute | solution.py:388
  31.0 11.5 %collective-permute-start.7 = (bf16[2,1024,128]{2,1,0:T(8,128)(2,1)S(1)}, bf16[2,1024,128]{2,1,0:T(8,128)(2,1)S(1)}, u32[]{:S(2)}, u32[]{:S(2)}) collective-permute-start(bf16[2,1024,128]{2,1,0:T(8,128)(2,1)S(1)} %pad_maximum_fusion.refs_0_), channel_id=1, source_target_pairs={{0,32},{32,0},{1,33},{33,1},{2,34},{34,2},{3,35},{35,3},{4,36},{36... | collective-permute-start | bytes 1572872 | tf_op jit(solution)/shard_map/ppermute | solution.py:313
  32.1 10.4 %collective-permute-start.8 = (bf16[2,1024,128]{2,1,0:T(8,128)(2,1)S(1)}, bf16[2,1024,128]{2,1,0:T(8,128)(2,1)}, u32[]{:S(2)}, u32[]{:S(2)}) collective-permute-start(bf16[2,1024,128]{2,1,0:T(8,128)(2,1)S(1)} %collective-permute-done.1.refs_1_), channel_id=1, source_target_pairs={{0,32},{32,0},{1,33},{33,1},{2,34},{34,2},{3,35},{35,3},{4,36},{36... | collective-permute-start | bytes 1572872 | tf_op jit(solution)/shard_map/ppermute | solution.py:313
  32.2 10.3 %collective-permute-start.9 = (bf16[2,1024,128]{2,1,0:T(8,128)(2,1)S(1)}, bf16[2,1024,128]{2,1,0:T(8,128)(2,1)}, u32[]{:S(2)}, u32[]{:S(2)}) collective-permute-start(bf16[2,1024,128]{2,1,0:T(8,128)(2,1)S(1)} %collective-permute-done.2.refs_2_), channel_id=1, source_target_pairs={{0,32},{32,0},{1,33},{33,1},{2,34},{34,2},{3,35},{35,3},{4,36},{36... | collective-permute-start | bytes 1572872 | tf_op jit(solution)/shard_map/ppermute | solution.py:313
  35.7 5.4 %collective-permute-start.11 = (bf16[1024,128]{1,0:T(8,128)(2,1)S(1)}, bf16[1024,128]{1,0:T(8,128)(2,1)}, u32[]{:S(2)}, u32[]{:S(2)}) collective-permute-start(bf16[1024,128]{1,0:T(8,128)(2,1)S(1)} %collective-permute-done.6.refs_4_), channel_id=1, source_target_pairs={{0,32},{32,0},{1,33},{33,1},{2,34},{34,2},{3,35},{35,3},{4,36},{36... | collective-permute-start | bytes 786440 | tf_op jit(solution)/shard_map/ppermute | solution.py:313
  39.0 3.5 %collective-permute-start.10 = (bf16[1024,128]{1,0:T(8,128)(2,1)}, bf16[1024,128]{1,0:T(8,128)(2,1)}, u32[]{:S(2)}, u32[]{:S(2)}) collective-permute-start(bf16[1024,128]{1,0:T(8,128)(2,1)} %collective-permute-done.5.refs_3_), channel_id=1, source_target_pairs={{0,32},{32,0},{1,33},{33,1},{2,34},{34,2},{3,35},{35,3},{4,36},{36... | collective-permute-start | bytes 786440 | tf_op jit(solution)/shard_map/ppermute | solution.py:313
  41.1 21.2 %copy-start.2 = (bf16[16,4096]{1,0:T(8,128)(2,1)S(1)}, bf16[16,4096]{1,0:T(8,128)(2,1)}, u32[]{:S(2)}) copy-start(bf16[16,4096]{1,0:T(8,128)(2,1)} %residual_ref.1) | copy-start | bytes 393220
  63.0 3.1 %collective-permute-start.12 = (bf16[16,4096]{1,0:T(8,128)(2,1)S(1)}, bf16[16,4096]{1,0:T(8,128)(2,1)S(1)}, u32[]{:S(2)}, u32[]{:S(2)}) collective-permute-start(bf16[16,4096]{1,0:T(8,128)(2,1)S(1)} %get-tuple-element.33.own_ref), channel_id=1, source_target_pairs={{0,32},{32,0},{1,33},{33,1},{2,34},{34,2},{3,35},{35,3},{4,36},{36... | collective-permute-start | bytes 393224 | tf_op jit(solution)/shard_map/ppermute | solution.py:313
  66.1 56.7 %collective-permute-start.13 = (bf16[2,4096,384]{2,1,0:T(8,128)(2,1)}, bf16[2,4096,384]{2,1,0:T(8,128)(2,1)S(1)}, u32[]{:S(2)}, u32[]{:S(2)}) collective-permute-start(bf16[2,4096,384]{2,1,0:T(8,128)(2,1)} %gate_a), channel_id=1, source_target_pairs={{0,32},{32,0},{1,33},{33,1},{2,34},{34,2},{3,35},{35,3},{4,36},{36... | collective-permute-start | bytes 18874376 | tf_op jit(solution)/shard_map/ppermute | solution.py:313
  66.4 56.3 %collective-permute-start.14 = (bf16[2,4096,384]{2,1,0:T(8,128)(2,1)}, bf16[2,4096,384]{2,1,0:T(8,128)(2,1)S(1)}, u32[]{:S(2)}, u32[]{:S(2)}) collective-permute-start(bf16[2,4096,384]{2,1,0:T(8,128)(2,1)} %up_a), channel_id=1, source_target_pairs={{0,32},{32,0},{1,33},{33,1},{2,34},{34,2},{3,35},{35,3},{4,36},{36... | collective-permute-start | bytes 18874376 | tf_op jit(solution)/shard_map/ppermute | solution.py:313
  66.6 56.2 %collective-permute-start.15 = (bf16[2,384,4096]{2,1,0:T(8,128)(2,1)}, bf16[2,384,4096]{2,1,0:T(8,128)(2,1)S(1)}, u32[]{:S(2)}, u32[]{:S(2)}) collective-permute-start(bf16[2,384,4096]{2,1,0:T(8,128)(2,1)} %down_a), channel_id=1, source_target_pairs={{0,32},{32,0},{1,33},{33,1},{2,34},{34,2},{3,35},{35,3},{4,36},{36... | collective-permute-start | bytes 18874376 | tf_op jit(solution)/shard_map/ppermute | solution.py:313
  133.2 56.3 %copy-start.4 = (bf16[64,512]{1,0:T(8,128)(2,1)S(1)}, bf16[64,512]{1,0:T(8,128)(2,1)}, u32[]{:S(2)}) copy-start(bf16[64,512]{1,0:T(8,128)(2,1)} %pad_maximum_fusion.2) | copy-start | bytes 196612
  133.2 61.9 %copy-start.1 = (bf16[8192,128]{1,0:T(8,128)(2,1)S(1)}, bf16[8192,128]{1,0:T(8,128)(2,1)}, u32[]{:S(2)}) copy-start(bf16[8192,128]{1,0:T(8,128)(2,1)} %param.20) | copy-start | bytes 6291460
  190.4 4.0 %collective-permute-start.16 = (bf16[16,4096]{1,0:T(8,128)(2,1)S(1)}, bf16[16,4096]{1,0:T(8,128)(2,1)S(1)}, u32[]{:S(2)}, u32[]{:S(2)}) collective-permute-start(bf16[16,4096]{1,0:T(8,128)(2,1)S(1)} %slice.39), channel_id=1, source_target_pairs={{0,32},{32,0},{1,33},{33,1},{2,34},{34,2},{3,35},{35,3},{4,36},{36... | collective-permute-start | bytes 393224 | tf_op jit(solution)/shard_map/ppermute | solution.py:313

commit v7 on v6

--- a/solution.py
+++ b/solution.py
@@ -73,7 +73,7 @@
             axis=0,
         )
         keys = [
-            jnp.broadcast_to(fresh_ref[row, 0:1, cols].astype(jnp.float32), (groups, HD)) for row, kv, cols, own in blocks
+            jnp.broadcast_to(fresh_ref[row, 0:1, cols], (groups, HD)) for row, kv, cols, own in blocks
         ]
         fresh = jnp.sum(query * jnp.concatenate(keys, axis=0), axis=1, keepdims=True) * scaling
         live = jnp.concatenate([position < lengths_ref[row] for row in those], axis=0)
@@ -86,7 +86,7 @@
         fresh = (fresh / denominator).astype(jnp.bfloat16).astype(jnp.float32)
         mixed = [
             jnp.dot(weights[own], cache[row, 1, :, cols], preferred_element_type=jnp.float32)
-            + fresh[own] * fresh_ref[row, 1:2, cols].astype(jnp.float32)
+            + fresh[own] * fresh_ref[row, 1:2, cols]
             for row, kv, cols, own in blocks
         ]
         heads[at, :] = jnp.concatenate(mixed, axis=0)
@@ -101,7 +101,7 @@
 def run_attend(queries, kv_cache, kv_new, lengths, parts, copies):
     rows = queries.shape[0]
     hbm = pl.BlockSpec(memory_space=pltpu.HBM)
-    operands = [pltpu.with_memory_space_constraint(value, pltpu.HBM) for value in (lengths, queries, kv_cache, kv_new)]
+    operands = [pltpu.with_memory_space_constraint(value, pltpu.HBM) for value in (lengths, queries, kv_cache, kv_new.astype(jnp.float32))]
     return pl.pallas_call(
         functools.partial(attend_kernel, parts=parts, copies=copies),
         out_shape=pltpu.HBM((copies * parts, rows, HEADS * HD // parts), jnp.bfloat16),
@@ -111,7 +111,7 @@
             pltpu.SMEM(lengths.shape, jnp.int32),
             pltpu.VMEM(queries.shape, jnp.bfloat16),
             pltpu.VMEM(kv_cache.shape, jnp.bfloat16),
-            pltpu.VMEM(kv_new.shape, jnp.bfloat16),
+            pltpu.VMEM(kv_new.shape, jnp.float32),
             pltpu.VMEM((rows * HEADS, HD), jnp.float32),
             pltpu.SemaphoreType.DMA((7,)),
         ],
@@ -195,49 +195,53 @@
     )(core, rows, gate_a, up_a, down_a, gate_b, up_b, down_b)
 
 
-def project_kernel(place_ref, rows_ref, *refs):
+def project_kernel(place_ref, rows_ref, *refs, other):
     *weights, out_ref = refs
-    kinds = len(weights) // 2
-    half, width = weights[0].shape[1:]
-    ring = kinds - 1
+    sums_ref = weights.pop() if other else None
+    own, before, after, first, second = weights
+    half, width = own.shape[1:]
+    pairs = ((own, own), (before, before), (first, second), (after, after))
+    ring = len(pairs)
     pair, turn, core = place_ref[0], place_ref[1], place_ref[2]
-    near = rows_ref[:, pl.ds(pl.multiple_of(core * half, half), half)]
-    far = rows_ref[:, pl.ds(pl.multiple_of((1 - core) * half, half), half)]
-    for step in range(ring):
-        total = None
-        for rows, (own, before, after, first, second) in ((near, weights[:kinds]), (far, weights[kinds:])):
-            if step == 2:
-                both = jnp.concatenate([first[...], second[...]], axis=1)
-            else:
-                weight = {0: own, 1: before, 3: after}[step]
-                both = jnp.concatenate([weight[0], weight[1]], axis=1)
-            term = jnp.dot(rows, both, preferred_element_type=jnp.float32)
-            total = term if total is None else total + term
-        total = total.astype(out_ref.dtype)
+    side = 1 - core if other else core
+    rows = rows_ref[:, pl.ds(pl.multiple_of(side * half, half), half)]
+    for step, (left, right) in enumerate(pairs):
+        if left is right:
+            both = jnp.concatenate([left[0], right[1]], axis=1)
+        else:
+            both = jnp.concatenate([left[...], right[...]], axis=1)
+        total = jnp.dot(rows, both, preferred_element_type=jnp.float32)
+        cols = slice(2 * step * width, 2 * (step + 1) * width)
+        if not other:
+            out_ref[:, cols] = total
+            continue
+        total = (total + sums_ref[:, cols]).astype(out_ref.dtype)
         for which in range(2):
             owner = (pair + which) % 2 * ring + (turn + ring - step) % ring
-            cols = pl.ds(pl.multiple_of(owner * width, width), width)
-            out_ref[:, cols] = total[:, which * width : (which + 1) * width]
-
-
-def run_project(place, rows, weights):
+            at = pl.ds(pl.multiple_of(owner * width, width), width)
+            out_ref[:, at] = total[:, which * width : (which + 1) * width]
+
+
+def run_project(place, rows, weights, sums=None):
     count, depth = rows.shape
     width = 8 * weights[0].shape[2]
     vmem = pl.BlockSpec(memory_space=pltpu.VMEM)
-    weights = [pltpu.with_memory_space_constraint(value, pltpu.VMEM) for value in weights]
+    other = sums is not None
+    operands = [rows, *weights] + ([sums] if other else [])
+    operands = [pltpu.with_memory_space_constraint(value, pltpu.VMEM) for value in operands]
     return pl.pallas_call(
-        project_kernel,
-        out_shape=pltpu.VMEM((count, width), jnp.bfloat16),
-        in_specs=[pl.BlockSpec(memory_space=pltpu.SMEM)] + [vmem] * (1 + len(weights)),
+        functools.partial(project_kernel, other=other),
+        out_shape=pltpu.VMEM((count, width), jnp.bfloat16 if other else jnp.float32),
+        in_specs=[pl.BlockSpec(memory_space=pltpu.SMEM)] + [vmem] * len(operands),
         out_specs=vmem,
         compiler_params=pltpu.CompilerParams(vmem_limit_bytes=16 * MIB),
         cost_estimate=pl.CostEstimate(
-            flops=2 * count * depth * width,
-            bytes_accessed=2 * (count * depth + count * width + depth * width),
+            flops=count * depth * width,
+            bytes_accessed=count * depth + depth * width + 6 * count * width,
             transcendentals=0,
         ),
-        name="project",
-    )(place, rows, *weights)
+        name="project_other" if other else "project_own",
+    )(place, *operands)
 
 
 def norm_kernel(terms_ref, residual_ref, gain_ref, out_ref, normed_ref, *, parts):
@@ -387,10 +391,11 @@
     passed, placing, mixing = lax.optimization_barrier((before[0], placing, mixing))
     weights = [own, before, after, lax.ppermute(passed, "z", forth), lax.ppermute(after[1], "z", back)]
     first = lax.optimization_barrier(weights[:3])
-    weights += [swap(value) for value in first + weights[3:]]
+    others = [swap(value) for value in first + weights[3:]]
     place = jnp.stack([pair, lax.axis_index("z"), core]).astype(jnp.int32)
     gathered = lax.all_to_all(sent, PLANE, split_axis=0, concat_axis=0, tiled=True)
-    columns = run_project(place, gathered.reshape(plane * row_count, depth), weights)
+    gathered = gathered.reshape(plane * row_count, depth)
+    columns = run_project(place, gathered, others, run_project(place, gathered, weights))
     terms = lax.all_to_all(
         columns.reshape(plane, row_count, -1), PLANE, split_axis=0, concat_axis=0, tiled=True
     )

time: 196 us -> 196 us (level)
  transfers between devices with their start and end apart: 18 -> 18, of which waited for: 8 -> 6; matrix products, arithmetic and copies ran while one was open for 2% -> 2% of each run, Pallas kernels for 3% -> 4%
where the time goes in v7:
time: 196 us; the launch traced here: 195 us
  blocking collectives  128 us (65%)
  starting transfers between devices  29.5 us (15%)
  Pallas kernels  21.2 us (11%)
  waiting for transfers between devices  8.26 us (4%)
  other arithmetic  3.92 us (2%)
  local copies, waits for them, and re-layouts  2.69 us (1%)
    all_to_all x1, blocking collectives, on_device(): lax.all_to_all(partial_value.reshape(chips, 2 * SLOTS, -1), CHIPS, split_...  56.2 us
    all_to_all x1, blocking collectives, on_device(): lax.all_to_all(outgoing.reshape(chips, 2 * SLOTS, -1), CHIPS, split_axis=...  55.1 us
    all_to_all x1, blocking collectives, on_device(): lax.all_to_all(columns.reshape(plane, row_count, -1), PLANE, split_axis=0...  16.4 us
    ppermute x12, starting transfers between devices, swap(): return lax.ppermute(value, 'core', SWAP)  13.4 us
    pallas_call x1, Pallas kernels, run_expert(): pl.pallas_call(expert_kernel, out_shape=pltpu.VMEM((count, depth), jnp.bf...  10.4 us
    all_to_all x1, starting transfers between devices, on_device(): lax.all_to_all(sent, PLANE, split_axis=0, concat_axis=0, tiled=True)  6.47 us
    pallas_call x1, Pallas kernels, run_attend(): pl.pallas_call(functools.partial(attend_kernel, parts=parts, copies=copie...  5.44 us
  transfers between devices with their start and end apart: 18, of which 6 were waited for; matrix products, arithmetic and copies ran while one was open for 2% of the time, Pallas kernels for 4%

profile of v7, /device:TPU:1, one launch (start us, length us, event | category | flops | bytes accessed | tf_op | source)
XLA Modules:
  0.0 195.1 jit_solution(10521860063297870563)
XLA Ops:
  0.7 1.6 copy-done
  2.3 2.2 %collective-permute-start = (bf16[1024,128]{1,0:T(8,128)(2,1)S(1)}, bf16[1024,128]{1,0:T(8,128)(2,1)S(1)}, u32[]{:S(2)}, u32[]{:S(2)}) collective-permute-start(bf16[1024,128]{1,0:T(8,128)(2,1)S(1)} %constant_dynamic-slice_fusion), channel_id=1, source_target_pairs={{0,4},{4,0},{1,5},{5,1},{2,6},{6,2},{3,7},{7,3},{8,12},{12,8},{9,1... | collective-permute-start | bytes 786440 | tf_op jit(solution)/shard_map/ppermute | solution.py:365
  4.5 1.4 convert_element_type.32.fresh_hbm
  5.9 5.4 %attend.1 = bf16[16,16,2048]{2,1,0:T(8,128)(2,1)} custom-call(s32[16]{0:T(128)} %lengths_hbm.1, bf16[16,8192]{1,0:T(8,128)(2,1)} %queries_hbm.1, bf16[16,2,128,512]{3,2,1,0:T(8,128)(2,1)} %cache_hbm.1, f32[16,2,512]{2,1,0:T(2,128)} %convert_element_type.32.fresh_hbm), custom_call_target="tpu_custom_call" | custom-call | flops 67108864 | bytes 5505024 | tf_op jit(solution)/shard_map/attend/pallas_call | solution.py:105
  11.5 0.1 eq.64
  11.6 1.0 collective-permute-start.6
  12.6 3.8 %collective-permute-start.2 = (bf16[2,1024,128]{2,1,0:T(8,128)(2,1)S(1)}, bf16[2,1024,128]{2,1,0:T(8,128)(2,1)S(1)}, u32[]{:S(2)}, u32[]{:S(2)}) collective-permute-start(bf16[2,1024,128]{2,1,0:T(8,128)(2,1)S(1)} %pad_maximum_fusion.refs_0_), channel_id=1, source_target_pairs={{0,3},{1,0},{2,1},{3,2},{4,7},{5,4},{6,5},{7,6},{8,11},{9,8},{10,9... | collective-permute-start | bytes 1572872 | tf_op jit(solution)/shard_map/ppermute | solution.py:372
  16.5 6.5 %all-to-all-start = ((bf16[16,16,2048]{2,1,0:T(8,128)(2,1)}), bf16[16,16,2048]{2,1,0:T(8,128)(2,1)S(1)}, u32[]{:S(2)}, u32[]{:S(2)}) async-start(bf16[16,16,2048]{2,1,0:T(8,128)(2,1)} %attend.1), calls=%async_computation | async-start | bytes 2097152 | tf_op jit(solution)/shard_map/all_to_all | solution.py:396
  23.0 0.7 collective-permute-start.7
  23.7 0.2 reduce_window_sum.17
  23.9 0.2 select_reduce_fusion.2
  24.2 0.2 collective-permute-done.7
  24.6 0.1 eq.69
  24.7 0.1 fusion.4
  24.8 0.2 reduce_window_sum.18
  25.0 0.2 select_reduce_fusion.1
  25.3 0.2 select_reduce_fusion
  25.5 0.1 reshape.44
  25.6 0.3 pad_maximum_fusion.1
  25.8 0.3 reshape.45
  26.1 0.2 fusion.3
  26.3 0.1 copy.54
  26.5 1.3 collective-permute-done.2.refs_2_
  27.8 3.5 %collective-permute-start.10 = (bf16[1024,128]{1,0:T(8,128)(2,1)S(1)}, bf16[1024,128]{1,0:T(8,128)(2,1)S(1)}, u32[]{:S(2)}, u32[]{:S(2)}) collective-permute-start(bf16[1024,128]{1,0:T(8,128)(2,1)S(1)} %slice_bitcast_fusion), channel_id=1, source_target_pairs={{0,3},{1,0},{2,1},{3,2},{4,7},{5,4},{6,5},{7,6},{8,11},{9,8},{10,9... | collective-permute-start | bytes 786440 | tf_op jit(solution)/shard_map/ppermute | solution.py:392
  31.4 1.2 collective-permute-start.3
  32.6 0.1 collective-permute-start.4
  32.7 0.4 collective-permute-start.5
  33.1 3.0 %collective-permute-done.10.refs_4_ = bf16[1024,128]{1,0:T(8,128)(2,1)S(1)} collective-permute-done((bf16[1024,128]{1,0:T(8,128)(2,1)S(1)}, bf16[1024,128]{1,0:T(8,128)(2,1)S(1)}, u32[]{:S(2)}, u32[]{:S(2)}) %collective-permute-start.10) | collective-permute-done | bytes 262176 | tf_op jit(solution)/shard_map/ppermute | solution.py:392
  36.1 1.7 collective-permute-start.11
  37.8 1.6 collective-permute-done.8.refs_3_
  39.4 2.0 %collective-permute-start.9 = (bf16[1024,128]{1,0:T(8,128)(2,1)}, bf16[1024,128]{1,0:T(8,128)(2,1)}, u32[]{:S(2)}, u32[]{:S(2)}) collective-permute-start(bf16[1024,128]{1,0:T(8,128)(2,1)} %collective-permute-done.8.refs_3_), channel_id=1, source_target_pairs={{0,32},{32,0},{1,33},{33,1},{2,34},{34,2},{3,35},{35,3},{4,36},{36... | collective-permute-start | bytes 786440 | tf_op jit(solution)/shard_map/ppermute | solution.py:317
  41.5 1.7 project_own.1.refs_5_
  43.3 2.2 %project_other.1 = bf16[256,1024]{1,0:T(8,128)(2,1)S(1)} custom-call(s32[3]{0:T(128)S(1)} %pad_add_fusion.1.place_ref, bf16[256,2048]{1,0:T(8,128)(2,1)S(1)} %bitcast.27, bf16[2,1024,128]{2,1,0:T(8,128)(2,1)S(1)} %collective-permute-done.3.refs_0_, bf16[2,1024,128]{2,1,0:T(8,128)(2,1)} %collective-permute-done.4.refs_1_, ...), custom_call_target="tpu_custom_call" | custom-call | flops 536870912 | bytes 4194304 | tf_op jit(solution)/shard_map/project_other/pallas_call | solution.py:232
  45.5 16.4 %all_to_all.20.terms_ref = bf16[16,16,1024]{2,1,0:T(8,128)(2,1)S(1)} all-to-all(bf16[16,16,1024]{2,1,0:T(8,128)(2,1)S(1)} %bitcast.28), channel_id=1, replica_groups=mesh['xh'=2,'core'=2,'xl'=2,'yh'=2,'yl'=2,'z'=4] {'xh','xl','yh','yl'}, dimensions={0} | all-to-all | bytes 1048576 | tf_op jit(solution)/shard_map/all_to_all | solution.py:399
  61.9 0.8 norm.1
  62.6 2.3 %collective-permute-start.12 = (bf16[16,4096]{1,0:T(8,128)(2,1)S(1)}, bf16[16,4096]{1,0:T(8,128)(2,1)S(1)}, u32[]{:S(2)}, u32[]{:S(2)}) collective-permute-start(bf16[16,4096]{1,0:T(8,128)(2,1)S(1)} %get-tuple-element.33.own_ref), channel_id=1, source_target_pairs={{0,32},{32,0},{1,33},{33,1},{2,34},{34,2},{3,35},{35,3},{4,36},{36... | collective-permute-start | bytes 393224 | tf_op jit(solution)/shard_map/ppermute | solution.py:317
  65.0 1.0 collective-permute-done.12.other_ref
  65.9 0.4 collective-permute-start.13
  66.3 0.1 collective-permute-start.14
  66.5 0.4 collective-permute-start.15
  66.8 0.7 place.1
  67.5 55.1 %all_to_all.21 = bf16[64,8,4096]{2,1,0:T(8,128)(2,1)S(1)} all-to-all(bf16[64,8,4096]{2,1,0:T(8,128)(2,1)S(1)} %bitcast.25), channel_id=1, replica_groups=mesh['xh'=2,'core'=2,'xl'=2,'yh'=2,'yl'=2,'z'=4] {'yh','yl','xl','xh','z'}, dimensions={0} | all-to-all | bytes 8388608 | tf_op jit(solution)/shard_map/all_to_all | solution.py:408
  122.6 10.4 %expert.1 = bf16[512,4096]{1,0:T(8,128)(2,1)S(1)} custom-call(s32[1]{0:T(128)} %bitcast.2.core_ref, bf16[512,4096]{1,0:T(8,128)(2,1)S(1)} %bitcast.23, bf16[2,4096,384]{2,1,0:T(8,128)(2,1)} %gate_a, bf16[2,4096,384]{2,1,0:T(8,128)(2,1)} %up_a, bf16[2,384,4096]{2,1,0:T(8,128)(2,1)} %down_a, bf16[2,4096,384]{2,1,0:T(8,128)(2,1)S(1)} %collective-permute-done.13.gate_b, ...), custom_call_target="tpu_custom_call" | custom-call | flops 9663676416 | bytes 27262976 | tf_op jit(solution)/shard_map/expert/pallas_call | solution.py:176
  133.1 56.2 %all_to_all.22 = bf16[64,8,4096]{2,1,0:T(8,128)(2,1)S(1)} all-to-all(bf16[64,8,4096]{2,1,0:T(8,128)(2,1)S(1)} %bitcast.24), channel_id=1, replica_groups=mesh['xh'=2,'core'=2,'xl'=2,'yh'=2,'yl'=2,'z'=4] {'yh','yl','xl','xh','z'}, dimensions={0} | all-to-all | bytes 8388608 | tf_op jit(solution)/shard_map/all_to_all | solution.py:421
  189.3 0.8 fusion
  190.2 3.2 %collective-permute-start.16 = (bf16[16,4096]{1,0:T(8,128)(2,1)S(1)}, bf16[16,4096]{1,0:T(8,128)(2,1)S(1)}, u32[]{:S(2)}, u32[]{:S(2)}) collective-permute-start(bf16[16,4096]{1,0:T(8,128)(2,1)S(1)} %slice.39), channel_id=1, source_target_pairs={{0,32},{32,0},{1,33},{33,1},{2,34},{34,2},{3,35},{35,3},{4,36},{36... | collective-permute-start | bytes 393224 | tf_op jit(solution)/shard_map/ppermute | solution.py:317
  193.4 1.0 collective-permute-done.16
  194.4 0.7 fusion.2
  (47 shorter events, 1.0 us)
Async XLA Ops:
  0.6 1.6 copy-start
  0.6 15.8 %copy-start.4 = (f32[16,8]{0,1:T(8,128)S(1)}, f32[16,8]{0,1:T(8,128)}, u32[]{:S(2)}) copy-start(f32[16,8]{0,1:T(8,128)} %param.19) | copy-start | bytes 1540
  0.7 10.7 %copy-start.5 = (s32[16,8]{0,1:T(8,128)S(1)}, s32[16,8]{0,1:T(8,128)}, u32[]{:S(2)}) copy-start(s32[16,8]{0,1:T(8,128)} %param.18) | copy-start | bytes 1540
  2.3 9.1 %collective-permute-start = (bf16[1024,128]{1,0:T(8,128)(2,1)S(1)}, bf16[1024,128]{1,0:T(8,128)(2,1)S(1)}, u32[]{:S(2)}, u32[]{:S(2)}) collective-permute-start(bf16[1024,128]{1,0:T(8,128)(2,1)S(1)} %constant_dynamic-slice_fusion), channel_id=1, source_target_pairs={{0,4},{4,0},{1,5},{5,1},{2,6},{6,2},{3,7},{7,3},{8,12},{12,8},{9,1... | collective-permute-start | bytes 786440 | tf_op jit(solution)/shard_map/ppermute | solution.py:365
  11.6 13.1 %collective-permute-start.6 = (s32[16,8]{1,0:T(8,128)S(1)}, s32[16,8]{1,0:T(8,128)S(1)}, u32[]{:S(2)}, u32[]{:S(2)}) collective-permute-start(s32[16,8]{1,0:T(8,128)S(1)} %copy.48), channel_id=1, source_target_pairs={{0,32},{32,0},{1,33},{33,1},{2,34},{34,2},{3,35},{35,3},{4,36},{36... | collective-permute-start | bytes 1544 | tf_op jit(solution)/shard_map/ppermute | solution.py:317
  12.6 15.2 %collective-permute-start.2 = (bf16[2,1024,128]{2,1,0:T(8,128)(2,1)S(1)}, bf16[2,1024,128]{2,1,0:T(8,128)(2,1)S(1)}, u32[]{:S(2)}, u32[]{:S(2)}) collective-permute-start(bf16[2,1024,128]{2,1,0:T(8,128)(2,1)S(1)} %pad_maximum_fusion.refs_0_), channel_id=1, source_target_pairs={{0,3},{1,0},{2,1},{3,2},{4,7},{5,4},{6,5},{7,6},{8,11},{9,8},{10,9... | collective-permute-start | bytes 1572872 | tf_op jit(solution)/shard_map/ppermute | solution.py:372
  16.5 14.8 %collective-permute-start.1 = (bf16[2,1024,128]{2,1,0:T(8,128)(2,1)S(1)}, bf16[2,1024,128]{2,1,0:T(8,128)(2,1)S(1)}, u32[]{:S(2)}, u32[]{:S(2)}) collective-permute-start(bf16[2,1024,128]{2,1,0:T(8,128)(2,1)S(1)} %pad_maximum_fusion.refs_0_), channel_id=1, source_target_pairs={{0,1},{1,2},{2,3},{3,0},{4,5},{5,6},{6,7},{7,4},{8,9},{9,10},{10,1... | collective-permute-start | bytes 1572872 | tf_op jit(solution)/shard_map/ppermute | solution.py:371
  16.5 25.0 %all-to-all-start = ((bf16[16,16,2048]{2,1,0:T(8,128)(2,1)}), bf16[16,16,2048]{2,1,0:T(8,128)(2,1)S(1)}, u32[]{:S(2)}, u32[]{:S(2)}) async-start(bf16[16,16,2048]{2,1,0:T(8,128)(2,1)} %attend.1), calls=%async_computation | async-start | bytes 2097152 | tf_op jit(solution)/shard_map/all_to_all | solution.py:396
  23.0 1.5 collective-permute-start.7
  27.8 8.3 %collective-permute-start.10 = (bf16[1024,128]{1,0:T(8,128)(2,1)S(1)}, bf16[1024,128]{1,0:T(8,128)(2,1)S(1)}, u32[]{:S(2)}, u32[]{:S(2)}) collective-permute-start(bf16[1024,128]{1,0:T(8,128)(2,1)S(1)} %slice_bitcast_fusion), channel_id=1, source_target_pairs={{0,3},{1,0},{2,1},{3,2},{4,7},{5,4},{6,5},{7,6},{8,11},{9,8},{10,9... | collective-permute-start | bytes 786440 | tf_op jit(solution)/shard_map/ppermute | solution.py:392
  31.3 8.1 %collective-permute-start.8 = (bf16[1024,128]{1,0:T(8,128)(2,1)S(1)}, bf16[1024,128]{1,0:T(8,128)(2,1)}, u32[]{:S(2)}, u32[]{:S(2)}) collective-permute-start(bf16[1024,128]{1,0:T(8,128)(2,1)S(1)} %slice_bitcast_fusion.1), channel_id=1, source_target_pairs={{0,1},{1,2},{2,3},{3,0},{4,5},{5,6},{6,7},{7,4},{8,9},{9,10},{10,1... | collective-permute-start | bytes 786440 | tf_op jit(solution)/shard_map/ppermute | solution.py:392
  31.4 11.8 %collective-permute-start.3 = (bf16[2,1024,128]{2,1,0:T(8,128)(2,1)S(1)}, bf16[2,1024,128]{2,1,0:T(8,128)(2,1)S(1)}, u32[]{:S(2)}, u32[]{:S(2)}) collective-permute-start(bf16[2,1024,128]{2,1,0:T(8,128)(2,1)S(1)} %pad_maximum_fusion.refs_0_), channel_id=1, source_target_pairs={{0,32},{32,0},{1,33},{33,1},{2,34},{34,2},{3,35},{35,3},{4,36},{36... | collective-permute-start | bytes 1572872 | tf_op jit(solution)/shard_map/ppermute | solution.py:317
  32.6 10.7 %collective-permute-start.4 = (bf16[2,1024,128]{2,1,0:T(8,128)(2,1)S(1)}, bf16[2,1024,128]{2,1,0:T(8,128)(2,1)}, u32[]{:S(2)}, u32[]{:S(2)}) collective-permute-start(bf16[2,1024,128]{2,1,0:T(8,128)(2,1)S(1)} %collective-permute-done.1.refs_1_), channel_id=1, source_target_pairs={{0,32},{32,0},{1,33},{33,1},{2,34},{34,2},{3,35},{35,3},{4,36},{36... | collective-permute-start | bytes 1572872 | tf_op jit(solution)/shard_map/ppermute | solution.py:317
  32.7 10.6 %collective-permute-start.5 = (bf16[2,1024,128]{2,1,0:T(8,128)(2,1)S(1)}, bf16[2,1024,128]{2,1,0:T(8,128)(2,1)}, u32[]{:S(2)}, u32[]{:S(2)}) collective-permute-start(bf16[2,1024,128]{2,1,0:T(8,128)(2,1)S(1)} %collective-permute-done.2.refs_2_), channel_id=1, source_target_pairs={{0,32},{32,0},{1,33},{33,1},{2,34},{34,2},{3,35},{35,3},{4,36},{36... | collective-permute-start | bytes 1572872 | tf_op jit(solution)/shard_map/ppermute | solution.py:317
  36.1 7.1 %collective-permute-start.11 = (bf16[1024,128]{1,0:T(8,128)(2,1)S(1)}, bf16[1024,128]{1,0:T(8,128)(2,1)}, u32[]{:S(2)}, u32[]{:S(2)}) collective-permute-start(bf16[1024,128]{1,0:T(8,128)(2,1)S(1)} %collective-permute-done.10.refs_4_), channel_id=1, source_target_pairs={{0,32},{32,0},{1,33},{33,1},{2,34},{34,2},{3,35},{35,3},{4,36},{36... | collective-permute-start | bytes 786440 | tf_op jit(solution)/shard_map/ppermute | solution.py:317
  39.4 3.8 %collective-permute-start.9 = (bf16[1024,128]{1,0:T(8,128)(2,1)}, bf16[1024,128]{1,0:T(8,128)(2,1)}, u32[]{:S(2)}, u32[]{:S(2)}) collective-permute-start(bf16[1024,128]{1,0:T(8,128)(2,1)} %collective-permute-done.8.refs_3_), channel_id=1, source_target_pairs={{0,32},{32,0},{1,33},{33,1},{2,34},{34,2},{3,35},{35,3},{4,36},{36... | collective-permute-start | bytes 786440 | tf_op jit(solution)/shard_map/ppermute | solution.py:317
  41.5 20.4 %copy-start.2 = (bf16[16,4096]{1,0:T(8,128)(2,1)S(1)}, bf16[16,4096]{1,0:T(8,128)(2,1)}, u32[]{:S(2)}) copy-start(bf16[16,4096]{1,0:T(8,128)(2,1)} %residual_ref.1) | copy-start | bytes 393220
  41.5 20.4 %copy-start.3 = (f32[4096]{0:T(1024)S(1)}, f32[4096]{0:T(1024)}, u32[]{:S(2)}) copy-start(f32[4096]{0:T(1024)} %param.17) | copy-start | bytes 49156
  62.6 3.3 %collective-permute-start.12 = (bf16[16,4096]{1,0:T(8,128)(2,1)S(1)}, bf16[16,4096]{1,0:T(8,128)(2,1)S(1)}, u32[]{:S(2)}, u32[]{:S(2)}) collective-permute-start(bf16[16,4096]{1,0:T(8,128)(2,1)S(1)} %get-tuple-element.33.own_ref), channel_id=1, source_target_pairs={{0,32},{32,0},{1,33},{33,1},{2,34},{34,2},{3,35},{35,3},{4,36},{36... | collective-permute-start | bytes 393224 | tf_op jit(solution)/shard_map/ppermute | solution.py:317
  65.9 56.7 %collective-permute-start.13 = (bf16[2,4096,384]{2,1,0:T(8,128)(2,1)}, bf16[2,4096,384]{2,1,0:T(8,128)(2,1)S(1)}, u32[]{:S(2)}, u32[]{:S(2)}) collective-permute-start(bf16[2,4096,384]{2,1,0:T(8,128)(2,1)} %gate_a), channel_id=1, source_target_pairs={{0,32},{32,0},{1,33},{33,1},{2,34},{34,2},{3,35},{35,3},{4,36},{36... | collective-permute-start | bytes 18874376 | tf_op jit(solution)/shard_map/ppermute | solution.py:317
  66.3 56.3 %collective-permute-start.14 = (bf16[2,4096,384]{2,1,0:T(8,128)(2,1)}, bf16[2,4096,384]{2,1,0:T(8,128)(2,1)S(1)}, u32[]{:S(2)}, u32[]{:S(2)}) collective-permute-start(bf16[2,4096,384]{2,1,0:T(8,128)(2,1)} %up_a), channel_id=1, source_target_pairs={{0,32},{32,0},{1,33},{33,1},{2,34},{34,2},{3,35},{35,3},{4,36},{36... | collective-permute-start | bytes 18874376 | tf_op jit(solution)/shard_map/ppermute | solution.py:317
  66.5 56.2 %collective-permute-start.15 = (bf16[2,384,4096]{2,1,0:T(8,128)(2,1)}, bf16[2,384,4096]{2,1,0:T(8,128)(2,1)S(1)}, u32[]{:S(2)}, u32[]{:S(2)}) collective-permute-start(bf16[2,384,4096]{2,1,0:T(8,128)(2,1)} %down_a), channel_id=1, source_target_pairs={{0,32},{32,0},{1,33},{33,1},{2,34},{34,2},{3,35},{35,3},{4,36},{36... | collective-permute-start | bytes 18874376 | tf_op jit(solution)/shard_map/ppermute | solution.py:317
  133.1 62.0 %copy-start.1 = (bf16[8192,128]{1,0:T(8,128)(2,1)S(1)}, bf16[8192,128]{1,0:T(8,128)(2,1)}, u32[]{:S(2)}) copy-start(bf16[8192,128]{1,0:T(8,128)(2,1)} %param.20) | copy-start | bytes 6291460
  190.2 4.2 %collective-permute-start.16 = (bf16[16,4096]{1,0:T(8,128)(2,1)S(1)}, bf16[16,4096]{1,0:T(8,128)(2,1)S(1)}, u32[]{:S(2)}, u32[]{:S(2)}) collective-permute-start(bf16[16,4096]{1,0:T(8,128)(2,1)S(1)} %slice.39), channel_id=1, source_target_pairs={{0,32},{32,0},{1,33},{33,1},{2,34},{34,2},{3,35},{35,3},{4,36},{36... | collective-permute-start | bytes 393224 | tf_op jit(solution)/shard_map/ppermute | solution.py:317
